TPU v7x, 32 devices: a whole 2x2x4 slice. The times are simulated.
32 devices in a mesh: seq: 16 (over z, x, core), batch: 2 (over y).
Axes of the slice: x: 2, y: 2, z: 4, core: 2. Of those that a mesh axis runs over, the one named last changes fastest.
Arguments:
- patches: bfloat16 [2, 2048, 1024], P('batch', 'seq'), may hold values from -6 to 6
- cotangent: bfloat16 [2, 2048, 1024], P('batch', 'seq'), may hold values from -6 to 6
- segment_ids: int32 [2, 2048], P('batch'), may hold values from 0 to 6, as said below
- kept_mask: int32 [2, 2048], P('batch'), may hold values from 0 to 1, as said below
- first_gain: bfloat16 [1024], P(('seq', 'batch')), may hold values from 0.5 to 1.5
- qkv_weight: bfloat16 [1024, 3072], P(('seq', 'batch')), may hold values from -0.25 to 0.25
- out_weight: bfloat16 [1024, 1024], P(('seq', 'batch')), may hold values from -1.5 to 1.5
- second_gain: bfloat16 [1024], P(('seq', 'batch')), may hold values from 0.5 to 1.5
- up_weight: bfloat16 [1024, 4096], P(('seq', 'batch')), may hold values from -0.1875 to 0.1875
- down_weight: bfloat16 [4096, 1024], P(('seq', 'batch')), may hold values from -0.09375 to 0.09375
Outputs:
- block_output: bfloat16 [2, 2048, 1024], P('batch', 'seq')
- input_grad: bfloat16 [2, 2048, 1024], P('batch', 'seq')
- first_gain_grad: float32 [1024], P(('seq', 'batch'))
- qkv_grad: float32 [1024, 3072], P(('seq', 'batch'))
- out_grad: float32 [1024, 1024], P(('seq', 'batch'))
- second_gain_grad: float32 [1024], P(('seq', 'batch'))
- up_grad: float32 [1024, 4096], P(('seq', 'batch'))
- down_grad: float32 [4096, 1024], P(('seq', 'batch'))
Inputs may be any that keep to these rules, and one draw needn't show every extreme that they name: `segment_ids`: segment ids never fall along a sequence; in each sequence one segment's first slot has an index from 1 to 64 and its last slot an index from 1983 to 2046. `kept_mask`: padded slots stand only at the end of a sequence.
All inputs are finite; a program needn't handle non-finite values.
Results may differ from a plain program's by a relative error of at most 0.029.
Values may be sent and summed in bfloat16 or wider, within the bound.
No kernel may reach another device: no remote copies, remote signals or barrier semaphores. Data moves between devices by JAX's collectives and lax.ppermute only.
A program may use at most 192 MiB of HBM per device.

v0:
```python
import math

import jax
import jax.numpy as jnp
from jax import lax
from jax.sharding import PartitionSpec as P

HEADS = 16
HDIM = 64


EPSILON = 1e-05
MASKED = -1e30


def layer_norm(values, scales):
    average = jnp.mean(values, axis=-1, keepdims=True)
    centred = values - average
    variance = jnp.mean(centred * centred, axis=-1, keepdims=True)
    return centred * lax.rsqrt(variance + EPSILON) * scales


def allowed_mask(query_segments, query_positions, segment_all, kept_all, offset, count):
    key_segments = lax.dynamic_slice_in_dim(segment_all, offset, count, 0)
    key_kept = lax.dynamic_slice_in_dim(kept_all, offset, count, 0)
    key_positions = offset + jnp.arange(count, dtype=jnp.int32)
    same = query_segments[:, None] == key_segments[None, :]
    return same & ((key_kept[None, :] == 1) | (query_positions[:, None] == key_positions[None, :]))


def forward_fold(query_heads, query_segments, query_positions, segment_all, kept_all):
    scaling = HDIM ** (-0.5)

    def fold(carry, piece, start):
        key_piece, value_piece = piece
        count = key_piece.shape[0]
        block = math.gcd(count, 512)
        key_blocks = key_piece.reshape(count // block, block, HEADS, HDIM)
        value_blocks = value_piece.reshape(count // block, block, HEADS, HDIM)
        offsets = block * jnp.arange(count // block, dtype=jnp.int32)

        def fold_step(state, parts):
            running, totals, accum = state
            key_block, value_block, offset = parts
            scores = (
                jnp.einsum(
                    "qhd,khd->hqk", query_heads, key_block, preferred_element_type=jnp.float32
                )
                * scaling
            )
            allowed = allowed_mask(
                query_segments, query_positions, segment_all, kept_all, offset, block
            )[None]
            scores = jnp.where(allowed, scores, MASKED)
            newest = jnp.maximum(running, jnp.max(scores, axis=-1))
            factor = jnp.exp(running - newest)
            expo = jnp.where(allowed, jnp.exp(scores - newest[..., None]), 0.0)
            totals = totals * factor + jnp.sum(expo, axis=-1)
            update = jnp.einsum(
                "hqk,khd->qhd",
                expo.astype(jnp.bfloat16),
                value_block,
                preferred_element_type=jnp.float32,
            )
            accum = accum * factor.T[..., None] + update
            return ((newest, totals, accum), None)

        carry, unused = lax.scan(fold_step, carry, (key_blocks, value_blocks, offsets))
        return carry

    return fold


def backward_blocks(
    query_heads,
    grad_heads,
    log_totals,
    delta,
    query_segments,
    query_positions,
    segment_all,
    kept_all,
    key_all,
    value_all,
):
    length = key_all.shape[0]
    block = math.gcd(length, 512)
    scaling = HDIM ** (-0.5)
    key_blocks = key_all.reshape(length // block, block, HEADS, HDIM)
    value_blocks = value_all.reshape(length // block, block, HEADS, HDIM)
    offsets = block * jnp.arange(length // block, dtype=jnp.int32)

    def backward_step(query_grad, parts):
        key_block, value_block, offset = parts
        scores = (
            jnp.einsum("qhd,khd->hqk", query_heads, key_block, preferred_element_type=jnp.float32)
            * scaling
        )
        allowed = allowed_mask(
            query_segments, query_positions, segment_all, kept_all, offset, block
        )[None]
        probs = jnp.where(allowed, jnp.exp(scores - log_totals[..., None]), 0.0)
        dprob = jnp.einsum(
            "qhd,khd->hqk", grad_heads, value_block, preferred_element_type=jnp.float32
        )
        dscore = (probs * (dprob - delta[..., None])).astype(jnp.bfloat16)
        query_grad = (
            query_grad
            + jnp.einsum("hqk,khd->qhd", dscore, key_block, preferred_element_type=jnp.float32)
            * scaling
        )
        probs_low = probs.astype(jnp.bfloat16)
        key_term = (
            jnp.einsum("hqk,qhd->khd", dscore, query_heads, preferred_element_type=jnp.float32)
            * scaling
        )
        value_term = jnp.einsum(
            "hqk,qhd->khd", probs_low, grad_heads, preferred_element_type=jnp.float32
        )
        return (
            query_grad,
            (key_term.reshape(block, HEADS * HDIM), value_term.reshape(block, HEADS * HDIM)),
        )

    starting = jnp.zeros(query_heads.shape, jnp.float32)
    query_grad, terms = lax.scan(backward_step, starting, (key_blocks, value_blocks, offsets))
    return (
        query_grad,
        terms[0].reshape(length, HEADS * HDIM),
        terms[1].reshape(length, HEADS * HDIM),
    )


def gelu_exact(values):
    return jax.nn.gelu(values, approximate=False)


def local(
    patches,
    cotangent,
    segment_ids,
    kept_mask,
    first_gain,
    qkv_weight,
    out_weight,
    second_gain,
    up_weight,
    down_weight,
):
    gain_one, qkv_full, out_full, gain_two, up_full, down_full = (
        lax.all_gather(first_gain, ("seq", "batch"), axis=0, tiled=True),
        lax.all_gather(qkv_weight, ("seq", "batch"), axis=0, tiled=True),
        lax.all_gather(out_weight, ("seq", "batch"), axis=0, tiled=True),
        lax.all_gather(second_gain, ("seq", "batch"), axis=0, tiled=True),
        lax.all_gather(up_weight, ("seq", "batch"), axis=0, tiled=True),
        lax.all_gather(down_weight, ("seq", "batch"), axis=0, tiled=True),
    )
    width = HEADS * HDIM
    tokens = patches.shape[1]
    inputs = patches[0].astype(jnp.float32)
    segment_all = segment_ids[0]
    kept_all = kept_mask[0]
    first_slot = lax.axis_index("seq") * tokens
    query_positions = first_slot + jnp.arange(tokens, dtype=jnp.int32)
    query_segments = lax.dynamic_slice_in_dim(segment_all, first_slot, tokens, 0)
    gain_first = gain_one.astype(jnp.float32)
    normed = layer_norm(inputs, gain_first).astype(jnp.bfloat16)
    project = jnp.dot(normed, qkv_full, preferred_element_type=jnp.float32).astype(jnp.bfloat16)
    queries = project[:, :width]
    keys_local = project[:, width : 2 * width]
    values_local = project[:, 2 * width :]
    query_heads = queries.reshape(tokens, HEADS, HDIM)
    fold = forward_fold(query_heads, query_segments, query_positions, segment_all, kept_all)
    initial = (
        jnp.full((HEADS, tokens), MASKED, jnp.float32),
        jnp.zeros((HEADS, tokens), jnp.float32),
        jnp.zeros((tokens, HEADS, HDIM), jnp.float32),
    )
    running, totals, accum = fold(
        initial,
        (
            lax.all_gather(keys_local, "seq", axis=0, tiled=True),
            lax.all_gather(values_local, "seq", axis=0, tiled=True),
        ),
        jnp.int32(0),
    )
    attended = accum / totals.T[..., None]
    log_totals = running + jnp.log(totals)
    mixed = attended.reshape(tokens, width).astype(jnp.bfloat16)
    middle = inputs + jnp.dot(mixed, out_full, preferred_element_type=jnp.float32)
    gain_second = gain_two.astype(jnp.float32)
    second = layer_norm(middle, gain_second).astype(jnp.bfloat16)
    hidden_pre = jnp.dot(second, up_full, preferred_element_type=jnp.float32)
    hidden = gelu_exact(hidden_pre).astype(jnp.bfloat16)
    block_output = (middle + jnp.dot(hidden, down_full, preferred_element_type=jnp.float32)).astype(
        jnp.bfloat16
    )
    upstream = cotangent[0]
    down_grad = jnp.einsum("tf,td->fd", hidden, upstream, preferred_element_type=jnp.float32)
    hidden_grad = jnp.einsum("td,fd->tf", upstream, down_full, preferred_element_type=jnp.float32)
    unused, gelu_back = jax.vjp(gelu_exact, hidden_pre)
    pre_grad = gelu_back(hidden_grad)[0].astype(jnp.bfloat16)
    up_grad = jnp.einsum("td,tf->df", second, pre_grad, preferred_element_type=jnp.float32)
    second_grad = jnp.einsum("tf,df->td", pre_grad, up_full, preferred_element_type=jnp.float32)
    unused, second_back = jax.vjp(layer_norm, middle, gain_second)
    middle_from_norm, gain_two_grad = second_back(second_grad)
    middle_grad = upstream.astype(jnp.float32) + middle_from_norm
    middle_low = middle_grad.astype(jnp.bfloat16)
    out_grad = jnp.einsum("te,td->ed", mixed, middle_low, preferred_element_type=jnp.float32)
    mixed_grad = jnp.einsum(
        "td,ed->te", middle_low, out_full, preferred_element_type=jnp.float32
    ).astype(jnp.bfloat16)
    grad_heads = mixed_grad.reshape(tokens, HEADS, HDIM)
    delta = jnp.einsum("qhd,qhd->hq", grad_heads.astype(jnp.float32), attended)
    key_again, value_again = (
        lax.all_gather(keys_local, "seq", axis=0, tiled=True),
        lax.all_gather(values_local, "seq", axis=0, tiled=True),
    )
    query_grad, key_terms, value_terms = backward_blocks(
        query_heads,
        grad_heads,
        log_totals,
        delta,
        query_segments,
        query_positions,
        segment_all,
        kept_all,
        key_again,
        value_again,
    )
    key_grad, value_grad = (
        lax.psum_scatter(
            key_terms.astype(jnp.bfloat16), "seq", scatter_dimension=0, tiled=True
        ).astype(jnp.float32),
        lax.psum_scatter(
            value_terms.astype(jnp.bfloat16), "seq", scatter_dimension=0, tiled=True
        ).astype(jnp.float32),
    )
    project_grad = jnp.concatenate(
        [query_grad.reshape(tokens, width), key_grad, value_grad], axis=1
    ).astype(jnp.bfloat16)
    qkv_grad = jnp.einsum("td,tc->dc", normed, project_grad, preferred_element_type=jnp.float32)
    normed_grad = jnp.einsum(
        "tc,dc->td", project_grad, qkv_full, preferred_element_type=jnp.float32
    )
    unused, first_back = jax.vjp(layer_norm, inputs, gain_first)
    input_from_norm, gain_one_grad = first_back(normed_grad)
    input_grad = (middle_grad + input_from_norm).astype(jnp.bfloat16)
    gain_one_sum, qkv_sum, out_sum, gain_two_sum, up_sum, down_sum = (
        lax.psum_scatter(gain_one_grad, ("seq", "batch"), scatter_dimension=0, tiled=True),
        lax.psum_scatter(qkv_grad, ("seq", "batch"), scatter_dimension=0, tiled=True),
        lax.psum_scatter(out_grad, ("seq", "batch"), scatter_dimension=0, tiled=True),
        lax.psum_scatter(gain_two_grad, ("seq", "batch"), scatter_dimension=0, tiled=True),
        lax.psum_scatter(up_grad, ("seq", "batch"), scatter_dimension=0, tiled=True),
        lax.psum_scatter(down_grad, ("seq", "batch"), scatter_dimension=0, tiled=True),
    )
    return (
        block_output[None],
        input_grad[None],
        gain_one_sum,
        qkv_sum,
        out_sum,
        gain_two_sum,
        up_sum,
        down_sum,
    )


def solution(mesh):
    in_specs = (
        P("batch", "seq", None),
        P("batch", "seq", None),
        P("batch", None),
        P("batch", None),
        P(("seq", "batch")),
        P(("seq", "batch"), None),
        P(("seq", "batch"), None),
        P(("seq", "batch")),
        P(("seq", "batch"), None),
        P(("seq", "batch"), None),
    )
    out_specs = (
        P("batch", "seq", None),
        P("batch", "seq", None),
        P(("seq", "batch")),
        P(("seq", "batch"), None),
        P(("seq", "batch"), None),
        P(("seq", "batch")),
        P(("seq", "batch"), None),
        P(("seq", "batch"), None),
    )
    return jax.shard_map(local, mesh=mesh, in_specs=in_specs, out_specs=out_specs, check_vma=False)
```

profile of v0, /device:TPU:0, one launch (start us, length us, event | category | flops | bytes accessed | tf_op | source)
XLA Modules:
  0.0 1699.3 jit_solution(7941612382659823401)
XLA Ops:
  9.7 43.0 %all-reduce.5 = (bf16[1024]{0:T(1024)(128)(2,1)S(1)}, bf16[1024]{0:T(1024)(128)(2,1)S(1)}) all-reduce(bf16[1024]{0:T(1024)(128)(2,1)S(1)} %dynamic-update-slice, bf16[1024]{0:T(1024)(128)(2,1)S(1)} %dynamic-update-slice.1), channel_id=1, replica_groups=mesh['seq'=16,'batch'=2] {'seq','batch'}, use_global_device_ids=true, to_apply=%add | all-reduce | flops 2048 | bytes 8192
  54.9 28.5 %all-gather.7.cloned.1.call-done = bf16[1024,3072]{1,0:T(8,128)(2,1)} async-done(((bf16[32,3072]{1,0:T(8,128)(2,1)}), bf16[1024,3072]{1,0:T(8,128)(2,1)}) %all-gather.7.cloned.1.call-update) | async-done | bytes 6291472 | tf_op jit(solution)/shard_map/all_gather | solution.py:152
  91.1 46.4 %all-gather.9.cloned.1.call-done = bf16[2048,1024]{1,0:T(8,128)(2,1)} async-done(((bf16[128,1024]{1,0:T(8,128)(2,1)}), bf16[2048,1024]{1,0:T(8,128)(2,1)}) %all-gather.9.cloned.1.call-update) | async-done | bytes 4194320 | tf_op jit(solution)/shard_map/all_gather | solution.py:182
  137.5 11.8 reshape.273
  149.3 9.7 copy.67
  159.1 30.2 %all-gather.11.cloned.1.call-done = bf16[2048,1024]{1,0:T(8,128)(2,1)} async-done(((bf16[128,1024]{1,0:T(8,128)(2,1)}), bf16[2048,1024]{1,0:T(8,128)(2,1)}) %all-gather.11.cloned.1.call-update) | async-done | bytes 4194320 | tf_op jit(solution)/shard_map/all_gather | solution.py:183
  189.3 11.6 reshape.274
  201.0 9.8 copy.68
  210.7 55.8 %while.30 = (s32[]{:T(128)}, f32[16,128]{1,0:T(8,128)S(1)}, f32[16,128]{1,0:T(8,128)S(1)}, f32[128,16,64]{0,2,1:T(8,128)S(1)}, s32[128]{0:T(128)S(1)}, /*index=5...) while((s32[]{:T(128)}, f32[16,128]{1,0:T(8,128)S(1)}, ...), condition=%wide.region_5.6_spmd.clone, body=%wide.region_2.5_spmd.clone.sunk | while | flops 282735744 | bytes 33176320 | solution.py:68
  228.3 4.1 fusion.140
  256.2 4.2 fusion.140
  269.3 57.4 %all-gather.15.cloned.1.call-done = bf16[1024,4096]{1,0:T(8,128)(2,1)} async-done(((bf16[32,4096]{1,0:T(8,128)(2,1)}), bf16[1024,4096]{1,0:T(8,128)(2,1)}) %all-gather.15.cloned.1.call-update) | async-done | bytes 8388624 | tf_op jit(solution)/shard_map/all_gather | solution.py:155
  326.7 6.0 fusion.89
  332.7 73.0 %all-gather.17.cloned.1.call-done = bf16[4096,1024]{1,0:T(8,128)(2,1)} async-done(((bf16[128,1024]{1,0:T(8,128)(2,1)}), bf16[4096,1024]{1,0:T(8,128)(2,1)}) %all-gather.17.cloned.1.call-update) | async-done | bytes 8388624 | tf_op jit(solution)/shard_map/all_gather | solution.py:156
  405.7 10.0 add_convert_fusion
  426.0 95.7 %while.31 = (s32[]{:T(128)}, f32[128,16,64]{0,2,1:T(8,128)}, bf16[4,512,1024]{2,1,0:T(8,128)(2,1)}, bf16[4,512,1024]{2,1,0:T(8,128)(2,1)}, bf16[4,512,16,64]{1,3...) while((s32[]{:T(128)}, f32[128,16,64]{0,2,1:T(8,128)}, ...), condition=%wide.region_11.12_spmd.clone, body=%wide.region_10.11_spmd.clone.sunk | while | flops 683279488 | bytes 51616544 | solution.py:126
  433.7 4.2 fusion.156
  457.6 4.2 fusion.156
  481.5 4.2 fusion.156
  505.4 4.2 fusion.156
  526.8 66.0 %reduce-scatter.21.cloned.1.call-done = bf16[128,1024]{1,0:T(8,128)(2,1)} async-done(((bf16[2048,1024]{1,0:T(8,128)(2,1)}), bf16[128,1024]{1,0:T(8,128)(2,1)}) %reduce-scatter.21.cloned.1.call-update) | async-done | bytes 262160
  593.9 74.7 %reduce-scatter.19.cloned.1.call-done = bf16[128,1024]{1,0:T(8,128)(2,1)} async-done(((bf16[2048,1024]{1,0:T(8,128)(2,1)}), bf16[128,1024]{1,0:T(8,128)(2,1)}) %reduce-scatter.19.cloned.1.call-update) | async-done | bytes 262160
  669.7 6.4 fusion.71
  677.5 8.2 fusion.88
  687.3 10.7 fusion.74
  698.1 8.7 fusion.57
  706.7 5.2 fusion.68
  712.2 40.4 %all-reduce.4 = (f32[1024]{0:T(1024)S(1)}, f32[1024]{0:T(1024)S(1)}) all-reduce(f32[1024]{0:T(1024)S(1)} %get-tuple-element.360, f32[1024]{0:T(1024)S(1)} %get-tuple-element.358), channel_id=4, replica_groups=mesh['seq'=16,'batch'=2] {'seq','batch'}, use_global_device_ids=true, to_apply=%region_17.18.clone | all-reduce | flops 2048 | bytes 16384
  754.8 57.6 %reduce-scatter.13.cloned.1.call-done = f32[32,1024]{1,0:T(8,128)} async-done(((f32[1024,1024]{1,0:T(8,128)}), f32[32,1024]{1,0:T(8,128)}) %reduce-scatter.13.cloned.1.call-update) | async-done | bytes 131088 | tf_op jit(solution)/shard_map/reduce_scatter | solution.py:252
  812.4 158.8 %reduce-scatter.11.cloned.1.call-done = f32[32,3072]{1,0:T(8,128)} async-done(((f32[1024,3072]{1,0:T(8,128)}), f32[32,3072]{1,0:T(8,128)}) %reduce-scatter.11.cloned.1.call-update) | async-done | bytes 393232 | tf_op jit(solution)/shard_map/reduce_scatter | solution.py:251
  971.2 359.5 %reduce-scatter.15.cloned.1.call-done = f32[32,4096]{1,0:T(8,128)} async-done(((f32[1024,4096]{1,0:T(8,128)}), f32[32,4096]{1,0:T(8,128)}) %reduce-scatter.15.cloned.1.call-update) | async-done | bytes 524304 | tf_op jit(solution)/shard_map/reduce_scatter | solution.py:254
  1330.7 361.3 %reduce-scatter.17.cloned.1.call-done = f32[128,1024]{1,0:T(8,128)} async-done(((f32[4096,1024]{1,0:T(8,128)}), f32[128,1024]{1,0:T(8,128)}) %reduce-scatter.17.cloned.1.call-update) | async-done | bytes 524304 | tf_op jit(solution)/shard_map/reduce_scatter | solution.py:255
  (236 shorter events, 148.3 us)
Async XLA Ops:
  7.2 76.3 %all-gather.7.cloned.1.call-start = ((), (), s32[]{:S(2)}) async-start(), calls=%async_computation.6 | async-start | bytes 6488064 | tf_op jit(solution)/shard_map/all_gather | solution.py:152
  7.9 129.6 %all-gather.9.cloned.1.call-start = ((), (), s32[]{:S(2)}) async-start(), calls=%async_computation.7 | async-start | bytes 4456448 | tf_op jit(solution)/shard_map/all_gather | solution.py:182
  54.9 32.5 %copy-start.26 = (f32[128]{0:T(128)}, f32[128]{0:T(128)S(1)}, u32[]{:S(2)}) copy-start(f32[128]{0:T(128)S(1)} %fusion.67) | copy-start | bytes 1540
  87.4 3.5 copy-start.24
  88.3 101.0 %all-gather.11.cloned.1.call-start = ((), (), s32[]{:S(2)}) async-start(), calls=%async_computation.8 | async-start | bytes 4456448 | tf_op jit(solution)/shard_map/all_gather | solution.py:183
  89.0 177.7 %all-gather.13.cloned.1.call-start = ((), (), s32[]{:S(2)}) async-start(), calls=%async_computation.9 | async-start | bytes 2162688 | tf_op jit(solution)/shard_map/all_gather | solution.py:153
  89.6 237.1 %all-gather.15.cloned.1.call-start = ((), (), s32[]{:S(2)}) async-start(), calls=%async_computation.10 | async-start | bytes 8650752 | tf_op jit(solution)/shard_map/all_gather | solution.py:155
  90.2 315.5 %all-gather.17.cloned.1.call-start = ((), (), s32[]{:S(2)}) async-start(), calls=%async_computation.11 | async-start | bytes 8650752 | tf_op jit(solution)/shard_map/all_gather | solution.py:156
  90.8 502.0 %reduce-scatter.21.cloned.1.call-start = ((), (), s32[]{:S(2)}) async-start(), calls=%async_computation.17 | async-start | bytes 4456448
  201.0 9.8 copy-start.25
  210.7 55.9 %copy-start.5 = (bf16[1,128,1024]{2,1,0:T(8,128)(2,1)S(1)}, bf16[1,128,1024]{2,1,0:T(8,128)(2,1)}, u32[]{:S(2)}) copy-start(bf16[1,128,1024]{2,1,0:T(8,128)(2,1)} %param.14) | copy-start | bytes 786436
  218.5 3.5 copy-start
  232.5 3.5 copy-start
  246.4 3.5 copy-start
  260.4 3.5 copy-start
  266.6 66.1 %copy-start.14 = (bf16[128,16,64]{0,2,1:T(8,128)(2,1)}, bf16[128,16,64]{0,2,1:T(8,128)(2,1)S(1)}, u32[]{:S(2)}) copy-start(bf16[128,16,64]{0,2,1:T(8,128)(2,1)S(1)} %fusion.80) | copy-start | bytes 786436
  269.0 150.8 %copy-start.3 = (f32[128,1024]{1,0:T(8,128)}, f32[128,1024]{1,0:T(8,128)S(1)}, u32[]{:S(2)}) copy-start(f32[128,1024]{1,0:T(8,128)S(1)} %get-tuple-element.432) | copy-start | bytes 1572868
  269.2 136.4 %copy-start.21 = (bf16[1,128,1024]{2,1,0:T(8,128)(2,1)S(1)}, bf16[1,128,1024]{2,1,0:T(8,128)(2,1)}, u32[]{:S(2)}) copy-start(bf16[1,128,1024]{2,1,0:T(8,128)(2,1)} %param.15) | copy-start | bytes 786436
  405.7 11.1 copy-start.2
  420.1 4.9 copy-start.8
  420.1 4.9 copy-start.18
  521.7 146.9 %reduce-scatter.19.cloned.1.call-start = ((), (), s32[]{:S(2)}) async-start(), calls=%async_computation.16 | async-start | bytes 4456448
  522.5 290.0 %reduce-scatter.13.cloned.1.call-start = ((), (), s32[]{:S(2)}) async-start(), calls=%async_computation.13 | async-start | bytes 4325376 | tf_op jit(solution)/shard_map/reduce_scatter | solution.py:252
  525.6 144.1 %copy-start.6 = (bf16[1,128,1024]{2,1,0:T(8,128)(2,1)S(1)}, bf16[1,128,1024]{2,1,0:T(8,128)(2,1)}, u32[]{:S(2)}) copy-start(bf16[1,128,1024]{2,1,0:T(8,128)(2,1)} %param.14) | copy-start | bytes 786436
  525.6 445.6 %reduce-scatter.11.cloned.1.call-start = ((), (), s32[]{:S(2)}) async-start(), calls=%async_computation.12 | async-start | bytes 12976128 | tf_op jit(solution)/shard_map/reduce_scatter | solution.py:251
  669.7 6.4 copy-start.19
  676.2 654.5 %reduce-scatter.15.cloned.1.call-start = ((), (), s32[]{:S(2)}) async-start(), calls=%async_computation.14 | async-start | bytes 17301504 | tf_op jit(solution)/shard_map/reduce_scatter | solution.py:254
  685.8 1006.2 %reduce-scatter.17.cloned.1.call-start = ((), (), s32[]{:S(2)}) async-start(), calls=%async_computation.15 | async-start | bytes 17301504 | tf_op jit(solution)/shard_map/reduce_scatter | solution.py:255
  698.0 8.7 copy-start.20
  706.7 5.2 copy-start.27
  706.7 47.1 %copy-start.9 = (f32[128,1024]{1,0:T(8,128)S(1)}, f32[128,1024]{1,0:T(8,128)}, u32[]{:S(2)}) copy-start(f32[128,1024]{1,0:T(8,128)} %copy-done.8) | copy-start | bytes 1572868
  706.7 47.1 %copy-start.23 = (bf16[1,128,1024]{2,1,0:T(8,128)(2,1)S(1)}, bf16[1,128,1024]{2,1,0:T(8,128)(2,1)}, u32[]{:S(2)}) copy-start(bf16[1,128,1024]{2,1,0:T(8,128)(2,1)} %param.15) | copy-start | bytes 786436
  (14 other events, 27.0 us)
Sparse Core Ops, SparseCore 0:
  10.9 72.4 all-gather.6
  88.4 49.0 all-gather.8
  140.2 49.0 all-gather.10
  192.3 55.0 all-gather.12
  250.3 76.2 all-gather.14
  329.6 75.9 all-gather.16
  521.8 70.8 reduce-scatter.20
  597.1 71.4 reduce-scatter.18
  671.4 140.9 reduce-scatter.12
  818.9 152.2 reduce-scatter.10
  974.2 356.4 reduce-scatter.14
  1333.5 358.4 reduce-scatter.16
where the time goes:
time: 1700 us
  waiting for transfers between devices  1320 us (78%)
  matrix products  159 us (9%)
  blocking collectives  83.4 us (5%)
  local copies, waits for them, and re-layouts  79.9 us (5%)
  other arithmetic  27.8 us (2%)
    reduce_scatter x1, waiting for transfers between devices, local(): lax.psum_scatter(down_grad, ('seq', 'batch'), scatter_dimension=0, tiled=...  361 us
    reduce_scatter x1, waiting for transfers between devices, local(): lax.psum_scatter(up_grad, ('seq', 'batch'), scatter_dimension=0, tiled=True)  359 us
    reduce_scatter x1, waiting for transfers between devices, local(): lax.psum_scatter(qkv_grad, ('seq', 'batch'), scatter_dimension=0, tiled=T...  159 us
    unnamed x14, waiting for transfers between devices  144 us
    unnamed x2, blocking collectives  83.4 us
    all_gather x1, waiting for transfers between devices, local(): lax.all_gather(down_weight, ('seq', 'batch'), axis=0, tiled=True)  73 us
    reduce_scatter x1, waiting for transfers between devices, local(): lax.psum_scatter(out_grad, ('seq', 'batch'), scatter_dimension=0, tiled=T...  57.6 us
    all_gather x1, waiting for transfers between devices, local(): lax.all_gather(up_weight, ('seq', 'batch'), axis=0, tiled=True)  57.4 us
  transfers between devices with their start and end apart: 12, of which 11 were waited for; matrix products, arithmetic and copies ran while one was open for 9% of the time, Pallas kernels for 0%

commit v1 on v0

v1 whole, which is shorter than its diff:
```python
import functools

import jax
import jax.numpy as jnp
from jax import lax
from jax.experimental import pallas as pl
from jax.experimental.pallas import tpu as pltpu
from jax.sharding import PartitionSpec as P

HEADS = 16
HDIM = 64
QUAD = 4

EPSILON = 1e-05
MASKED = -1e30
SCALING = HDIM**-0.5
BF16 = jnp.bfloat16
F32 = jnp.float32
EVERY = ("seq", "batch")


def contract(left, right, left_dim, right_dim):
    return lax.dot_general(
        left, right, (((left_dim,), (right_dim,)), ((), ())), preferred_element_type=F32
    )


def masked_scores(keys, queries, key_ids, query_ids, query_slots):
    scores = contract(keys, queries, 0, 0)
    slots = lax.broadcasted_iota(jnp.int32, scores.shape, 0)
    allowed = (key_ids == query_ids) | (slots == query_slots)
    return jnp.where(allowed, scores, MASKED)


def forward_kernel(
    tokens, q_ref, k_ref, v_ref, key_id_ref, query_id_ref, slot_ref, mixed_ref, attended_ref, log_ref
):
    scores = masked_scores(
        k_ref[...], q_ref[...], key_id_ref[...], query_id_ref[...], slot_ref[...]
    )
    highest = jnp.max(scores, axis=0, keepdims=True)
    expo = jnp.exp(scores - highest)
    totals = jnp.sum(expo, axis=0, keepdims=True)
    attended = contract(v_ref[...], expo.astype(BF16), 1, 0) / totals
    attended_ref[...] = attended
    log_ref[...] = highest + jnp.log(totals)
    low = attended.astype(BF16)
    for piece in range(low.shape[1] // tokens):
        mixed_ref[piece] = low[:, piece * tokens : (piece + 1) * tokens]


def backward_kernel(
    tokens,
    q_ref,
    k_ref,
    v_ref,
    key_id_ref,
    query_id_ref,
    slot_ref,
    attended_ref,
    log_ref,
    grad_ref,
    dq_ref,
    dk_ref,
    dv_ref,
    dk_sum,
    dv_sum,
):
    step = pl.program_id(0)
    queries = q_ref[...]
    pieces = grad_ref.shape[0]
    grads = jnp.concatenate([grad_ref[piece] for piece in range(pieces)], axis=1)
    scores = masked_scores(k_ref[...], queries, key_id_ref[...], query_id_ref[...], slot_ref[...])
    probs = jnp.exp(scores - log_ref[...])
    delta = jnp.sum(grads.astype(F32) * attended_ref[...], axis=0, keepdims=True)
    dprob = contract(v_ref[...], grads, 0, 0)
    dscore = (probs * (dprob - delta)).astype(BF16)
    dq_ref[...] = (contract(k_ref[...], dscore, 1, 0) * SCALING).astype(BF16)
    dk = contract(queries, dscore, 1, 1)
    dv = contract(grads, probs.astype(BF16), 1, 1)

    @pl.when(step == 0)
    def _():
        dk_sum[...] = dk
        dv_sum[...] = dv

    @pl.when(step > 0)
    def _():
        dk_sum[...] += dk
        dv_sum[...] += dv

    @pl.when(step == pl.num_programs(0) - 1)
    def _():
        dk_ref[...] = dk_sum[...].astype(BF16)
        dv_ref[...] = dv_sum[...].astype(BF16)


def attention_forward(queries, keys, values, key_ids, query_ids, slots, tokens):
    length, count = keys.shape[1], queries.shape[1]
    block = min(256, count)
    whole = pl.BlockSpec((HDIM, length), lambda i: (0, 0))
    part = pl.BlockSpec((HDIM, block), lambda i: (0, i))
    row = pl.BlockSpec((1, block), lambda i: (0, i))
    return pl.pallas_call(
        functools.partial(forward_kernel, tokens),
        grid=(count // block,),
        in_specs=[
            part, whole, whole, pl.BlockSpec((length, 1), lambda i: (0, 0)), row, row
        ],
        out_specs=[
            pl.BlockSpec((block // tokens, HDIM, tokens), lambda i: (i, 0, 0)), part, row
        ],
        out_shape=[
            jax.ShapeDtypeStruct((count // tokens, HDIM, tokens), BF16),
            jax.ShapeDtypeStruct((HDIM, count), F32),
            jax.ShapeDtypeStruct((1, count), F32),
        ],
        compiler_params=pltpu.CompilerParams(vmem_limit_bytes=50 << 20),
        cost_estimate=pl.CostEstimate(
            flops=4 * HDIM * length * count,
            bytes_accessed=8 * HDIM * length,
            transcendentals=length * count,
        ),
    )(queries, keys, values, key_ids, query_ids, slots)


def attention_backward(
    queries, keys, values, key_ids, query_ids, slots, attended, logs, grads, tokens
):
    length, count = keys.shape[1], queries.shape[1]
    block = min(256, count)
    whole = pl.BlockSpec((HDIM, length), lambda i: (0, 0))
    part = pl.BlockSpec((HDIM, block), lambda i: (0, i))
    row = pl.BlockSpec((1, block), lambda i: (0, i))
    return pl.pallas_call(
        functools.partial(backward_kernel, tokens),
        grid=(count // block,),
        in_specs=[
            part,
            whole,
            whole,
            pl.BlockSpec((length, 1), lambda i: (0, 0)),
            row,
            row,
            part,
            row,
            pl.BlockSpec((block // tokens, HDIM, tokens), lambda i: (i, 0, 0)),
        ],
        out_specs=[part, whole, whole],
        out_shape=[
            jax.ShapeDtypeStruct((HDIM, count), BF16),
            jax.ShapeDtypeStruct((HDIM, length), BF16),
            jax.ShapeDtypeStruct((HDIM, length), BF16),
        ],
        scratch_shapes=[pltpu.VMEM((HDIM, length), F32)] * 2,
        compiler_params=pltpu.CompilerParams(vmem_limit_bytes=56 << 20),
        cost_estimate=pl.CostEstimate(
            flops=10 * HDIM * length * count,
            bytes_accessed=16 * HDIM * length,
            transcendentals=length * count,
        ),
    )(queries, keys, values, key_ids, query_ids, slots, attended, logs, grads)


def flip(array, bit, size):
    return lax.ppermute(array, "seq", [(i, i ^ bit) for i in range(size)])


def shifter(axis, size, stride):
    def shift(array, step):
        return lax.ppermute(
            array, axis, [(i, (i + step * stride) % size) for i in range(size)]
        )

    return shift


def ring_gather(block, ring, shift):
    rows = block.shape[0]
    pieces = [(0, 0, block)]
    right = left = block
    for step in range(1, (ring - 1) // 2 + 1):
        right, left = shift(right, 1), shift(left, -1)
        pieces += [(-step, 0, right), (step, 0, left)]
    if ring == 2:
        pieces.append((1, 0, shift(block, 1)))
    elif ring % 2 == 0:
        half = rows // 2
        pieces.append((ring // 2, 0, shift(right[:half], 1)))
        pieces.append((ring // 2, half, shift(left[half:], -1)))
    return pieces


def ring_reduce(block_at, ring, shift):
    if ring == 1:
        return block_at(0)
    if ring == 2:
        return block_at(0) + shift(block_at(1).astype(BF16), 1)
    right = left = None
    if ring % 2 == 0:
        far = block_at(ring // 2).astype(BF16)
        half = far.shape[0] // 2
        right, left = shift(far[:half], 1), shift(far[half:], -1)
        for_right, for_left = block_at(ring // 2 - 1), block_at(1 - ring // 2)
        for_right = jnp.concatenate([for_right[:half] + right, for_right[half:]])
        for_left = jnp.concatenate([for_left[:half], for_left[half:] + left])
        steps = ring // 2 - 1
    else:
        steps = (ring - 1) // 2
        for_right, for_left = block_at(steps), block_at(-steps)
    for step in range(steps, 0, -1):
        right, left = shift(for_right.astype(BF16), 1), shift(for_left.astype(BF16), -1)
        for_right, for_left = block_at(step - 1) + right, left
        if step > 1:
            for_left = block_at(1 - step) + left
    return for_right + for_left


def quad_gather(rows, size):
    rows = jnp.concatenate([rows, flip(rows, 2, size)], axis=0)
    return jnp.concatenate([rows, flip(rows, 1, size)], axis=0)


def quad_scatter(rows, size):
    half = rows.shape[0] // 2
    rows = rows[:half] + flip(rows[half:].astype(BF16), 1, size)
    half = half // 2
    return rows[:half] + flip(rows[half:].astype(BF16), 2, size)


def standardize(values):
    average = jnp.mean(values, axis=-1, keepdims=True)
    centred = values - average
    variance = jnp.mean(centred * centred, axis=-1, keepdims=True)
    inverse = lax.rsqrt(variance + EPSILON)
    return centred * inverse, inverse


def standardize_back(grad, hat, inverse):
    return inverse * (
        grad
        - jnp.mean(grad, axis=-1, keepdims=True)
        - hat * jnp.mean(grad * hat, axis=-1, keepdims=True)
    )


def gelu_exact(values):
    return jax.nn.gelu(values, approximate=False)


def local(
    seqs,
    batches,
    patches,
    cotangent,
    segment_ids,
    kept_mask,
    first_gain,
    qkv_weight,
    out_weight,
    second_gain,
    up_weight,
    down_weight,
):
    width = HEADS * HDIM
    tokens = patches.shape[1]
    length = tokens * seqs
    devices = seqs * batches
    groups = seqs // QUAD
    splits = seqs // HEADS
    count = length // splits
    lines = qkv_weight.shape[0]
    hidden_rows = down_weight.shape[0]
    quarter = hidden_rows * groups * batches
    place = lax.axis_index("seq")
    group, at_batch = place // QUAD, lax.axis_index("batch")
    quads = [[QUAD * g + q for q in range(QUAD)] for g in range(groups)]
    along_groups = shifter("seq", seqs, QUAD)
    along_batch = shifter("batch", batches, 1)

    inputs = patches[0].astype(F32)
    first_hat, first_inverse = standardize(inputs)
    own = first_hat.astype(BF16)
    near = jnp.concatenate([own, flip(own, 2, seqs)], axis=0)
    first_all = jnp.zeros((groups, 2, 2, tokens, width), BF16)
    zero = jnp.int32(0)
    swap_x, swap_core = (place // 2) % 2, place % 2
    side = tokens
    for distance, start, piece in ring_gather(near, groups, along_groups):
        at = (group + distance) % groups
        both = [(swap_core, piece), (1 - swap_core, flip(piece, 1, seqs))]
        for core, part in both:
            for row in range(start, start + part.shape[0], side):
                x = swap_x if row == 0 else 1 - swap_x
                first_all = lax.dynamic_update_slice(
                    first_all,
                    part[row - start : row - start + side][None, None, None],
                    (at, x, core, zero, zero),
                )
    first_all = first_all.reshape(length, width)

    first_rows = first_gain.astype(F32)[:, None]
    second_rows = second_gain.astype(F32)[:, None]
    qkv_rows = (qkv_weight.astype(F32) * first_rows).astype(BF16)
    qkv_rows = qkv_rows.reshape(lines, 3, HEADS, HDIM).transpose(2, 0, 1, 3)
    sent = jnp.broadcast_to(
        qkv_rows.reshape(HEADS, 1, lines, 3 * HDIM), (HEADS, splits * batches, lines, 3 * HDIM)
    )
    head_weight = lax.all_to_all(
        sent.reshape(devices, lines, 3 * HDIM), EVERY, split_axis=0, concat_axis=0, tiled=True
    ).reshape(width, 3 * HDIM)
    wide = jnp.concatenate(
        [out_weight, qkv_rows.transpose(1, 0, 2, 3).reshape(lines, 3 * width)], axis=1
    )
    wide = lax.all_gather(wide, EVERY, axis=0, tiled=True)
    out_full, qkv_full = wide[:, :width], wide[:, width:]

    up_rows = (up_weight.astype(F32) * second_rows).astype(BF16)
    up_rows = up_rows.reshape(lines, groups, QUAD, batches, hidden_rows).transpose(2, 0, 1, 3, 4)
    up_rows = lax.all_to_all(
        up_rows.reshape(QUAD, lines, quarter),
        "seq",
        split_axis=0,
        concat_axis=0,
        tiled=True,
        axis_index_groups=quads,
    )
    split_rows = QUAD * lines
    packed = jnp.concatenate(
        [up_rows.reshape(split_rows, quarter), down_weight.reshape(-1, quarter)], axis=0
    )
    up_quarter = jnp.zeros((groups, QUAD, batches, lines, quarter), BF16)
    down_quarter = jnp.zeros((groups, batches, packed.shape[0] - split_rows, quarter), BF16)
    for distance, start, piece in ring_gather(packed, groups, along_groups):
        at_group = (group + distance) % groups
        for hop, inner, part in ring_gather(piece, batches, along_batch):
            at = (at_batch + hop) % batches
            first = start + inner
            if first < split_rows:
                up_quarter = lax.dynamic_update_slice(
                    up_quarter,
                    part[: split_rows - first].reshape(1, -1, 1, lines, quarter),
                    (at_group, jnp.int32(first // lines), at, zero, zero),
                )
            if first + part.shape[0] > split_rows:
                skip = max(split_rows - first, 0)
                down_quarter = lax.dynamic_update_slice(
                    down_quarter,
                    part[skip:][None, None],
                    (at_group, at, jnp.int32(first + skip - split_rows), zero),
                )
    up_quarter = up_quarter.reshape(width, quarter)
    down_quarter = down_quarter.reshape(quarter, width)
    upstream = cotangent[0]
    upstream_quad = quad_gather(upstream, seqs)

    project = contract(head_weight, first_all, 0, 1)
    keys = project[HDIM : 2 * HDIM].astype(BF16)
    values = project[2 * HDIM :].astype(BF16)
    ids = segment_ids[0]
    key_ids = jnp.where(kept_mask[0] == 1, ids, -1)[:, None]
    begin = (place % splits) * count
    queries = (project[:HDIM] * SCALING).astype(BF16)
    queries = lax.dynamic_slice_in_dim(queries, begin, count, 1)
    query_ids = lax.dynamic_slice_in_dim(ids, begin, count, 0)[None]
    slots = (begin + jnp.arange(count, dtype=jnp.int32))[None]
    mixed_blocks, attended, logs = attention_forward(
        queries, keys, values, key_ids, query_ids, slots, tokens
    )
    if splits > 1:
        sent = jnp.zeros((seqs, HDIM, tokens), BF16)
        mixed_blocks = lax.dynamic_update_slice_in_dim(sent, mixed_blocks, begin // tokens, 0)
    mixed = lax.all_to_all(mixed_blocks, "seq", split_axis=0, concat_axis=0, tiled=True)
    if splits > 1:
        mixed = mixed.reshape(HEADS, splits, HDIM, tokens).sum(1)
    mixed = mixed.reshape(width, tokens)

    middle = inputs + contract(mixed, out_full, 0, 0)
    second_hat, second_inverse = standardize(middle)
    second_quad = quad_gather(second_hat.astype(BF16), seqs)
    hidden_pre = contract(second_quad, up_quarter, 1, 0)
    hidden, gelu_back = jax.vjp(gelu_exact, hidden_pre)
    hidden = hidden.astype(BF16)
    hidden_grad = contract(upstream_quad, down_quarter, 1, 1)
    pre_grad = gelu_back(hidden_grad)[0].astype(BF16)
    second_grad = quad_scatter(contract(pre_grad, up_quarter, 1, 1), seqs)
    middle_grad = upstream.astype(F32) + standardize_back(second_grad, second_hat, second_inverse)
    middle_low = middle_grad.astype(BF16)
    mixed_grad = contract(out_full, middle_low, 1, 1).astype(BF16)

    sent = jnp.broadcast_to(
        mixed_grad.reshape(HEADS, 1, HDIM, tokens), (HEADS, splits, HDIM, tokens)
    ).reshape(seqs, HDIM, tokens)
    grads = lax.all_to_all(sent, "seq", split_axis=0, concat_axis=0, tiled=True)
    grads = lax.dynamic_slice_in_dim(grads, begin // tokens, count // tokens, 0)
    dq, dk, dv = attention_backward(
        queries, keys, values, key_ids, query_ids, slots, attended, logs, grads, tokens
    )
    if splits > 1:
        dq = lax.dynamic_update_slice_in_dim(jnp.zeros((HDIM, length), BF16), dq, begin, 1)
    project_grad = jnp.concatenate([dq, dk, dv], axis=0)
    sent = project_grad.reshape(3 * HDIM, seqs, tokens).transpose(1, 0, 2)
    got = lax.all_to_all(sent, "seq", split_axis=0, concat_axis=0, tiled=True)
    if splits > 1:
        got = got.reshape(HEADS, splits, 3 * HDIM, tokens).sum(1)
    first_grad = contract(got.reshape(3 * width, tokens), qkv_full, 0, 1)
    input_grad = middle_grad + standardize_back(first_grad, first_hat, first_inverse)
    input_grad = input_grad.astype(BF16)

    block_output = middle + quad_scatter(contract(hidden, down_quarter, 1, 0), seqs)
    block_output = block_output.astype(BF16)

    qkv_terms = contract(first_all, project_grad, 0, 1).astype(BF16)
    qkv_terms = lax.all_to_all(
        qkv_terms.reshape(devices, lines, 3 * HDIM), EVERY, split_axis=0, concat_axis=0, tiled=True
    )
    qkv_sum = qkv_terms.reshape(HEADS, splits * batches, lines, 3, HDIM).astype(F32).sum(1)
    qkv_sum = qkv_sum.transpose(1, 2, 0, 3).reshape(lines, 3 * width)

    out_terms = contract(mixed, middle_low, 1, 0).astype(BF16)
    out_sum = lax.psum_scatter(out_terms, EVERY, scatter_dimension=0, tiled=True).astype(F32)

    up_terms = contract(second_quad, pre_grad, 0, 0).astype(BF16)
    up_terms = up_terms.reshape(groups, QUAD, batches, lines, quarter)
    down_terms = contract(hidden, upstream_quad, 0, 0).astype(BF16)
    down_terms = down_terms.reshape(groups, batches, hidden_rows, width)

    def scatter(terms, rows):
        def for_batch(distance):
            at = (at_batch + distance) % batches
            return lax.dynamic_index_in_dim(terms, at, 1, keepdims=False)

        mine = ring_reduce(for_batch, batches, along_batch)

        def for_group(distance):
            at = (group + distance) % groups
            return lax.dynamic_index_in_dim(mine, at, 0, keepdims=False)

        return ring_reduce(for_group, groups, along_groups).astype(F32)

    down_sum = scatter(down_terms, hidden_rows)
    up_sum = scatter(
        up_terms.transpose(0, 2, 1, 3, 4).reshape(groups, batches, QUAD * lines, quarter),
        QUAD * lines,
    )
    up_sum = lax.all_to_all(
        up_sum.astype(BF16).reshape(QUAD, lines, quarter),
        "seq",
        split_axis=0,
        concat_axis=0,
        tiled=True,
        axis_index_groups=quads,
    ).astype(F32)
    up_sum = up_sum.reshape(QUAD, lines, groups, batches, hidden_rows).transpose(1, 2, 0, 3, 4)
    up_sum = up_sum.reshape(lines, -1)

    first_gain_grad = jnp.sum(qkv_weight.astype(F32) * qkv_sum, axis=1)
    second_gain_grad = jnp.sum(up_weight.astype(F32) * up_sum, axis=1)
    return (
        block_output[None],
        input_grad[None],
        first_gain_grad,
        qkv_sum * first_rows,
        out_sum,
        second_gain_grad,
        up_sum * second_rows,
        down_sum,
    )


def solution(mesh):
    rows = P(EVERY)
    tokens = P("batch", "seq", None)
    in_specs = (
        tokens, tokens, P("batch", None), P("batch", None), rows, P(EVERY, None), P(EVERY, None),
        rows, P(EVERY, None), P(EVERY, None),
    )
    out_specs = (
        tokens, tokens, rows, P(EVERY, None), P(EVERY, None), rows, P(EVERY, None), P(EVERY, None)
    )
    body = functools.partial(local, mesh.shape["seq"], mesh.shape["batch"])
    return jax.shard_map(body, mesh=mesh, in_specs=in_specs, out_specs=out_specs, check_vma=False)
```

time: 1700 us -> 414 us (0.24)
  waiting for transfers between devices: 1320 us -> 157 us
  matrix products: 159 us -> 36.9 us
  starting transfers between devices: 0.73 us -> 98.1 us
  blocking collectives: 83.4 us -> 0 us
  local copies, waits for them, and re-layouts: 79.9 us -> 45.8 us
  Pallas kernels: 0 us -> 28.6 us
    reduce_scatter x4 -> x1, waiting for transfers between devices: 937 us -> 22.1 us  [local(): lax.psum_scatter(out_terms, EVERY, scatter_dimension=0, tiled=True)]
    all_gather x6 -> x1, waiting for transfers between devices: 236 us -> 0.01 us  [local(): wide = lax.all_gather(wide, EVERY, axis=0, tiled=True)]
    unnamed x14 -> x2, waiting for transfers between devices: 144 us -> 0.03 us
    dot_general x40 -> x12, matrix products: 159 us -> 36.9 us  [contract(): lax.dot_general(left, right, (((left_dim,), (right_dim,)), ((), ())), pre...]
    ppermute x0 -> x37, waiting for transfers between devices: none -> 113 us  [the longest x23 94.5 us: shift(): lax.ppermute(array, axis, [(i, (i + step * stride) % size) for i in range...]
    unnamed x2 -> x0, blocking collectives: 83.4 us -> none
    ppermute x0 -> x37, starting transfers between devices: none -> 65.1 us  [the longest x23 59.8 us: shift(): lax.ppermute(array, axis, [(i, (i + step * stride) % size) for i in range...]
    all_to_all x0 -> x7, starting transfers between devices: none -> 33 us  [the longest x1 6.83 us: local(): lax.all_to_all(sent.reshape(devices, lines, 3 * HDIM), EVERY, split_axis=...]
  transfers between devices with their start and end apart: 12 -> 46, of which waited for: 11 -> 18; matrix products, arithmetic and copies ran while one was open for 9% -> 23% of each run, Pallas kernels for 0% -> 7%
where the time goes in v1:
time: 414 us; the launch traced here: 406 us
  waiting for transfers between devices  157 us (38%)
  starting transfers between devices  98.1 us (24%)
  local copies, waits for them, and re-layouts  45.8 us (11%)
  matrix products  36.9 us (9%)
  Pallas kernels  28.6 us (7%)
  other arithmetic  23.6 us (6%)
  between operations  15.4 us (4%)
    ppermute x23, waiting for transfers between devices, shift(): lax.ppermute(array, axis, [(i, (i + step * stride) % size) for i in range...  94.5 us
    ppermute x23, starting transfers between devices, shift(): lax.ppermute(array, axis, [(i, (i + step * stride) % size) for i in range...  59.8 us
    dot_general x12, matrix products, contract(): lax.dot_general(left, right, (((left_dim,), (right_dim,)), ((), ())), pre...  36.9 us
    reduce_scatter x1, waiting for transfers between devices, local(): lax.psum_scatter(out_terms, EVERY, scatter_dimension=0, tiled=True)  22.1 us
    ppermute x14, waiting for transfers between devices, flip(): return lax.ppermute(array, 'seq', [(i, i ^ bit) for i in range(size)])  18.3 us
    pallas_call x1, Pallas kernels, attention_backward(): pl.pallas_call(functools.partial(backward_kernel, tokens), grid=(count //...  17.6 us
    all_to_all x1, waiting for transfers between devices, local(): lax.all_to_all(qkv_terms.reshape(devices, lines, 3 * HDIM), EVERY, split_...  12.4 us
    pallas_call x1, Pallas kernels, attention_forward(): pl.pallas_call(functools.partial(forward_kernel, tokens), grid=(count //...  11.1 us
  transfers between devices with their start and end apart: 46, of which 18 were waited for; matrix products, arithmetic and copies ran while one was open for 23% of the time, Pallas kernels for 7%

profile of v1, /device:TPU:0, one launch (start us, length us, event | category | flops | bytes accessed | tf_op | source)
XLA Modules:
  0.0 405.5 jit_solution(7273226955829437812)
XLA Ops:
  12.4 4.2 %all-to-all-start.2 = ((bf16[4,32,1024]{2,1,0:T(8,128)(2,1)}), bf16[4,32,1024]{2,1,0:T(8,128)(2,1)S(1)}, u32[]{:S(2)}, u32[]{:S(2)}) async-start(bf16[4,32,1024]{2,1,0:T(8,128)(2,1)} %reshape.256), calls=%async_computation.2 | async-start | bytes 524288 | tf_op jit(solution)/shard_map/all_to_all | solution.py:320
  27.2 6.8 %all-to-all-start = ((bf16[32,32,192]{2,1,0:T(8,128)(2,1)}), bf16[32,32,192]{2,1,0:T(8,128)(2,1)S(1)}, u32[]{:S(2)}, u32[]{:S(2)}) async-start(bf16[32,32,192]{2,1,0:T(8,128)(2,1)} %bitcast.2), calls=%async_computation | async-start | bytes 1048576 | tf_op jit(solution)/shard_map/all_to_all | solution.py:309
  34.1 3.7 collective-permute-start.15
  39.6 3.9 collective-permute-start.4
  46.0 12.6 %collective-permute-done.12 = bf16[256,1024]{1,0:T(8,128)(2,1)S(1)} collective-permute-done((bf16[256,1024]{1,0:T(8,128)(2,1)S(1)}, bf16[256,1024]{1,0:T(8,128)(2,1)S(1)}, u32[]{:S(2)}, u32[]{:S(2)}) %collective-permute-start.12) | collective-permute-done | bytes 524320 | tf_op jit(solution)/shard_map/ppermute | solution.py:171
  59.4 21.9 %collective-permute-done.13 = bf16[256,1024]{1,0:T(8,128)(2,1)S(1)} collective-permute-done((bf16[256,1024]{1,0:T(8,128)(2,1)S(1)}, bf16[256,1024]{1,0:T(8,128)(2,1)S(1)}, u32[]{:S(2)}, u32[]{:S(2)}) %collective-permute-start.13) | collective-permute-done | bytes 524320 | tf_op jit(solution)/shard_map/ppermute | solution.py:171
  82.2 18.9 %collective-permute-start.17 = (bf16[128,1024]{1,0:T(8,128)(2,1)S(1)}, bf16[128,1024]{1,0:T(8,128)(2,1)}, u32[]{:S(2)}, u32[]{:S(2)}) collective-permute-start(bf16[128,1024]{1,0:T(8,128)(2,1)S(1)} %slice.253), channel_id=1, source_target_pairs={{0,8},{2,10},{4,12},{6,14},{8,16},{10,18},{12,20},{14,22},{16,24},... | collective-permute-start | bytes 786440 | tf_op jit(solution)/shard_map/ppermute | solution.py:171
  101.2 21.9 %collective-permute-done.2 = bf16[256,1024]{1,0:T(8,128)(2,1)S(1)} collective-permute-done((bf16[256,1024]{1,0:T(8,128)(2,1)S(1)}, bf16[256,1024]{1,0:T(8,128)(2,1)S(1)}, u32[]{:S(2)}, u32[]{:S(2)}) %collective-permute-start.2) | collective-permute-done | bytes 524320 | tf_op jit(solution)/shard_map/ppermute | solution.py:171
  126.8 3.9 collective-permute-start.19
  131.4 3.7 collective-permute-done.14
  135.1 5.1 %collective-permute-start.6 = (bf16[128,1024]{1,0:T(8,128)(2,1)S(1)}, bf16[128,1024]{1,0:T(8,128)(2,1)S(1)}, u32[]{:S(2)}, u32[]{:S(2)}) collective-permute-start(bf16[128,1024]{1,0:T(8,128)(2,1)S(1)} %slice.240), channel_id=1, source_target_pairs={{0,8},{2,10},{4,12},{6,14},{8,16},{10,18},{12,20},{14,22},{16,24},... | collective-permute-start | bytes 786440 | tf_op jit(solution)/shard_map/ppermute | solution.py:171
  156.9 3.8 fusion.77
  160.9 11.1 %shard_map.161 = (bf16[16,64,128]{2,1,0:T(8,128)(2,1)}, f32[64,2048]{1,0:T(8,128)S(1)}, f32[1,2048]{1,0:T(1,128)S(1)}) custom-call(bf16[64,2048]{1,0:T(8,128)(2,1)S(1)} %fusion.37.q_ref, bf16[64,2048]{1,0:T(8,128)(2,1)S(1)} %get-tuple-element.39.k_ref, bf16[64,2048]{1,0:T(8,128)(2,1)S(1)} %get-tuple-element.38.v_ref, s32[2048,1]{1,0:T(8,128)S(1)} %copy.48.key_id_ref, ...), custom_call_target="tpu_custom_call" | custom-call | flops 1073741824 | bytes 1048576 | tf_op jit(solution)/shard_map/pallas_call | solution.py:104
  173.3 6.5 %all-to-all-start.1 = ((bf16[16,64,128]{2,1,0:T(8,128)(2,1)}), bf16[16,64,128]{2,1,0:T(8,128)(2,1)S(1)}, u32[]{:S(2)}, u32[]{:S(2)}) async-start(bf16[16,64,128]{2,1,0:T(8,128)(2,1)} %get-tuple-element.14), calls=%async_computation.1 | async-start | bytes 524288 | tf_op jit(solution)/shard_map/all_to_all | solution.py:373
  182.0 7.7 %all-to-all-done.1 = bf16[16,64,128]{2,1,0:T(8,128)(2,1)S(1)} async-done(((bf16[16,64,128]{2,1,0:T(8,128)(2,1)}), bf16[16,64,128]{2,1,0:T(8,128)(2,1)S(1)}, u32[]{:S(2)}, u32[]{:S(2)}) %all-to-all-start.1) | async-done | bytes 262176 | tf_op jit(solution)/shard_map/all_to_all | solution.py:373
  193.5 7.0 %collective-permute-done.10 = bf16[128,1024]{1,0:T(8,128)(2,1)S(1)} collective-permute-done((bf16[128,1024]{1,0:T(8,128)(2,1)S(1)}, bf16[128,1024]{1,0:T(8,128)(2,1)S(1)}, u32[]{:S(2)}, u32[]{:S(2)}) %collective-permute-start.10) | collective-permute-done | bytes 262176 | tf_op jit(solution)/shard_map/ppermute | solution.py:166
  205.0 5.5 %multiply_convert_fusion = (bf16[512,1024]{1,0:T(8,128)(2,1)S(1)}, f32[512,1024]{1,0:T(8,128)S(1)}, f32[512,1024]{1,0:T(8,128)S(1)}) fusion(bf16[1024,1024]{1,0:T(8,128)(2,1)S(1)} %bitcast.240, bf16[256,1024]{1,0:T(8,128)(2,1)S(1)} %collective-permute-done.11, bf16[128,1024]{1,0:T(8,128)(2,1)S(1)} %collective-permute-done.10, bf16[128,1024]{1,0:T(8,128)(2,1)S(1)} %fusion.40), kind=kOutput, calls=%fused_computation.5 | convolution fusion | flops 1110966272 | bytes 8388608 | tf_op jit(solution)/shard_map/dot_general | solution.py:23
  213.4 3.7 add_convert_fusion
  230.1 6.9 %collective-permute-done.26 = bf16[128,1024]{1,0:T(8,128)(2,1)S(1)} collective-permute-done((bf16[128,1024]{1,0:T(8,128)(2,1)S(1)}, bf16[128,1024]{1,0:T(8,128)(2,1)S(1)}, u32[]{:S(2)}, u32[]{:S(2)}) %collective-permute-start.26) | collective-permute-done | bytes 262176 | tf_op jit(solution)/shard_map/ppermute | solution.py:166
  237.2 4.3 %collective-permute-done.22 = bf16[128,1024]{1,0:T(8,128)(2,1)S(1)} collective-permute-done((bf16[128,1024]{1,0:T(8,128)(2,1)S(1)}, bf16[128,1024]{1,0:T(8,128)(2,1)S(1)}, u32[]{:S(2)}, u32[]{:S(2)}) %collective-permute-start.22) | collective-permute-done | bytes 262176 | tf_op jit(solution)/shard_map/ppermute | solution.py:166
  245.4 3.5 all-to-all-start.3
  257.3 4.0 collective-permute-done.28
  267.2 17.6 %shard_map.162 = (bf16[64,2048]{1,0:T(8,128)(2,1)}, bf16[64,2048]{1,0:T(8,128)(2,1)}, bf16[64,2048]{1,0:T(8,128)(2,1)}) custom-call(bf16[64,2048]{1,0:T(8,128)(2,1)} %copy-done.1, bf16[64,2048]{1,0:T(8,128)(2,1)} %copy-done.3, bf16[64,2048]{1,0:T(8,128)(2,1)} %copy-done.2, s32[2048,1]{1,0:T(8,128)} %copy-done, s32[1,2048]{1,0:T(1,128)} %query_id_ref.1, ...), custom_call_target="tpu_custom_call" | custom-call | flops 2684354560 | bytes 2097152 | tf_op jit(solution)/shard_map/pallas_call | solution.py:135
  289.4 3.4 all-to-all-start.6
  299.2 4.3 %all-to-all-start.5 = ((bf16[32,32,192]{2,1,0:T(8,128)(2,1)}), bf16[32,32,192]{2,1,0:T(8,128)(2,1)S(1)}, u32[]{:S(2)}, u32[]{:S(2)}) async-start(bf16[32,32,192]{2,1,0:T(8,128)(2,1)} %bitcast.51), calls=%async_computation.5 | async-start | bytes 1048576 | tf_op jit(solution)/shard_map/all_to_all | solution.py:414
  310.8 12.4 %all-to-all-done.5 = bf16[32,32,192]{2,1,0:T(8,128)(2,1)S(1)} async-done(((bf16[32,32,192]{2,1,0:T(8,128)(2,1)}), bf16[32,32,192]{2,1,0:T(8,128)(2,1)S(1)}, u32[]{:S(2)}, u32[]{:S(2)}) %all-to-all-start.5) | async-done | bytes 393248 | tf_op jit(solution)/shard_map/all_to_all | solution.py:414
  323.1 4.3 %all-to-all-start.4 = ((bf16[16,192,128]{2,1,0:T(8,128)(2,1)}), bf16[16,192,128]{2,1,0:T(8,128)(2,1)}, u32[]{:S(2)}, u32[]{:S(2)}) async-start(bf16[16,192,128]{2,1,0:T(8,128)(2,1)} %bitcast_bitcast_fusion), calls=%async_computation.4 | async-start | bytes 1572864 | tf_op jit(solution)/shard_map/all_to_all | solution.py:403
  328.5 3.7 collective-permute-start.36
  332.3 17.9 %collective-permute-done.36 = bf16[128,1024]{1,0:T(8,128)(2,1)S(1)} collective-permute-done((bf16[128,1024]{1,0:T(8,128)(2,1)S(1)}, bf16[128,1024]{1,0:T(8,128)(2,1)S(1)}, u32[]{:S(2)}, u32[]{:S(2)}) %collective-permute-start.36) | collective-permute-done | bytes 262176 | tf_op jit(solution)/shard_map/ppermute | solution.py:171
  350.2 8.1 %collective-permute-done.34 = bf16[128,1024]{1,0:T(8,128)(2,1)S(1)} collective-permute-done((bf16[128,1024]{1,0:T(8,128)(2,1)S(1)}, bf16[128,1024]{1,0:T(8,128)(2,1)S(1)}, u32[]{:S(2)}, u32[]{:S(2)}) %collective-permute-start.34) | collective-permute-done | bytes 262176 | tf_op jit(solution)/shard_map/ppermute | solution.py:171
  368.4 5.3 %fusion.73 = (f32[128]{0:T(128)S(1)}, f32[128]{0:T(128)S(1)}, f32[128,1024]{1,0:T(8,128)S(1)}) fusion(f32[128]{0:T(128)S(1)} %add_rsqrt_fusion.1, f32[128]{0:T(128)S(1)} %broadcast_multiply_fusion.7, bf16[1,128,1024]{2,1,0:T(8,128)(2,1)S(1)} %copy-done.7, bf16[3072,128]{1,0:T(8,128)(2,1)} %bitcast.49, bf16[1024,4096]{1,0:T(8,128)(2,1)} %all-gather.2.cloned.1.call-done), kind=kOutput, calls=%fused_computation.182 | convolution fusion | flops 806092544 | bytes 7866368 | tf_op jit(solution)/shard_map/dot_general | solution.py:23
  374.7 22.1 %reduce-scatter.2.cloned.1.call-done = bf16[32,1024]{1,0:T(8,128)(2,1)} async-done(((bf16[1024,1024]{1,0:T(8,128)(2,1)}), bf16[32,1024]{1,0:T(8,128)(2,1)}) %reduce-scatter.2.cloned.1.call-update) | async-done | bytes 65552 | tf_op jit(solution)/shard_map/reduce_scatter | solution.py:421
  (252 shorter events, 120.7 us)
Async XLA Ops:
  7.2 182.5 %all-gather.2.cloned.1.call-start = ((), (), s32[]{:S(2)}) async-start(), calls=%async_computation.8 | async-start | bytes 8650752 | tf_op jit(solution)/shard_map/all_gather | solution.py:315
  12.4 13.9 %all-to-all-start.2 = ((bf16[4,32,1024]{2,1,0:T(8,128)(2,1)}), bf16[4,32,1024]{2,1,0:T(8,128)(2,1)S(1)}, u32[]{:S(2)}, u32[]{:S(2)}) async-start(bf16[4,32,1024]{2,1,0:T(8,128)(2,1)} %reshape.256), calls=%async_computation.2 | async-start | bytes 524288 | tf_op jit(solution)/shard_map/all_to_all | solution.py:320
  17.2 22.4 %collective-permute-start = (bf16[128,1024]{1,0:T(8,128)(2,1)S(1)}, bf16[128,1024]{1,0:T(8,128)(2,1)S(1)}, u32[]{:S(2)}, u32[]{:S(2)}) collective-permute-start(bf16[128,1024]{1,0:T(8,128)(2,1)S(1)} %fusion.23), channel_id=1, source_target_pairs={{0,4},{2,6},{4,0},{6,2},{8,12},{10,14},{12,8},{14,10},{16,20},{18,... | collective-permute-start | bytes 786440 | tf_op jit(solution)/shard_map/ppermute | solution.py:166
  19.4 24.1 %collective-permute-start.23 = (bf16[128,1024]{1,0:T(8,128)(2,1)S(1)}, bf16[128,1024]{1,0:T(8,128)(2,1)}, u32[]{:S(2)}, u32[]{:S(2)}) collective-permute-start(bf16[128,1024]{1,0:T(8,128)(2,1)S(1)} %bitcast.251), channel_id=1, source_target_pairs={{0,4},{2,6},{4,0},{6,2},{8,12},{10,14},{12,8},{14,10},{16,20},{18,... | collective-permute-start | bytes 786440 | tf_op jit(solution)/shard_map/ppermute | solution.py:166
  27.2 129.8 %all-to-all-start = ((bf16[32,32,192]{2,1,0:T(8,128)(2,1)}), bf16[32,32,192]{2,1,0:T(8,128)(2,1)S(1)}, u32[]{:S(2)}, u32[]{:S(2)}) async-start(bf16[32,32,192]{2,1,0:T(8,128)(2,1)} %bitcast.2), calls=%async_computation | async-start | bytes 1048576 | tf_op jit(solution)/shard_map/all_to_all | solution.py:309
  34.1 48.1 %collective-permute-start.15 = (bf16[256,1024]{1,0:T(8,128)(2,1)S(1)}, bf16[256,1024]{1,0:T(8,128)(2,1)S(1)}, u32[]{:S(2)}, u32[]{:S(2)}) collective-permute-start(bf16[256,1024]{1,0:T(8,128)(2,1)S(1)} %pad_maximum_fusion.4), channel_id=1, source_target_pairs={{0,24},{2,26},{4,28},{6,30},{8,0},{10,2},{12,4},{14,6},{16,8},{18,... | collective-permute-start | bytes 1572872 | tf_op jit(solution)/shard_map/ppermute | solution.py:171
  37.7 43.6 %collective-permute-start.13 = (bf16[256,1024]{1,0:T(8,128)(2,1)S(1)}, bf16[256,1024]{1,0:T(8,128)(2,1)S(1)}, u32[]{:S(2)}, u32[]{:S(2)}) collective-permute-start(bf16[256,1024]{1,0:T(8,128)(2,1)S(1)} %pad_maximum_fusion.4), channel_id=1, source_target_pairs={{0,8},{2,10},{4,12},{6,14},{8,16},{10,18},{12,20},{14,22},{16,24},... | collective-permute-start | bytes 1572872 | tf_op jit(solution)/shard_map/ppermute | solution.py:171
  37.7 20.9 %collective-permute-start.12 = (bf16[256,1024]{1,0:T(8,128)(2,1)S(1)}, bf16[256,1024]{1,0:T(8,128)(2,1)S(1)}, u32[]{:S(2)}, u32[]{:S(2)}) collective-permute-start(bf16[256,1024]{1,0:T(8,128)(2,1)S(1)} %pad_maximum_fusion.4), channel_id=1, source_target_pairs={{0,1},{1,0},{2,3},{3,2},{4,5},{5,4},{6,7},{7,6},{8,9},{9,8},{10,11... | collective-permute-start | bytes 1572872 | tf_op jit(solution)/shard_map/ppermute | solution.py:171
  39.6 87.2 %collective-permute-start.4 = (bf16[256,1024]{1,0:T(8,128)(2,1)S(1)}, bf16[256,1024]{1,0:T(8,128)(2,1)S(1)}, u32[]{:S(2)}, u32[]{:S(2)}) collective-permute-start(bf16[256,1024]{1,0:T(8,128)(2,1)S(1)} %pad_maximum_fusion.2), channel_id=1, source_target_pairs={{0,24},{2,26},{4,28},{6,30},{8,0},{10,2},{12,4},{14,6},{16,8},{18,... | collective-permute-start | bytes 1572872 | tf_op jit(solution)/shard_map/ppermute | solution.py:171
  43.5 79.6 %collective-permute-start.2 = (bf16[256,1024]{1,0:T(8,128)(2,1)S(1)}, bf16[256,1024]{1,0:T(8,128)(2,1)S(1)}, u32[]{:S(2)}, u32[]{:S(2)}) collective-permute-start(bf16[256,1024]{1,0:T(8,128)(2,1)S(1)} %pad_maximum_fusion.2), channel_id=1, source_target_pairs={{0,8},{2,10},{4,12},{6,14},{8,16},{10,18},{12,20},{14,22},{16,24},... | collective-permute-start | bytes 1572872 | tf_op jit(solution)/shard_map/ppermute | solution.py:171
  58.6 65.9 %collective-permute-start.1 = (bf16[256,1024]{1,0:T(8,128)(2,1)S(1)}, bf16[256,1024]{1,0:T(8,128)(2,1)S(1)}, u32[]{:S(2)}, u32[]{:S(2)}) collective-permute-start(bf16[256,1024]{1,0:T(8,128)(2,1)S(1)} %pad_maximum_fusion.2), channel_id=1, source_target_pairs={{0,2},{2,0},{4,6},{6,4},{8,10},{10,8},{12,14},{14,12},{16,18},{18,... | collective-permute-start | bytes 1572872 | tf_op jit(solution)/shard_map/ppermute | solution.py:166
  81.3 132.1 %collective-permute-start.24 = (bf16[256,1024]{1,0:T(8,128)(2,1)}, bf16[256,1024]{1,0:T(8,128)(2,1)}, u32[]{:S(2)}, u32[]{:S(2)}) collective-permute-start(bf16[256,1024]{1,0:T(8,128)(2,1)} %pad_maximum_fusion.5), channel_id=1, source_target_pairs={{0,2},{2,0},{4,6},{6,4},{8,10},{10,8},{12,14},{14,12},{16,18},{18,... | collective-permute-start | bytes 1572872 | tf_op jit(solution)/shard_map/ppermute | solution.py:166
  82.2 70.2 %collective-permute-start.17 = (bf16[128,1024]{1,0:T(8,128)(2,1)S(1)}, bf16[128,1024]{1,0:T(8,128)(2,1)}, u32[]{:S(2)}, u32[]{:S(2)}) collective-permute-start(bf16[128,1024]{1,0:T(8,128)(2,1)S(1)} %slice.253), channel_id=1, source_target_pairs={{0,8},{2,10},{4,12},{6,14},{8,16},{10,18},{12,20},{14,22},{16,24},... | collective-permute-start | bytes 786440 | tf_op jit(solution)/shard_map/ppermute | solution.py:171
  124.6 16.4 %collective-permute-start.3 = (bf16[256,1024]{1,0:T(8,128)(2,1)S(1)}, bf16[256,1024]{1,0:T(8,128)(2,1)S(1)}, u32[]{:S(2)}, u32[]{:S(2)}) collective-permute-start(bf16[256,1024]{1,0:T(8,128)(2,1)S(1)} %collective-permute-done.2), channel_id=1, source_target_pairs={{0,2},{2,0},{4,6},{6,4},{8,10},{10,8},{12,14},{14,12},{16,18},{18,... | collective-permute-start | bytes 1572872 | tf_op jit(solution)/shard_map/ppermute | solution.py:166
  126.8 24.4 %collective-permute-start.19 = (bf16[128,1024]{1,0:T(8,128)(2,1)S(1)}, bf16[128,1024]{1,0:T(8,128)(2,1)}, u32[]{:S(2)}, u32[]{:S(2)}) collective-permute-start(bf16[128,1024]{1,0:T(8,128)(2,1)S(1)} %get-tuple-element.44), channel_id=1, source_target_pairs={{0,24},{2,26},{4,28},{6,30},{8,0},{10,2},{12,4},{14,6},{16,8},{18,... | collective-permute-start | bytes 786440 | tf_op jit(solution)/shard_map/ppermute | solution.py:171
  151.2 30.1 %collective-permute-start.16 = (bf16[256,1024]{1,0:T(8,128)(2,1)S(1)}, bf16[256,1024]{1,0:T(8,128)(2,1)S(1)}, u32[]{:S(2)}, u32[]{:S(2)}) collective-permute-start(bf16[256,1024]{1,0:T(8,128)(2,1)S(1)} %collective-permute-done.15), channel_id=1, source_target_pairs={{0,1},{1,0},{2,3},{3,2},{4,5},{5,4},{6,7},{7,6},{8,9},{9,8},{10,11... | collective-permute-start | bytes 1572872 | tf_op jit(solution)/shard_map/ppermute | solution.py:171
  152.4 50.9 %collective-permute-start.20 = (bf16[128,1024]{1,0:T(8,128)(2,1)}, bf16[128,1024]{1,0:T(8,128)(2,1)}, u32[]{:S(2)}, u32[]{:S(2)}) collective-permute-start(bf16[128,1024]{1,0:T(8,128)(2,1)} %collective-permute-done.19), channel_id=1, source_target_pairs={{0,1},{1,0},{2,3},{3,2},{4,5},{5,4},{6,7},{7,6},{8,9},{9,8},{10,11... | collective-permute-start | bytes 786440 | tf_op jit(solution)/shard_map/ppermute | solution.py:171
  154.1 46.5 %collective-permute-start.18 = (bf16[128,1024]{1,0:T(8,128)(2,1)}, bf16[128,1024]{1,0:T(8,128)(2,1)}, u32[]{:S(2)}, u32[]{:S(2)}) collective-permute-start(bf16[128,1024]{1,0:T(8,128)(2,1)} %collective-permute-done.17), channel_id=1, source_target_pairs={{0,1},{1,0},{2,3},{3,2},{4,5},{5,4},{6,7},{7,6},{8,9},{9,8},{10,11... | collective-permute-start | bytes 786440 | tf_op jit(solution)/shard_map/ppermute | solution.py:171
  173.3 16.4 %all-to-all-start.1 = ((bf16[16,64,128]{2,1,0:T(8,128)(2,1)}), bf16[16,64,128]{2,1,0:T(8,128)(2,1)S(1)}, u32[]{:S(2)}, u32[]{:S(2)}) async-start(bf16[16,64,128]{2,1,0:T(8,128)(2,1)} %get-tuple-element.14), calls=%async_computation.1 | async-start | bytes 524288 | tf_op jit(solution)/shard_map/all_to_all | solution.py:373
  221.7 27.3 %collective-permute-start.27 = (bf16[4,128,1024]{2,1,0:T(8,128)(2,1)}, bf16[4,128,1024]{2,1,0:T(8,128)(2,1)}, u32[]{:S(2)}, u32[]{:S(2)}) collective-permute-start(bf16[4,128,1024]{2,1,0:T(8,128)(2,1)} %dynamic-slice_bitcast_fusion.1), channel_id=1, source_target_pairs={{0,1},{1,0},{2,3},{3,2},{4,5},{5,4},{6,7},{7,6},{8,9},{9,8},{10,11... | collective-permute-start | bytes 3145736 | tf_op jit(solution)/shard_map/ppermute | solution.py:171
  226.2 77.2 %collective-permute-start.32 = (bf16[4,128,1024]{2,1,0:T(8,128)(2,1)}, bf16[4,128,1024]{2,1,0:T(8,128)(2,1)}, u32[]{:S(2)}, u32[]{:S(2)}) collective-permute-start(bf16[4,128,1024]{2,1,0:T(8,128)(2,1)} %dynamic-slice_bitcast_fusion), channel_id=1, source_target_pairs={{0,1},{1,0},{2,3},{3,2},{4,5},{5,4},{6,7},{7,6},{8,9},{9,8},{10,11... | collective-permute-start | bytes 3145736 | tf_op jit(solution)/shard_map/ppermute | solution.py:171
  228.6 12.9 %collective-permute-start.22 = (bf16[128,1024]{1,0:T(8,128)(2,1)S(1)}, bf16[128,1024]{1,0:T(8,128)(2,1)S(1)}, u32[]{:S(2)}, u32[]{:S(2)}) collective-permute-start(bf16[128,1024]{1,0:T(8,128)(2,1)S(1)} %slice.346), channel_id=1, source_target_pairs={{0,4},{2,6},{4,0},{6,2},{8,12},{10,14},{12,8},{14,10},{16,20},{18,... | collective-permute-start | bytes 786440 | tf_op jit(solution)/shard_map/ppermute | solution.py:166
  245.4 21.1 %all-to-all-start.3 = ((bf16[16,64,128]{2,1,0:T(8,128)(2,1)}), bf16[16,64,128]{2,1,0:T(8,128)(2,1)S(1)}, u32[]{:S(2)}, u32[]{:S(2)}) async-start(bf16[16,64,128]{2,1,0:T(8,128)(2,1)} %bitcast.255), calls=%async_computation.3 | async-start | bytes 524288 | tf_op jit(solution)/shard_map/all_to_all | solution.py:394
  248.9 147.8 %reduce-scatter.2.cloned.1.call-start = ((), (), s32[]{:S(2)}) async-start(), calls=%async_computation.9 | async-start | bytes 2162688 | tf_op jit(solution)/shard_map/reduce_scatter | solution.py:421
  263.2 24.4 %collective-permute-start.31 = (bf16[128,1024]{1,0:T(8,128)(2,1)}, bf16[128,1024]{1,0:T(8,128)(2,1)}, u32[]{:S(2)}, u32[]{:S(2)}) collective-permute-start(bf16[128,1024]{1,0:T(8,128)(2,1)} %pad_maximum_fusion.14), channel_id=1, source_target_pairs={{0,24},{2,26},{4,28},{6,30},{8,0},{10,2},{12,4},{14,6},{16,8},{18,... | collective-permute-start | bytes 786440 | tf_op jit(solution)/shard_map/ppermute | solution.py:171
  266.4 21.2 %collective-permute-start.29 = (bf16[128,1024]{1,0:T(8,128)(2,1)}, bf16[128,1024]{1,0:T(8,128)(2,1)S(1)}, u32[]{:S(2)}, u32[]{:S(2)}) collective-permute-start(bf16[128,1024]{1,0:T(8,128)(2,1)} %pad_maximum_fusion.13), channel_id=1, source_target_pairs={{0,8},{2,10},{4,12},{6,14},{8,16},{10,18},{12,20},{14,22},{16,24},... | collective-permute-start | bytes 786440 | tf_op jit(solution)/shard_map/ppermute | solution.py:171
  299.2 23.9 %all-to-all-start.5 = ((bf16[32,32,192]{2,1,0:T(8,128)(2,1)}), bf16[32,32,192]{2,1,0:T(8,128)(2,1)S(1)}, u32[]{:S(2)}, u32[]{:S(2)}) async-start(bf16[32,32,192]{2,1,0:T(8,128)(2,1)} %bitcast.51), calls=%async_computation.5 | async-start | bytes 1048576 | tf_op jit(solution)/shard_map/all_to_all | solution.py:414
  305.9 21.5 %collective-permute-start.33 = (bf16[64,1024]{1,0:T(8,128)(2,1)}, bf16[64,1024]{1,0:T(8,128)(2,1)}, u32[]{:S(2)}, u32[]{:S(2)}) collective-permute-start(bf16[64,1024]{1,0:T(8,128)(2,1)} %get-tuple-element.28), channel_id=1, source_target_pairs={{0,8},{2,10},{4,12},{6,14},{8,16},{10,18},{12,20},{14,22},{16,24},... | collective-permute-start | bytes 393224 | tf_op jit(solution)/shard_map/ppermute | solution.py:171
  307.7 19.8 %collective-permute-start.35 = (bf16[64,1024]{1,0:T(8,128)(2,1)}, bf16[64,1024]{1,0:T(8,128)(2,1)}, u32[]{:S(2)}, u32[]{:S(2)}) collective-permute-start(bf16[64,1024]{1,0:T(8,128)(2,1)} %get-tuple-element.30), channel_id=1, source_target_pairs={{0,24},{2,26},{4,28},{6,30},{8,0},{10,2},{12,4},{14,6},{16,8},{18,... | collective-permute-start | bytes 393224 | tf_op jit(solution)/shard_map/ppermute | solution.py:171
  323.1 45.2 %all-to-all-start.4 = ((bf16[16,192,128]{2,1,0:T(8,128)(2,1)}), bf16[16,192,128]{2,1,0:T(8,128)(2,1)}, u32[]{:S(2)}, u32[]{:S(2)}) async-start(bf16[16,192,128]{2,1,0:T(8,128)(2,1)} %bitcast_bitcast_fusion), calls=%async_computation.4 | async-start | bytes 1572864 | tf_op jit(solution)/shard_map/all_to_all | solution.py:403
  328.5 21.6 %collective-permute-start.36 = (bf16[128,1024]{1,0:T(8,128)(2,1)S(1)}, bf16[128,1024]{1,0:T(8,128)(2,1)S(1)}, u32[]{:S(2)}, u32[]{:S(2)}) collective-permute-start(bf16[128,1024]{1,0:T(8,128)(2,1)S(1)} %pad_maximum_fusion.16), channel_id=1, source_target_pairs={{0,24},{2,26},{4,28},{6,30},{8,0},{10,2},{12,4},{14,6},{16,8},{18,... | collective-permute-start | bytes 786440 | tf_op jit(solution)/shard_map/ppermute | solution.py:171
  332.3 26.1 %collective-permute-start.34 = (bf16[128,1024]{1,0:T(8,128)(2,1)S(1)}, bf16[128,1024]{1,0:T(8,128)(2,1)S(1)}, u32[]{:S(2)}, u32[]{:S(2)}) collective-permute-start(bf16[128,1024]{1,0:T(8,128)(2,1)S(1)} %pad_maximum_fusion.15), channel_id=1, source_target_pairs={{0,8},{2,10},{4,12},{6,14},{8,16},{10,18},{12,20},{14,22},{16,24},... | collective-permute-start | bytes 786440 | tf_op jit(solution)/shard_map/ppermute | solution.py:171
  (44 other events, 515.4 us)
Sparse Core Ops, SparseCore 0:
  11.7 123.7 all-gather.1
  257.5 139.2 reduce-scatter.1

commit v2 on v1

v2 whole, which is shorter than its diff:
```python
import functools
import math

import jax
import jax.numpy as jnp
from jax import lax
from jax.experimental import pallas as pl
from jax.experimental.pallas import tpu as pltpu
from jax.sharding import PartitionSpec as P

HEADS = 16
HDIM = 64
QUAD = 4
EIGHT = 8

EPSILON = 1e-05
MASKED = -1e30
SCALING = HDIM**-0.5
BF16 = jnp.bfloat16
F32 = jnp.float32
EVERY = ("seq", "batch")
LARGE = pl.CostEstimate(flops=30_000_000_000, bytes_accessed=1, transcendentals=0)
VMEM_LIMIT = 60 << 20
SMALL = pl.CostEstimate(flops=1, bytes_accessed=1, transcendentals=0)


def contract(left, right, left_dim, right_dim):
    return lax.dot_general(
        left, right, (((left_dim,), (right_dim,)), ((), ())), preferred_element_type=F32
    )


def masked_scores(keys, queries, key_ids, query_ids, first):
    scores = contract(keys, queries, 0, 0)
    slots = lax.broadcasted_iota(jnp.int32, scores.shape, 0)
    columns = first + lax.broadcasted_iota(jnp.int32, scores.shape, 1)
    allowed = (key_ids == query_ids) | (slots == columns)
    return jnp.where(allowed, scores, MASKED)


def load_heads(own_ref, other_ref, held, key_id_ref, key_column):
    half = own_ref.shape[1]
    held[:, :half] = own_ref[...]
    held[:, half:] = other_ref[...]
    key_column[...] = jnp.broadcast_to(key_id_ref[...], (8, 2 * half)).T[:, :1]


def forward_kernel(
    tokens, core_ref, own_ref, other_ref, key_id_ref, query_id_ref, mixed_ref, attended_ref,
    log_ref, held, key_column,
):
    step = pl.program_id(0)

    @pl.when(step == 0)
    def _():
        load_heads(own_ref, other_ref, held, key_id_ref, key_column)

    block = attended_ref.shape[1]
    first = pl.multiple_of(step * block, block)
    queries = held[:HDIM, pl.ds(first, block)]
    scores = masked_scores(
        held[HDIM : 2 * HDIM, :], queries, key_column[...], query_id_ref[...], first
    )
    highest = jnp.max(scores, axis=0, keepdims=True)
    expo = jnp.exp(scores - highest)
    totals = jnp.sum(expo, axis=0, keepdims=True)
    attended = contract(held[2 * HDIM :, :], expo.astype(BF16), 1, 0) / totals
    attended_ref[...] = attended
    log_ref[...] = highest + jnp.log(totals)
    low = attended.astype(BF16)
    for x in range(2):
        mixed_ref[0, x, 0] = low[:, x * tokens : (x + 1) * tokens]


def backward_kernel(
    tokens, core_ref, own_ref, other_ref, key_id_ref, query_id_ref, attended_ref, log_ref, grad_ref,
    out_ref, own_grad_ref, other_grad_ref, held, key_column, dk_sum, dv_sum,
):
    step = pl.program_id(0)
    steps = pl.num_programs(0)
    groups = out_ref.shape[0]
    half = own_ref.shape[1]

    @pl.when(step == 0)
    def _():
        load_heads(own_ref, other_ref, held, key_id_ref, key_column)
        dk_sum[...] = jnp.zeros_like(dk_sum)
        dv_sum[...] = jnp.zeros_like(dv_sum)

    block = attended_ref.shape[1]
    first = pl.multiple_of(step * block, block)
    queries = held[:HDIM, pl.ds(first, block)]
    keys = held[HDIM : 2 * HDIM, :]
    grads = jnp.concatenate([grad_ref[0, x, 0] for x in range(2)], axis=1)
    scores = masked_scores(keys, queries, key_column[...], query_id_ref[...], first)
    probs = jnp.exp(scores - log_ref[...])
    delta = jnp.sum(grads.astype(F32) * attended_ref[...], axis=0, keepdims=True)
    dprob = contract(held[2 * HDIM :, :], grads, 0, 0)
    dscore = (probs * (dprob - delta)).astype(BF16)
    dq = (contract(keys, dscore, 1, 0) * SCALING).astype(BF16)
    dk_sum[...] += contract(queries, dscore, 1, 1)
    dv_sum[...] += contract(grads, probs.astype(BF16), 1, 1)
    side = step // groups
    core = jnp.where(side == 0, core_ref[0], 1 - core_ref[0])
    for x in range(2):
        out_ref[step % groups, x, core, :HDIM, :] = dq[:, x * tokens : (x + 1) * tokens]
    inside = pl.multiple_of((step % groups) * block, block)

    @pl.when(side == 0)
    def _():
        own_grad_ref[:HDIM, pl.ds(inside, block)] = dq

    @pl.when(side == 1)
    def _():
        other_grad_ref[:HDIM, pl.ds(inside, block)] = dq

    @pl.when(step == steps - 1)
    def _():
        for first_row, total in ((HDIM, dk_sum), (2 * HDIM, dv_sum)):
            rows = pl.ds(first_row, HDIM)
            low = total[...].astype(BF16)
            own_grad_ref[rows, :] = low[:, :half]
            other_grad_ref[rows, :] = low[:, half:]
            for side_at in range(2):
                to_core = core_ref[0] if side_at == 0 else 1 - core_ref[0]
                for group in range(groups):
                    for x in range(2):
                        at = side_at * half + (2 * group + x) * tokens
                        out_ref[group, x, to_core, rows, :] = low[:, at : at + tokens]
        if steps < 2 * groups:
            other_grad_ref[:HDIM, :] = jnp.zeros((HDIM, half), BF16)
            for group in range(groups):
                for x in range(2):
                    out_ref[group, x, 1 - core_ref[0], :HDIM, :] = jnp.zeros((HDIM, tokens), BF16)


def side_core(step, groups, core):
    return jnp.where(step < groups, core, 1 - core)


def attention_specs(length, block, tokens, groups):
    half = length // 2
    whole = pl.BlockSpec((3 * HDIM, half), lambda i, core: (0, 0))
    part = pl.BlockSpec((HDIM, block), lambda i, core: (0, i))
    row = pl.BlockSpec((1, block), lambda i, core: (0, i))
    column = pl.BlockSpec((1, length), lambda i, core: (0, 0))
    tile = pl.BlockSpec(
        (1, 2, 1, HDIM, tokens),
        lambda i, core: (i % groups, 0, side_core(i, groups, core[0]), 0, 0),
    )
    return whole, part, row, column, tile


def attention_forward(core, own, other, key_ids, query_ids, tokens, splits):
    length = 2 * own.shape[1]
    block = 2 * tokens
    groups = length // (2 * block)
    count = length // splits
    whole, part, row, column, tile = attention_specs(length, block, tokens, groups)
    return pl.pallas_call(
        functools.partial(forward_kernel, tokens),
        grid_spec=pltpu.PrefetchScalarGridSpec(
            num_scalar_prefetch=1,
            grid=(count // block,),
            in_specs=[whole, whole, column, row],
            out_specs=[tile, part, row],
            scratch_shapes=[
                pltpu.VMEM((3 * HDIM, length), BF16), pltpu.VMEM((length, 1), jnp.int32)
            ],
        ),
        out_shape=[
            jax.ShapeDtypeStruct((groups, 2, 2, HDIM, tokens), BF16),
            jax.ShapeDtypeStruct((HDIM, count), F32),
            jax.ShapeDtypeStruct((1, count), F32),
        ],
        compiler_params=pltpu.CompilerParams(vmem_limit_bytes=VMEM_LIMIT),
        cost_estimate=SMALL,
    )(core, own, other, key_ids, query_ids)


def attention_backward(core, own, other, key_ids, query_ids, attended, logs, grads, tokens, splits):
    length = 2 * own.shape[1]
    half = length // 2
    block = 2 * tokens
    groups = length // (2 * block)
    count = length // splits
    whole, part, row, column, tile = attention_specs(length, block, tokens, groups)
    return pl.pallas_call(
        functools.partial(backward_kernel, tokens),
        grid_spec=pltpu.PrefetchScalarGridSpec(
            num_scalar_prefetch=1,
            grid=(count // block,),
            in_specs=[whole, whole, column, row, part, row, tile],
            out_specs=[
                pl.BlockSpec(
                    (groups, 2, 2, 3 * HDIM, tokens), lambda i, core: (0, 0, 0, 0, 0)
                ),
                whole,
                whole,
            ],
            scratch_shapes=[
                pltpu.VMEM((3 * HDIM, length), BF16),
                pltpu.VMEM((length, 1), jnp.int32),
                pltpu.VMEM((HDIM, length), F32),
                pltpu.VMEM((HDIM, length), F32),
            ],
        ),
        out_shape=[
            jax.ShapeDtypeStruct((groups, 2, 2, 3 * HDIM, tokens), BF16),
            jax.ShapeDtypeStruct((3 * HDIM, half), BF16),
            jax.ShapeDtypeStruct((3 * HDIM, half), BF16),
        ],
        compiler_params=pltpu.CompilerParams(vmem_limit_bytes=VMEM_LIMIT),
        cost_estimate=LARGE,
    )(core, own, other, key_ids, query_ids, attended, logs, grads)


def project_kernel(layout, tokens, where_ref, mine_w_ref, theirs_w_ref, *refs):
    pieces, (mine_ref, theirs_ref, all_ref) = refs[:-3], refs[-3:]
    for index, (source, row) in enumerate(layout):
        if isinstance(source, tuple):
            hat = jnp.concatenate([pieces[member][...] for member in source], axis=0)
        else:
            hat = pieces[source][row : row + tokens]
        at = where_ref[index]
        columns = pl.ds(pl.multiple_of(at * tokens, tokens), tokens)
        mine_ref[:, columns] = contract(mine_w_ref[...], hat, 1, 1).astype(BF16)
        theirs_ref[:, columns] = contract(theirs_w_ref[...], hat, 1, 1).astype(BF16)
        all_ref[at] = hat


def project_pieces(where, mine_w, theirs_w, pieces, layout, tokens):
    blocks = len(layout)
    width = mine_w.shape[1]
    columns = mine_w.shape[0]
    return whole_call(
        functools.partial(project_kernel, layout, tokens),
        where,
        [mine_w, theirs_w, *pieces],
        [
            jax.ShapeDtypeStruct((columns, blocks * tokens), BF16),
            jax.ShapeDtypeStruct((columns, blocks * tokens), BF16),
            jax.ShapeDtypeStruct((blocks, tokens, width), BF16),
        ],
    )


def whole(array):
    rank = len(array.shape)
    return pl.BlockSpec(array.shape, lambda *step: (0,) * rank)


def whole_call(kernel, scalars, arrays, outs, scratch=(), cost=SMALL):
    return pl.pallas_call(
        kernel,
        grid=(1,),
        in_specs=[pl.BlockSpec(memory_space=pltpu.SMEM)] + [whole(array) for array in arrays],
        out_specs=[whole(out) for out in outs],
        out_shape=outs,
        scratch_shapes=list(scratch),
        compiler_params=pltpu.CompilerParams(vmem_limit_bytes=VMEM_LIMIT),
        cost_estimate=cost,
    )(scalars, *arrays)


def together(refs):
    values = [ref[...] for ref in refs]
    return values[0] if len(values) == 1 else jnp.concatenate(values, axis=0)


def mlp_kernel(count, toggles, place_ref, *refs):
    pieces, refs = refs[:count], refs[count:]
    all_ref, up_ref, down_ref, hidden_ref, pre_grad_ref = refs[:5]
    hat = together(pieces)
    upstream = jnp.concatenate([all_ref[place_ref[0] ^ toggle] for toggle in toggles], axis=0)
    units = up_ref.shape[1]
    block = min(256, units)
    grad = out = None
    for first in range(0, units, block):
        chunk = slice(first, first + block)
        up, down = up_ref[:, chunk], down_ref[chunk, :]
        pre = contract(hat, up, 1, 0)
        cdf = 0.5 * (1.0 + lax.erf(pre * (0.5**0.5)))
        slope = cdf + pre * jnp.exp(-0.5 * pre * pre) * ((2.0 * math.pi) ** -0.5)
        hidden = (pre * cdf).astype(BF16)
        pre_grad = (contract(upstream, down, 1, 1) * slope).astype(BF16)
        hidden_ref[:, chunk] = hidden
        pre_grad_ref[:, chunk] = pre_grad
        grad_term = contract(pre_grad, up, 1, 1)
        out_term = contract(hidden, down, 1, 0)
        grad = grad_term if grad is None else grad + grad_term
        out = out_term if out is None else out + out_term
    for total, kept_refs in ((out, refs[5 : 5 + count]), (grad, refs[5 + count :])):
        first = 0
        for ref in kept_refs:
            ref[...] = total[first : first + ref.shape[0]].astype(ref.dtype)
            first += ref.shape[0]


def mlp(hats, toggles, place, upstream_all, up, down):
    count = len(hats)
    rows = sum(hat.shape[0] for hat in hats)
    width, units = up.shape
    sums = [
        jax.ShapeDtypeStruct(hat.shape, F32 if 2 * index < count else BF16)
        for index, hat in enumerate(hats)
    ]
    outs = whole_call(
        functools.partial(mlp_kernel, count, toggles),
        place,
        [*hats, upstream_all, up, down],
        [
            jax.ShapeDtypeStruct((rows, units), BF16),
            jax.ShapeDtypeStruct((rows, units), BF16),
            *sums,
            *sums,
        ],
    )
    return outs[0], outs[1], list(outs[2 : 2 + count]), list(outs[2 + count :])


def mlp_weight_kernel(counts, toggles, blocks, at_ref, *refs):
    hats, pres, hiddens = (
        refs[: counts[0]], refs[counts[0] : sum(counts[:2])], refs[sum(counts[:2]) : sum(counts)]
    )
    refs = refs[sum(counts) :]
    all_ref, up_refs, down_refs = refs[0], refs[1 : 1 + blocks], refs[1 + blocks : 1 + 2 * blocks]
    hat_held, hidden_held = refs[1 + 2 * blocks :]
    hat_held[...] = together(hats)
    hidden_held[...] = together(hiddens)
    pre_grad = together(pres)
    upstream = jnp.concatenate([all_ref[at_ref[0] ^ toggle] for toggle in toggles], axis=0)
    for index in range(blocks):
        for held, other, out_ref in (
            (hat_held, pre_grad, up_refs[index]), (hidden_held, upstream, down_refs[index])
        ):
            wide = out_ref.shape[0]
            columns = pl.ds(pl.multiple_of(at_ref[1 + index] * wide, wide), wide)
            out_ref[...] = contract(held[:, columns], other, 0, 0).astype(BF16)


def mlp_weight_terms(numbers, blocks, hats, toggles, pres, hiddens, upstream_all):
    tokens = sum(hat.shape[0] for hat in hats)
    width, units = hats[0].shape[1], pres[0].shape[1]
    counts = (len(hats), len(pres), len(hiddens))
    outs = whole_call(
        functools.partial(mlp_weight_kernel, counts, toggles, blocks),
        numbers,
        [*hats, *pres, *hiddens, upstream_all],
        [jax.ShapeDtypeStruct((width // blocks, units), BF16)] * blocks
        + [jax.ShapeDtypeStruct((units // blocks, width), BF16)] * blocks,
        [pltpu.VMEM((tokens, width), BF16), pltpu.VMEM((tokens, units), BF16)],
        LARGE,
    )
    return list(outs[:blocks]), list(outs[blocks:])


def out_weight_kernel(order, at_ref, mixed_ref, grad_ref, *refs):
    out_refs, held = refs[:-1], refs[-1]
    terms = contract(mixed_ref[...], grad_ref[...], 1, 0).astype(BF16)
    held[...] = terms.reshape(held.shape)
    for index, ref in enumerate(out_refs):
        toggle_core, toggle_x = index // 2, index % 2
        for y in range(2):
            for block, (g, p) in enumerate(order):
                ref[y, block] = held[
                    at_ref[g], at_ref[0] ^ toggle_x, at_ref[1] ^ toggle_core, at_ref[p],
                    at_ref[2] ^ y,
                ]


def out_weight_terms(at, order, mixed, grad, shape):
    lines, width = shape[-2:]
    return whole_call(
        functools.partial(out_weight_kernel, order),
        at,
        [mixed, grad],
        [jax.ShapeDtypeStruct((2, len(order), lines, width), BF16)] * 4,
        [pltpu.VMEM(shape, BF16)],
        LARGE,
    )


def finish_input_kernel(got_ref, weight_ref, hat_ref, inverse_ref, middle_ref, out_ref, total):
    step = pl.program_id(0)
    term = contract(got_ref[...], weight_ref[...], 0, 1)

    @pl.when(step == 0)
    def _():
        total[...] = term

    @pl.when(step > 0)
    def _():
        total[...] += term

    @pl.when(step == pl.num_programs(0) - 1)
    def _():
        grad = standardize_back(total[...], hat_ref[...], inverse_ref[...])
        out_ref[...] = (middle_ref[...] + grad).astype(BF16)


def finish_input(got, weight, hat, inverse, middle_grad):
    columns, tokens = got.shape
    width = weight.shape[0]
    block = columns // 4
    rows = [hat, inverse, middle_grad]
    return pl.pallas_call(
        finish_input_kernel,
        grid=(4,),
        in_specs=[
            pl.BlockSpec((block, tokens), lambda i: (i, 0)),
            pl.BlockSpec((width, block), lambda i: (0, i)),
            *[whole(array) for array in rows],
        ],
        out_specs=pl.BlockSpec((tokens, width), lambda i: (0, 0)),
        out_shape=jax.ShapeDtypeStruct((tokens, width), BF16),
        scratch_shapes=[pltpu.VMEM((tokens, width), F32)],
        compiler_params=pltpu.CompilerParams(vmem_limit_bytes=VMEM_LIMIT),
        cost_estimate=LARGE,
    )(got, weight, *rows)


def finish_qkv_kernel(gain_ref, terms_ref, weight_ref, out_ref, gain_grad_ref):
    copies = terms_ref.shape[0] // HEADS
    gains = gain_ref[...]
    total = None
    for head in range(HEADS):
        term = terms_ref[head * copies].astype(F32)
        for copy in range(1, copies):
            term += terms_ref[head * copies + copy].astype(F32)
        for kind in range(3):
            first = (kind * HEADS + head) * HDIM
            columns = slice(first, first + HDIM)
            part = term[:, kind * HDIM : (kind + 1) * HDIM]
            out_ref[:, columns] = part * gains
            part = part * weight_ref[:, columns].astype(F32)
            total = part if total is None else total + part
    gain_grad_ref[...] = jnp.sum(total, axis=1, keepdims=True)


def finish_qkv(gains, terms, weight):
    lines, columns = weight.shape
    outs = [
        jax.ShapeDtypeStruct((lines, columns), F32), jax.ShapeDtypeStruct((lines, 1), F32)
    ]
    arrays = [gains, terms, weight]
    return pl.pallas_call(
        finish_qkv_kernel,
        grid=(1,),
        in_specs=[whole(array) for array in arrays],
        out_specs=[whole(out) for out in outs],
        out_shape=outs,
        compiler_params=pltpu.CompilerParams(vmem_limit_bytes=VMEM_LIMIT),
        cost_estimate=SMALL,
    )(*arrays)


def finish_up_kernel(sizes, at_ref, gain_ref, near_ref, far_ref, weight_ref, out_ref, gain_grad_ref):
    groups, batches = sizes
    chunk = near_ref.shape[-1] // (groups * (batches // 2))
    gains = gain_ref[...]
    total = None
    for y, ref in enumerate((near_ref, far_ref)):
        for x in range(2):
            for core in range(2):
                quad = 2 * (at_ref[0] ^ x) + (at_ref[1] ^ core)
                term = ref[x, core].astype(F32)
                for index in range(groups * (batches // 2)):
                    group, pair = index // (batches // 2), index % (batches // 2)
                    block = (QUAD * group + quad) * batches + 2 * pair + (at_ref[2] ^ y)
                    columns = pl.ds(pl.multiple_of(block * chunk, chunk), chunk)
                    part = term[:, index * chunk : (index + 1) * chunk]
                    out_ref[:, columns] = part * gains
                    part = part * weight_ref[:, columns].astype(F32)
                    total = part if total is None else total + part
    gain_grad_ref[...] = jnp.sum(total, axis=1, keepdims=True)


def finish_up(at, gains, near, far, weight, sizes):
    lines, columns = weight.shape
    return whole_call(
        functools.partial(finish_up_kernel, sizes),
        at,
        [gains, near, far, weight],
        [jax.ShapeDtypeStruct((lines, columns), F32), jax.ShapeDtypeStruct((lines, 1), F32)],
    )


def place_kernel(plan, count, at_ref, *refs):
    sources, targets = refs[:count], refs[count:]
    for source, block, lanes, target, where in plan:
        rows = sources[source][block] if lanes is None else sources[source][block, :, lanes]
        targets[target][tuple(at_ref[entry] for entry in where)] = rows


def place(at, sources, plan, shapes):
    outs = [jax.ShapeDtypeStruct(shape, BF16) for shape in shapes]
    return whole_call(functools.partial(place_kernel, plan, len(sources)), at, sources, outs)


def flip(array, axis, bit, size):
    return lax.ppermute(array, axis, [(i, i ^ bit) for i in range(size)])


def shifter(axis, size, stride):
    def shift(array, step):
        return lax.ppermute(
            array, axis, [(i, (i + step * stride) % size) for i in range(size)]
        )

    return shift


def after(array, *others):
    return lax.optimization_barrier((array, *others))[0]


def join(*values):
    flat, shape = jax.tree.flatten(values)
    return jax.tree.unflatten(shape, lax.optimization_barrier(tuple(flat)))


class Ring:
    def __init__(self, block, ring, shift, split):
        self.ring, self.shift, self.split = ring, shift, split
        self.right = self.left = block
        self.taken = 0

    def step(self, *gates):
        self.taken += 1
        right, left = after(self.right, *gates), after(self.left, *gates)
        if 2 * self.taken == self.ring:
            right, left = right[: self.split], left[self.split :]
        self.right, self.left = self.shift(right, 1), self.shift(left, -1)
        return [self.right, self.left]


def standardize(values):
    average = jnp.mean(values, axis=-1, keepdims=True)
    centred = values - average
    variance = jnp.mean(centred * centred, axis=-1, keepdims=True)
    inverse = lax.rsqrt(variance + EPSILON)
    return centred * inverse, inverse


def standardize_back(grad, hat, inverse):
    return inverse * (
        grad
        - jnp.mean(grad, axis=-1, keepdims=True)
        - hat * jnp.mean(grad * hat, axis=-1, keepdims=True)
    )


def local(
    seqs,
    batches,
    patches,
    cotangent,
    segment_ids,
    kept_mask,
    first_gain,
    qkv_weight,
    out_weight,
    second_gain,
    up_weight,
    down_weight,
):
    width = HEADS * HDIM
    tokens = patches.shape[1]
    length = tokens * seqs
    devices = seqs * batches
    groups = seqs // QUAD
    pairs = batches // 2
    splits = seqs // HEADS
    lines = qkv_weight.shape[0]
    hidden_rows = down_weight.shape[0]
    units = hidden_rows * groups * pairs
    at_seq = lax.axis_index("seq")
    at_batch = lax.axis_index("batch")
    group, at_x, at_core = at_seq // QUAD, (at_seq // 2) % 2, at_seq % 2
    pair, at_y = at_batch // 2, at_batch % 2
    quad = at_seq % QUAD
    along_groups = shifter("seq", seqs, QUAD)
    along_pairs = shifter("batch", batches, 2)
    distances = sorted(range(groups), key=lambda step: min(step, groups - step))
    hops = [(step, hop) for hop in range(pairs) for step in distances]

    def flip_x(array, *gates):
        return flip(after(array, *gates), "seq", 2, seqs)

    def flip_core(array, *gates):
        return flip(after(array, *gates), "seq", 1, seqs)

    def flip_y(array, *gates):
        return flip(after(array, *gates), "batch", 1, batches)

    def pick(array, at, axis):
        return lax.dynamic_index_in_dim(array, at, axis, keepdims=False)

    def rows(*arrays):
        return jnp.concatenate(arrays, axis=0)

    def shifted(array, step, hop):
        array = along_groups(array, step) if step else array
        return along_pairs(array, hop) if hop else array

    def fetch(block, *gates):
        block = after(block, *gates)
        return [shifted(block, step, hop) for step, hop in hops[1:]]

    def owners(hop_list=hops):
        return [((group - step) % groups, (pair - hop) % pairs) for step, hop in hop_list]

    def deliver(terms, *gates):
        return [
            shifted(after(term, *gates), step, hop) for term, (step, hop) in zip(terms[1:], hops[1:])
        ]

    def in_order(terms):
        return [
            pick(pick(terms, (group + step) % groups, 0), (pair + hop) % pairs, 0)
            for step, hop in hops
        ]

    out_full = lax.all_gather(out_weight, EVERY, axis=0, tiled=True)
    at, plan = [], []
    for index, (g, p) in enumerate(owners()):
        first = len(at)
        at += [g, p]
        for row, (y, x, c) in enumerate(
            (y, x, c) for y in range(2) for x in range(2) for c in range(2)
        ):
            plan.append((index, (y, x, c), None, 0, (first, len(at), first + 1, len(at) + 1)))
            at += [quad ^ (2 * x + c), at_y ^ y]
        plan.append((len(hops) + index, slice(None), None, 1, (first, first + 1)))
    place_numbers = jnp.stack(at).astype(jnp.int32)
    order = [(3 + 2 * index, 4 + 2 * index) for index in range(len(hops))]
    at = [at_x, at_core, at_y]
    for step, hop in hops:
        at += [(group + step) % groups, (pair + hop) % pairs]
    out_numbers = jnp.stack(at).astype(jnp.int32)
    place_at = (4 * at_x + 2 * at_core + at_y).astype(jnp.int32)[None]
    group_numbers = [(group + step) % groups for step in distances]
    group_numbers = jnp.stack([place_at[0], *group_numbers]).astype(jnp.int32)
    core = at_core.astype(jnp.int32)[None]
    sides = jnp.stack([at_x, at_core, at_y]).astype(jnp.int32)
    numbers = [place_numbers, out_numbers, place_at, group_numbers, core, sides]

    inputs = patches[0].astype(F32)
    first_hat, first_inverse = standardize(inputs)
    own = first_hat.astype(BF16)
    first_rows = first_gain.astype(F32)[:, None]
    second_rows = second_gain.astype(F32)[:, None]
    ring = Ring(own, groups, along_groups, tokens // 2)
    rounds = [[own], ring.step()]
    beside = []
    qkv_rows = after(qkv_weight, own).astype(F32) * first_rows
    qkv_rows = qkv_rows.reshape(lines, 3, HEADS, HDIM).transpose(2, 0, 1, 3)
    scales = jnp.array([SCALING, 1.0, 1.0], F32)[:, None]
    sent = jnp.broadcast_to(
        (qkv_rows * scales).astype(BF16).reshape(HEADS, 1, lines, 3 * HDIM),
        (HEADS, splits * batches, lines, 3 * HDIM),
    ).reshape(devices, lines, 3 * HDIM)
    eights = [
        [(QUAD * g + q) * batches + 2 * p + y for q in range(QUAD) for y in range(2)]
        for g in range(groups)
        for p in range(pairs)
    ]
    qkv_part = qkv_rows.astype(BF16).transpose(1, 0, 2, 3).reshape(lines, 3 * width)
    up_rows = (after(up_weight, own).astype(F32) * second_rows).astype(BF16)
    up_rows = up_rows.reshape(lines, groups, 2, 2, pairs, 2, hidden_rows)
    up_rows = up_rows.transpose(2, 3, 5, 0, 1, 4, 6).reshape(2, 2, 2, lines, units)
    up_kept = pick(up_rows, at_core, 1)
    up_core = flip_core(pick(up_rows, 1 - at_core, 1))
    rounds[1], up_core = join(rounds[1], up_core)

    while ring.taken < groups // 2:
        beside.append(flip_x(rows(*sum(rounds if len(rounds) == 2 else rounds[-1:], []))))
        rounds.append(ring.step(*rounds[-1]))
    up_rows = jnp.stack([up_kept, up_core], axis=1)
    up_kept, up_x = pick(up_rows, at_x, 0), flip_x(pick(up_rows, 1 - at_x, 0), *rounds[1])

    def by_side(row):
        row = row.reshape(2 * groups, 2, tokens)
        sides = [pick(row, side, 1) for side in (at_core, 1 - at_core)]
        return rows(*sides).reshape(length)

    ids = by_side(segment_ids[0])
    key_ids = jnp.where(by_side(kept_mask[0]) == 1, ids, -1)[None]
    head_weight = lax.all_to_all(
        after(sent, *rounds[1]), EVERY, split_axis=0, concat_axis=0, tiled=True
    )
    farthest = rounds[-1]
    rounds, beside, up_x, head_weight, ids, key_ids, numbers = join(
        rounds, beside, up_x, head_weight, ids, key_ids, numbers
    )

    place_numbers, out_numbers, place_at, group_numbers, core, sides = numbers

    beside.append(flip_x(rows(*rounds[-1])))
    head_weight = head_weight.reshape(width, 3 * HDIM).T
    near_weight = flip_core(head_weight)
    up_rows = jnp.stack([up_kept, up_x], axis=0)
    up_kept, up_y = pick(up_rows, at_y, 2), flip_y(pick(up_rows, 1 - at_y, 2))
    down_around = fetch(down_weight, *farthest)
    beside, near_weight, up_y, down_around[:-1] = join(
        beside, near_weight, up_y, down_around[:-1]
    )
    up_packed = jnp.stack([up_kept, up_y], axis=0)
    up_around = fetch(up_packed)

    pieces, layout, where = [own], [(0, 0)], [2 * group + at_x]
    flipped = [(1, 0, 2 * group + 1 - at_x)]
    for number in range(1, len(rounds)):
        steps = [number] if 2 * number == groups else [-number, number]
        spots = [2 * ((group + step) % groups) for step in steps]
        if len(steps) == 1 and len(rounds[number]) == 2:
            layout.append(((len(pieces), len(pieces) + 1), 0))
        else:
            layout += [(len(pieces) + index, 0) for index in range(len(steps))]
        where += [spot + at_x for spot in spots]
        pieces += rounds[number]
        first = tokens if number == 1 and groups > 2 else 0
        flipped += [
            (number, first + row * tokens, spot + 1 - at_x) for row, spot in enumerate(spots)
        ]
    layout += [(len(pieces) + number - 1, row) for number, row, spot in flipped]
    where += [spot for number, row, spot in flipped]
    pieces += beside
    where = jnp.stack(where).astype(jnp.int32)
    mine, theirs, first_own = project_pieces(
        where, head_weight, near_weight, pieces, layout, tokens
    )

    other = flip_core(theirs)
    upstream = cotangent[0]
    upstream_all = lax.all_gather(
        after(upstream, mine), EVERY, axis=0, axis_index_groups=eights
    )

    query_ids = ids[None]
    mixed_blocks, attended, logs = attention_forward(
        core, mine, other, key_ids, query_ids, tokens, splits
    )
    mixed_blocks = mixed_blocks.reshape(seqs, HDIM, tokens)
    if splits > 1:
        filled = (jnp.arange(seqs, dtype=jnp.int32) % 2 == at_core)[:, None, None]
        mixed_blocks = jnp.where(filled, mixed_blocks, 0)
    mixed_blocks, down_around, up_around[:-1] = join(
        mixed_blocks, down_around, up_around[:-1]
    )

    mixed = lax.all_to_all(mixed_blocks, "seq", split_axis=0, concat_axis=0, tiled=True)
    if splits > 1:
        mixed = mixed.reshape(HEADS, splits, HDIM, tokens).sum(1)
    mixed, out_full = join(mixed.reshape(width, tokens), out_full)

    middle = inputs + contract(mixed, out_full, 0, 0)
    second_hat, second_inverse = standardize(middle)
    second = second_hat.astype(BF16)
    second_x, second_y, second_core = flip_x(second), flip_y(second), flip_core(second)
    second_core, up_around, upstream_all = join(second_core, up_around, upstream_all)
    qkv_full = lax.all_gather(after(qkv_part, second_core), EVERY, axis=0, tiled=True)
    up_part, down_part = place(
        place_numbers,
        [up_packed, *up_around, down_weight, *down_around],
        plan,
        [(groups, QUAD, pairs, 2, lines, units), (groups, pairs, hidden_rows, width)],
    )
    up_part = up_part.reshape(width, units)
    down_part = down_part.reshape(units, width)

    weights = (place_at, upstream_all, up_part, down_part)
    hidden_near, pre_near, sum_near, grad_near = mlp([second, second_core], (0, 2), *weights)
    second_x, second_y, grad_near = join(second_x, second_y, grad_near)
    second_xy = flip_x(second_y)
    second_x_core, second_y_core = flip_core(second_x), flip_core(second_y)
    hidden_mid, pre_mid, sum_mid, grad_mid = mlp(
        [second_x, second_y, second_x_core, second_y_core], (4, 1, 6, 3), *weights
    )
    second_xy, grad_mid = join(second_xy, grad_mid)
    second_xy_core = flip_core(second_xy)
    hidden_far, pre_far, sum_far, grad_far = mlp([second_xy, second_xy_core], (5, 7), *weights)

    far_sum = grad_far[0] + flip_core(grad_far[1])
    far_x = flip_x(far_sum.astype(BF16))
    x_sum = grad_mid[0] + flip_core(grad_mid[2])
    y_sum = grad_mid[1] + flip_core(grad_mid[3])
    near_sum = grad_near[0] + flip_core(grad_near[1])
    mid_x = flip_x(x_sum.astype(BF16), far_x)
    mid_y = flip_y((y_sum + far_x).astype(BF16))
    sum_other = [flip_core(term, far_sum) for term in (sum_near[1], *sum_mid[2:], sum_far[1])]
    seconds = [
        second, second_core, second_x, second_y, second_x_core, second_y_core, second_xy,
        second_xy_core,
    ]
    toggles = (0, 2, 4, 1, 6, 3, 5, 7)
    hiddens = [hidden_near, hidden_mid, hidden_far]
    pres = [pre_near, pre_mid, after(pre_far, far_sum)]
    if pairs == 1:
        up_terms, down_terms = mlp_weight_terms(
            group_numbers, len(hops), seconds, toggles, pres, hiddens, upstream_all
        )
    else:
        up_terms = contract(rows(*seconds), rows(*pres), 0, 0).astype(BF16)
        up_terms = up_terms.reshape(groups, QUAD, pairs, 2, lines, units).swapaxes(1, 2)
        sorted_places = jnp.stack([place_at[0] ^ toggle for toggle in toggles])
        down_terms = jnp.take(upstream_all, sorted_places, axis=0).reshape(-1, width)
        down_terms = contract(rows(*hiddens), down_terms, 0, 0).astype(BF16)
        down_terms = down_terms.reshape(groups, pairs, hidden_rows, width)
        up_terms, down_terms = in_order(up_terms), in_order(down_terms)
    mid_x, mid_y, up_terms, down_terms, sum_other = join(
        mid_x, mid_y, up_terms, down_terms, sum_other
    )
    second_grad = near_sum + mid_x + mid_y

    middle_grad = upstream.astype(F32) + standardize_back(second_grad, second_hat, second_inverse)
    middle_low = middle_grad.astype(BF16)
    mixed_grad = contract(out_full, middle_low, 1, 1).astype(BF16)
    up_got = deliver(up_terms, second_grad)
    sent = jnp.broadcast_to(
        mixed_grad.reshape(HEADS, 1, HDIM, tokens), (HEADS, splits, HDIM, tokens)
    ).reshape(seqs, HDIM, tokens)
    grads = lax.all_to_all(sent, "seq", split_axis=0, concat_axis=0, tiled=True)
    out_kept, out_kept_x, out_sent, out_sent_x = out_weight_terms(
        out_numbers, order, after(mixed, sent), middle_low,
        (groups, 2, 2, pairs, 2, lines, width),
    )
    out_core, out_core_x = flip_core(out_sent), flip_core(out_sent_x)
    first_own = first_own.reshape(length // 2, width)
    first_other = flip_core(first_own, sent)
    grads, first_other, out_core, out_core_x, qkv_full = join(
        grads, first_other, out_core, out_core_x, qkv_full
    )

    grads = grads.reshape(groups, 2, 2, HDIM, tokens)
    out_x = flip_x(out_kept_x + out_core_x)
    project_grad, own_grad, other_grad = attention_backward(
        core, mine, other, key_ids, query_ids, attended, logs, grads, tokens, splits
    )
    project_grad, own_grad, other_grad, out_x, up_got = join(
        project_grad, own_grad, other_grad, out_x, up_got
    )

    got = lax.all_to_all(
        project_grad.reshape(seqs, 3 * HDIM, tokens), "seq", split_axis=0, concat_axis=0, tiled=True
    )
    up_sum = sum(up_got, up_terms[0]).astype(BF16).reshape(2, 2, 2, lines, units)
    up_kept, up_core = pick(up_sum, at_core, 1), flip_core(pick(up_sum, 1 - at_core, 1))
    up_rows = jnp.stack([up_kept, up_core], axis=1)
    up_kept, up_x = pick(up_rows, at_x, 0), flip_x(pick(up_rows, 1 - at_x, 0))
    up_rows = jnp.stack([up_kept, up_x], axis=0)
    up_kept, up_y = pick(up_rows, at_y, 2), flip_y(pick(up_rows, 1 - at_y, 2))
    out_sum = out_kept + out_core + out_x
    out_sum = out_sum[0] + flip_y(out_sum[1], got)
    far_x = flip_x((sum_far[0] + after(sum_other[3], project_grad)).astype(BF16))
    mid_x = flip_x((sum_mid[0] + after(sum_other[1], project_grad)).astype(BF16))
    out_got = deliver([out_sum[index] for index in range(len(hops))])
    qkv_terms = contract(first_own, own_grad, 0, 1)
    qkv_terms = qkv_terms + contract(first_other, other_grad, 0, 1)
    if splits > 1:
        got = got.reshape(HEADS, splits, 3 * HDIM, tokens).sum(1)
    qkv_terms = after(qkv_terms, got)
    got, far_x, mid_x = join(got, far_x, mid_x)
    down_got = deliver(down_terms, got)

    qkv_terms = lax.all_to_all(
        qkv_terms.astype(BF16).reshape(devices, lines, 3 * HDIM),
        EVERY, split_axis=0, concat_axis=0, tiled=True,
    )
    mid_y = flip_y((sum_mid[1] + sum_other[2] + far_x).astype(BF16))

    input_grad = finish_input(
        got.reshape(3 * width, tokens), qkv_full, first_hat, first_inverse, middle_grad
    )
    block_output = middle + (sum_near[0] + sum_other[0] + mid_x + mid_y)
    block_output = block_output.astype(BF16)
    qkv_terms, input_grad, block_output = join(qkv_terms, input_grad, block_output)
    qkv_sum, first_gain_grad = finish_qkv(first_rows, qkv_terms, qkv_weight)
    if hidden_rows % 128 == 0:
        up_sum, second_gain_grad = finish_up(
            sides, second_rows, up_kept, up_y,
            up_weight, (groups, batches),
        )
    else:
        up_sum = jnp.stack([up_kept, up_y], axis=2)
        for axis, at in ((0, at_x), (1, at_core), (2, at_y)):
            up_sum = jnp.where(at == 0, up_sum, jnp.flip(up_sum, axis))
        up_sum = up_sum.astype(F32).reshape(2, 2, 2, lines, groups, pairs, hidden_rows)
        up_sum = up_sum.transpose(3, 4, 0, 1, 5, 2, 6).reshape(lines, -1)
        second_gain_grad = jnp.sum(up_weight.astype(F32) * up_sum, axis=1)
        up_sum = up_sum * second_rows
    down_sum = sum(down_got, down_terms[0]).astype(F32).reshape(hidden_rows, width)
    out_sum = sum(out_got, out_sum[0]).astype(F32)

    return (
        block_output[None],
        input_grad[None],
        first_gain_grad.reshape(lines),
        qkv_sum,
        out_sum,
        second_gain_grad.reshape(lines),
        up_sum,
        down_sum,
    )


def solution(mesh):
    rows = P(EVERY)
    tokens = P("batch", "seq", None)
    in_specs = (
        tokens, tokens, P("batch", None), P("batch", None), rows, P(EVERY, None), P(EVERY, None),
        rows, P(EVERY, None), P(EVERY, None),
    )
    out_specs = (
        tokens, tokens, rows, P(EVERY, None), P(EVERY, None), rows, P(EVERY, None), P(EVERY, None)
    )
    body = functools.partial(local, mesh.shape["seq"], mesh.shape["batch"])
    return jax.shard_map(body, mesh=mesh, in_specs=in_specs, out_specs=out_specs, check_vma=False)
```

time: 414 us -> 332 us (0.80); the launches traced: 406 us -> 331 us
  waiting for transfers between devices: 157 us -> 89.4 us
  Pallas kernels: 28.6 us -> 74.7 us
  matrix products: 36.9 us -> 6.4 us
  local copies, waits for them, and re-layouts: 45.8 us -> 16.1 us
  other arithmetic: 23.6 us -> 32.3 us
    ppermute x23 -> x19, waiting for transfers between devices: 94.5 us -> 39.7 us  [shift(): lax.ppermute(array, axis, [(i, (i + step * stride) % size) for i in range...]
    pallas_call x2 -> x12, Pallas kernels: 28.6 us -> 74.7 us  [the longest x8 35.8 us: whole_call(): pl.pallas_call(kernel, grid=(1,), in_specs=[pl.BlockSpec(memory_space=plt...]
    dot_general x12 -> x4, matrix products: 36.9 us -> 6.4 us  [contract(): lax.dot_general(left, right, (((left_dim,), (right_dim,)), ((), ())), pre...]
    ppermute x23 -> x19, starting transfers between devices: 59.8 us -> 36.2 us  [shift(): lax.ppermute(array, axis, [(i, (i + step * stride) % size) for i in range...]
    reduce_scatter x1 -> x0, waiting for transfers between devices: 22.1 us -> none  [local(): lax.psum_scatter(out_terms, EVERY, scatter_dimension=0, tiled=True)]
    dynamic_update_slice x31 -> x0, local copies, waits for them, and re-layouts: 21.3 us -> none  [the longest x15 10.8 us: local(): lax.dynamic_update_slice(first_all, part[row - start:row - start + side][...]
    ppermute x14 -> x36, starting transfers between devices: 5.24 us -> 24.1 us  [flip(): return lax.ppermute(array, axis, [(i, i ^ bit) for i in range(size)])]
    ppermute x14 -> x36, waiting for transfers between devices: 18.3 us -> 34.5 us  [flip(): return lax.ppermute(array, axis, [(i, i ^ bit) for i in range(size)])]
  transfers between devices with their start and end apart: 46 -> 63, of which waited for: 18 -> 23; matrix products, arithmetic and copies ran while one was open for 23% -> 14% of each run, Pallas kernels for 7% -> 22%
where the time goes in v2:
time: 332 us; the launch traced here: 331 us
  starting transfers between devices  97 us (29%)
  waiting for transfers between devices  89.4 us (27%)
  Pallas kernels  74.7 us (22%)
  other arithmetic  32.3 us (10%)
  local copies, waits for them, and re-layouts  16.1 us (5%)
  between operations  14.8 us (4%)
  matrix products  6.4 us (2%)
    ppermute x19, waiting for transfers between devices, shift(): lax.ppermute(array, axis, [(i, (i + step * stride) % size) for i in range...  39.7 us
    ppermute x19, starting transfers between devices, shift(): lax.ppermute(array, axis, [(i, (i + step * stride) % size) for i in range...  36.2 us
    pallas_call x8, Pallas kernels, whole_call(): pl.pallas_call(kernel, grid=(1,), in_specs=[pl.BlockSpec(memory_space=plt...  35.8 us
    ppermute x36, waiting for transfers between devices, flip(): return lax.ppermute(array, axis, [(i, i ^ bit) for i in range(size)])  34.5 us
    ppermute x36, starting transfers between devices, flip(): return lax.ppermute(array, axis, [(i, i ^ bit) for i in range(size)])  24.1 us
    pallas_call x1, Pallas kernels, attention_backward(): pl.pallas_call(functools.partial(backward_kernel, tokens), grid_spec=pltp...  17.4 us
    all_to_all x1, starting transfers between devices, local(): lax.all_to_all(project_grad.reshape(seqs, 3 * HDIM, tokens), 'seq', split...  15.4 us
    pallas_call x1, Pallas kernels, attention_forward(): pl.pallas_call(functools.partial(forward_kernel, tokens), grid_spec=pltpu...  12.6 us
  transfers between devices with their start and end apart: 63, of which 23 were waited for; matrix products, arithmetic and copies ran while one was open for 14% of the time, Pallas kernels for 22%

profile of v2, /device:TPU:0, one launch (start us, length us, event | category | flops | bytes accessed | tf_op | source)
XLA Modules:
  0.0 330.7 jit_solution(11004035821204731881)
XLA Ops:
  12.7 3.0 collective-permute-start
  25.0 4.8 %collective-permute-done.1.refs_2_ = bf16[128,1024]{1,0:T(8,128)(2,1)S(1)} collective-permute-done((bf16[128,1024]{1,0:T(8,128)(2,1)S(1)}, bf16[128,1024]{1,0:T(8,128)(2,1)S(1)}, u32[]{:S(2)}, u32[]{:S(2)}) %collective-permute-start.1) | collective-permute-done | bytes 262176 | tf_op jit(solution)/shard_map/ppermute | solution.py:507
  33.0 3.5 %all-to-all-start = ((bf16[32,32,192]{2,1,0:T(8,128)(2,1)}), bf16[32,32,192]{2,1,0:T(8,128)(2,1)S(1)}, u32[]{:S(2)}, u32[]{:S(2)}) async-start(bf16[32,32,192]{2,1,0:T(8,128)(2,1)} %bitcast.14), calls=%async_computation | async-start | bytes 1048576 | tf_op jit(solution)/shard_map/all_to_all | solution.py:690
  39.4 3.4 %collective-permute-start.4 = (bf16[64,1024]{1,0:T(8,128)(2,1)S(1)}, bf16[64,1024]{1,0:T(8,128)(2,1)S(1)}, u32[]{:S(2)}, u32[]{:S(2)}) collective-permute-start(bf16[64,1024]{1,0:T(8,128)(2,1)S(1)} %slice.25), channel_id=1, source_target_pairs={{0,24},{2,26},{4,28},{6,30},{8,0},{10,2},{12,4},{14,6},{16,8},{18,... | collective-permute-start | bytes 393224 | tf_op jit(solution)/shard_map/ppermute | solution.py:507
  46.1 12.7 %collective-permute-done.6 = bf16[2,2,32,512]{3,2,0,1:T(8,128)(2,1)S(1)} collective-permute-done((bf16[2,2,32,512]{3,2,0,1:T(8,128)(2,1)S(1)}, bf16[2,2,32,512]{3,2,0,1:T(8,128)(2,1)S(1)}, u32[]{:S(2)}, u32[]{:S(2)}) %collective-permute-start.6) | collective-permute-done | bytes 131104 | tf_op jit(solution)/shard_map/ppermute | solution.py:502
  69.7 4.9 %collective-permute-done.10.refs_5_ = bf16[128,1024]{1,0:T(8,128)(2,1)S(1)} collective-permute-done((bf16[128,1024]{1,0:T(8,128)(2,1)}, bf16[128,1024]{1,0:T(8,128)(2,1)S(1)}, u32[]{:S(2)}, u32[]{:S(2)}) %collective-permute-start.10) | collective-permute-done | bytes 262176 | tf_op jit(solution)/shard_map/ppermute | solution.py:507
  74.6 5.9 %collective-permute-done.11.refs_6_ = bf16[128,1024]{1,0:T(8,128)(2,1)S(1)} collective-permute-done((bf16[128,1024]{1,0:T(8,128)(2,1)}, bf16[128,1024]{1,0:T(8,128)(2,1)S(1)}, u32[]{:S(2)}, u32[]{:S(2)}) %collective-permute-start.11) | collective-permute-done | bytes 262176 | tf_op jit(solution)/shard_map/ppermute | solution.py:507
  81.4 5.1 %shard_map.170 = (bf16[192,1024]{1,0:T(8,128)(2,1)}, bf16[192,1024]{1,0:T(8,128)(2,1)}, bf16[8,128,1024]{2,1,0:T(8,128)(2,1)}) custom-call(s32[8]{0:T(128)} %stack.86.where_ref, bf16[192,1024]{1,0:T(8,128)(2,1)} %bitcast.147, bf16[192,1024]{1,0:T(8,128)(2,1)} %copy-done.25, bf16[128,1024]{1,0:T(8,128)(2,1)} %copy-done.2, bf16[128,1024]{1,0:T(8,128)(2,1)} %copy-done.5, ...), custom_call_target="tpu_custom_call" | custom-call | flops 1 | bytes 1 | tf_op jit(solution)/shard_map/pallas_call | solution.py:254
  90.2 3.3 collective-permute-start.15
  94.3 12.6 %shard_map.171 = (bf16[4,2,2,64,128]{4,3,2,1,0:T(8,128)(2,1)}, f32[64,2048]{1,0:T(8,128)}, f32[1,2048]{1,0:T(1,128)}) custom-call(s32[1]{0:T(128)} %bitcast.34.core_ref, bf16[192,1024]{1,0:T(8,128)(2,1)} %get-tuple-element.184.own_ref, bf16[192,1024]{1,0:T(8,128)(2,1)} %copy-done.28, s32[1,2048]{1,0:T(1,128)} %bitcast.161, s32[1,2048]{1,0:T(1,128)} %bitcast.163), custom_call_target="tpu_custom_call" | custom-call | flops 1 | bytes 1 | tf_op jit(solution)/shard_map/pallas_call | solution.py:160
  108.7 8.0 %all-to-all-start.1 = ((bf16[16,64,128]{2,1,0:T(8,128)(2,1)}), bf16[16,64,128]{2,1,0:T(8,128)(2,1)S(1)}, u32[]{:S(2)}, u32[]{:S(2)}) async-start(bf16[16,64,128]{2,1,0:T(8,128)(2,1)} %bitcast.153), calls=%async_computation.1 | async-start | bytes 524288 | tf_op jit(solution)/shard_map/all_to_all | solution.py:753
  116.9 2.9 collective-permute-start.19
  119.8 7.4 %all-to-all-done.1 = bf16[16,64,128]{2,1,0:T(8,128)(2,1)S(1)} async-done(((bf16[16,64,128]{2,1,0:T(8,128)(2,1)}), bf16[16,64,128]{2,1,0:T(8,128)(2,1)S(1)}, u32[]{:S(2)}, u32[]{:S(2)}) %all-to-all-start.1) | async-done | bytes 262176 | tf_op jit(solution)/shard_map/all_to_all | solution.py:753
  131.3 6.3 %collective-permute-done.19.refs_3_ = bf16[2,2,2,32,512]{4,3,2,1,0:T(8,128)(2,1)S(1)} collective-permute-done((bf16[2,2,2,32,512]{4,3,2,1,0:T(8,128)(2,1)S(1)}, bf16[2,2,2,32,512]{4,3,2,1,0:T(8,128)(2,1)S(1)}, u32[]{:S(2)}, u32[]{:S(2)}) %collective-permute-start.19) | collective-permute-done | bytes 262176 | tf_op jit(solution)/shard_map/ppermute | solution.py:507
  140.7 3.0 shard_map.172
  143.7 4.9 %shard_map.173 = (bf16[256,512]{1,0:T(8,128)(2,1)}, bf16[256,512]{1,0:T(8,128)(2,1)}, f32[128,1024]{1,0:T(8,128)}, bf16[128,1024]{1,0:T(8,128)(2,1)}, f32[128,1024]{1,0:T(8,128)}, /*index=5*/bf16[128,1024]{1,0:T(8,128)(2,1)}) custom-call(s32[1]{0:T(128)} %bitcast.38.place_ref, bf16[128,1024]{1,0:T(8,128)(2,1)} %copy-done.10, bf16[128,1024]{1,0:T(8,128)(2,1)} %copy-done.32, ...), custom_call_target="tpu_custom_call" | custom-call | flops 1 | bytes 1 | tf_op jit(solution)/shard_map/pallas_call | solution.py:254
  151.7 6.3 %shard_map.174 = (bf16[512,512]{1,0:T(8,128)(2,1)}, bf16[512,512]{1,0:T(8,128)(2,1)}, f32[128,1024]{1,0:T(8,128)}, f32[128,1024]{1,0:T(8,128)}, bf16[128,1024]{1...) custom-call(s32[1]{0:T(128)} %bitcast.38.place_ref, ...), custom_call_target="tpu_custom_call" | custom-call | flops 1 | bytes 1 | tf_op jit(solution)/shard_map/pallas_call | solution.py:254
  160.4 4.8 %shard_map.175 = (bf16[256,512]{1,0:T(8,128)(2,1)}, bf16[256,512]{1,0:T(8,128)(2,1)}, f32[128,1024]{1,0:T(8,128)}, bf16[128,1024]{1,0:T(8,128)(2,1)}, f32[128,1024]{1,0:T(8,128)}, /*index=5*/bf16[128,1024]{1,0:T(8,128)(2,1)}) custom-call(s32[1]{0:T(128)} %bitcast.38.place_ref, bf16[128,1024]{1,0:T(8,128)(2,1)} %copy-done.33, bf16[128,1024]{1,0:T(8,128)(2,1)} %copy-done.34, ...), custom_call_target="tpu_custom_call" | custom-call | flops 1 | bytes 1 | tf_op jit(solution)/shard_map/pallas_call | solution.py:254
  170.3 6.2 %collective-permute-done.27 = bf16[128,1024]{1,0:T(8,128)(2,1)S(1)} collective-permute-done((bf16[128,1024]{1,0:T(8,128)(2,1)S(1)}, bf16[128,1024]{1,0:T(8,128)(2,1)S(1)}, u32[]{:S(2)}, u32[]{:S(2)}) %collective-permute-start.27) | collective-permute-done | bytes 262176 | tf_op jit(solution)/shard_map/ppermute | solution.py:502
  178.4 6.3 %shard_map.176 = (bf16[256,512]{1,0:T(8,128)(2,1)}, bf16[256,512]{1,0:T(8,128)(2,1)}, bf16[256,512]{1,0:T(8,128)(2,1)}, bf16[256,512]{1,0:T(8,128)(2,1)}, bf16[1...) custom-call(s32[5]{0:T(128)} %stack.106.at_ref, ...), custom_call_target="tpu_custom_call" | custom-call | flops 30000001024 | bytes 1 | tf_op jit(solution)/shard_map/pallas_call | solution.py:254
  190.9 3.3 %shard_map.177 = (bf16[2,4,32,1024]{3,2,1,0:T(8,128)(2,1)}, bf16[2,4,32,1024]{3,2,1,0:T(8,128)(2,1)}, bf16[2,4,32,1024]{3,2,1,0:T(8,128)(2,1)}, bf16[2,4,32,1024]{3,2,1,0:T(8,128)(2,1)}) custom-call(s32[11]{0:T(128)} %stack.105.at_ref, bf16[1024,128]{1,0:T(8,128)(2,1)} %bitcast.152, bf16[128,1024]{1,0:T(8,128)(2,1)} %copy-done.8), custom_call_target="tpu_custom_call" | custom-call | flops 30000001024 | bytes 1 | tf_op jit(solution)/shard_map/pallas_call | solution.py:254
  194.7 4.8 %all-to-all-start.2 = ((bf16[16,64,128]{2,1,0:T(8,128)(2,1)}), bf16[16,64,128]{2,1,0:T(8,128)(2,1)}, u32[]{:S(2)}, u32[]{:S(2)}) async-start(bf16[16,64,128]{2,1,0:T(8,128)(2,1)} %bitcast.53), calls=%async_computation.2 | async-start | bytes 524288 | tf_op jit(solution)/shard_map/all_to_all | solution.py:824
  206.5 5.9 %all-to-all-done.2 = bf16[16,64,128]{2,1,0:T(8,128)(2,1)} async-done(((bf16[16,64,128]{2,1,0:T(8,128)(2,1)}), bf16[16,64,128]{2,1,0:T(8,128)(2,1)}, u32[]{:S(2)}, u32[]{:S(2)}) %all-to-all-start.2) | async-done | bytes 262176 | tf_op jit(solution)/shard_map/all_to_all | solution.py:824
  214.9 17.4 %shard_map.178 = (bf16[4,2,2,192,128]{4,3,2,1,0:T(8,128)(2,1)}, bf16[192,1024]{1,0:T(8,128)(2,1)}, bf16[192,1024]{1,0:T(8,128)(2,1)}) custom-call(s32[1]{0:T(128)} %bitcast.34.core_ref, bf16[192,1024]{1,0:T(8,128)(2,1)} %get-tuple-element.184.own_ref, bf16[192,1024]{1,0:T(8,128)(2,1)} %copy-done.28, s32[1,2048]{1,0:T(1,128)} %bitcast.162, ...), custom_call_target="tpu_custom_call" | custom-call | flops 30000001024 | bytes 1 | tf_op jit(solution)/shard_map/pallas_call | solution.py:188
  238.0 15.4 %all-to-all-start.3 = ((bf16[16,192,128]{2,1,0:T(8,128)(2,1)}), bf16[16,192,128]{2,1,0:T(8,128)(2,1)}, u32[]{:S(2)}, u32[]{:S(2)}) async-start(bf16[16,192,128]{2,1,0:T(8,128)(2,1)} %bitcast.56), calls=%async_computation.3 | async-start | bytes 1572864 | tf_op jit(solution)/shard_map/all_to_all | solution.py:845
  261.0 5.4 %collective-permute-done.50 = bf16[2,2,32,512]{3,2,0,1:T(8,128)(2,1)S(1)} collective-permute-done((bf16[2,2,32,512]{3,2,0,1:T(8,128)(2,1)S(1)}, bf16[2,2,32,512]{3,2,0,1:T(8,128)(2,1)S(1)}, u32[]{:S(2)}, u32[]{:S(2)}) %collective-permute-start.50) | collective-permute-done | bytes 131104 | tf_op jit(solution)/shard_map/ppermute | solution.py:502
  268.6 3.4 %collective-permute-done.51.far_ref = bf16[2,2,32,512]{3,2,1,0:T(8,128)(2,1)S(1)} collective-permute-done((bf16[2,2,32,512]{3,2,1,0:T(8,128)(2,1)S(1)}, bf16[2,2,32,512]{3,2,1,0:T(8,128)(2,1)S(1)}, u32[]{:S(2)}, u32[]{:S(2)}) %collective-permute-start.51) | collective-permute-done | bytes 131104 | tf_op jit(solution)/shard_map/ppermute | solution.py:502
  277.6 3.5 %collective-permute-start.53 = (bf16[128,1024]{1,0:T(8,128)(2,1)}, bf16[128,1024]{1,0:T(8,128)(2,1)}, u32[]{:S(2)}, u32[]{:S(2)}) collective-permute-start(bf16[128,1024]{1,0:T(8,128)(2,1)} %get-tuple-element.313), channel_id=1, source_target_pairs={{0,24},{2,26},{4,28},{6,30},{8,0},{10,2},{12,4},{14,6},{16,8},{18,... | collective-permute-start | bytes 786440 | tf_op jit(solution)/shard_map/ppermute | solution.py:507
  285.7 4.6 %all-to-all-start.4 = ((bf16[32,32,192]{2,1,0:T(8,128)(2,1)}), bf16[32,32,192]{2,1,0:T(8,128)(2,1)S(1)}, u32[]{:S(2)}, u32[]{:S(2)}) async-start(bf16[32,32,192]{2,1,0:T(8,128)(2,1)} %bitcast.57), calls=%async_computation.4 | async-start | bytes 1048576 | tf_op jit(solution)/shard_map/all_to_all | solution.py:867
  290.4 6.5 %shard_map.179 = bf16[128,1024]{1,0:T(8,128)(2,1)} custom-call(bf16[3072,128]{1,0:T(8,128)(2,1)} %bitcast.58.got_ref, bf16[1024,3072]{1,0:T(8,128)(2,1)} %all-gather.7.cloned.1.call-done.weight_ref, f32[128,1024]{1,0:T(8,128)} %get-tuple-element.323.hat_ref, f32[128,1]{1,0:T(8,128)} %copy.42.inverse_ref, f32[128,1024]{1,0:T(8,128)} %get-tuple-element.319.middle_ref), custom_call_target="tpu_custom_call" | custom-call | flops 30000001024 | bytes 1 | tf_op jit(solution)/shard_map/pallas_call | solution.py:407
  303.6 7.8 %collective-permute-done.54 = bf16[128,1024]{1,0:T(8,128)(2,1)} collective-permute-done((bf16[128,1024]{1,0:T(8,128)(2,1)}, bf16[128,1024]{1,0:T(8,128)(2,1)}, u32[]{:S(2)}, u32[]{:S(2)}) %collective-permute-start.54) | collective-permute-done | bytes 262176 | tf_op jit(solution)/shard_map/ppermute | solution.py:507
  313.2 5.7 %collective-permute-done.48 = bf16[32,1024]{1,0:T(8,128)(2,1)S(1)} collective-permute-done((bf16[32,1024]{1,0:T(8,128)(2,1)S(1)}, bf16[32,1024]{1,0:T(8,128)(2,1)S(1)}, u32[]{:S(2)}, u32[]{:S(2)}) %collective-permute-start.48) | collective-permute-done | bytes 65568 | tf_op jit(solution)/shard_map/ppermute | solution.py:507
  (307 shorter events, 116.9 us)
Async XLA Ops:
  7.2 120.1 %all-gather.5.cloned.1.call-start = ((), (), s32[]{:S(2)}) async-start(), calls=%async_computation.5 | async-start | bytes 2162688 | tf_op jit(solution)/shard_map/all_gather | solution.py:625
  29.8 29.1 %collective-permute-start.5 = (bf16[384,1024]{1,0:T(8,128)(2,1)S(1)}, bf16[384,1024]{1,0:T(8,128)(2,1)S(1)}, u32[]{:S(2)}, u32[]{:S(2)}) collective-permute-start(bf16[384,1024]{1,0:T(8,128)(2,1)S(1)} %pad_maximum_fusion), channel_id=1, source_target_pairs={{0,4},{2,6},{4,0},{6,2},{8,12},{10,14},{12,8},{14,10},{16,20},{18,... | collective-permute-start | bytes 2359304 | tf_op jit(solution)/shard_map/ppermute | solution.py:502
  33.0 25.8 %all-to-all-start = ((bf16[32,32,192]{2,1,0:T(8,128)(2,1)}), bf16[32,32,192]{2,1,0:T(8,128)(2,1)S(1)}, u32[]{:S(2)}, u32[]{:S(2)}) async-start(bf16[32,32,192]{2,1,0:T(8,128)(2,1)} %bitcast.14), calls=%async_computation | async-start | bytes 1048576 | tf_op jit(solution)/shard_map/all_to_all | solution.py:690
  36.5 101.1 %all-gather.9.cloned.1.call-start = ((), (), s32[]{:S(2)}) async-start(), calls=%async_computation.7 | async-start | bytes 2359296 | tf_op jit(solution)/shard_map/all_gather | solution.py:737
  37.6 21.3 %collective-permute-start.6 = (bf16[2,2,32,512]{3,2,0,1:T(8,128)(2,1)S(1)}, bf16[2,2,32,512]{3,2,0,1:T(8,128)(2,1)S(1)}, u32[]{:S(2)}, u32[]{:S(2)}) collective-permute-start(bf16[2,2,32,512]{3,2,0,1:T(8,128)(2,1)S(1)} %get-tuple-element.168), channel_id=1, source_target_pairs={{0,4},{2,6},{4,0},{6,2},{8,12},{10,14},{12,8},{14,10},{16,20},{18,... | collective-permute-start | bytes 393224 | tf_op jit(solution)/shard_map/ppermute | solution.py:502
  39.4 19.4 %collective-permute-start.4 = (bf16[64,1024]{1,0:T(8,128)(2,1)S(1)}, bf16[64,1024]{1,0:T(8,128)(2,1)S(1)}, u32[]{:S(2)}, u32[]{:S(2)}) collective-permute-start(bf16[64,1024]{1,0:T(8,128)(2,1)S(1)} %slice.25), channel_id=1, source_target_pairs={{0,24},{2,26},{4,28},{6,30},{8,0},{10,2},{12,4},{14,6},{16,8},{18,... | collective-permute-start | bytes 393224 | tf_op jit(solution)/shard_map/ppermute | solution.py:507
  59.7 20.8 %collective-permute-start.8 = (bf16[192,1024]{1,0:T(8,128)(2,1)S(1)}, bf16[192,1024]{1,0:T(8,128)(2,1)S(1)}, u32[]{:S(2)}, u32[]{:S(2)}) collective-permute-start(bf16[192,1024]{1,0:T(8,128)(2,1)S(1)} %bitcast.146), channel_id=1, source_target_pairs={{0,2},{2,0},{4,6},{6,4},{8,10},{10,8},{12,14},{14,12},{16,18},{18,... | collective-permute-start | bytes 1179656 | tf_op jit(solution)/shard_map/ppermute | solution.py:502
  61.9 18.6 %collective-permute-start.11 = (bf16[128,1024]{1,0:T(8,128)(2,1)}, bf16[128,1024]{1,0:T(8,128)(2,1)S(1)}, u32[]{:S(2)}, u32[]{:S(2)}) collective-permute-start(bf16[128,1024]{1,0:T(8,128)(2,1)} %refs_4_.1), channel_id=1, source_target_pairs={{0,24},{2,26},{4,28},{6,30},{8,0},{10,2},{12,4},{14,6},{16,8},{18,... | collective-permute-start | bytes 786440 | tf_op jit(solution)/shard_map/ppermute | solution.py:507
  64.4 16.1 %collective-permute-start.7 = (bf16[128,1024]{1,0:T(8,128)(2,1)}, bf16[128,1024]{1,0:T(8,128)(2,1)}, u32[]{:S(2)}, u32[]{:S(2)}) collective-permute-start(bf16[128,1024]{1,0:T(8,128)(2,1)} %pad_maximum_fusion.1), channel_id=1, source_target_pairs={{0,4},{2,6},{4,0},{6,2},{8,12},{10,14},{12,8},{14,10},{16,20},{18,... | collective-permute-start | bytes 786440 | tf_op jit(solution)/shard_map/ppermute | solution.py:502
  86.6 21.4 %collective-permute-start.13 = (bf16[128,1024]{1,0:T(8,128)(2,1)S(1)}, bf16[128,1024]{1,0:T(8,128)(2,1)S(1)}, u32[]{:S(2)}, u32[]{:S(2)}) collective-permute-start(bf16[128,1024]{1,0:T(8,128)(2,1)S(1)} %copy-done.29), channel_id=1, source_target_pairs={{0,16},{2,18},{4,20},{6,22},{8,24},{10,26},{12,28},{14,30},{16,0},... | collective-permute-start | bytes 786440 | tf_op jit(solution)/shard_map/ppermute | solution.py:507
  89.6 18.4 %collective-permute-start.14 = (bf16[2,2,2,32,512]{4,3,2,1,0:T(8,128)(2,1)S(1)}, bf16[2,2,2,32,512]{4,3,2,1,0:T(8,128)(2,1)S(1)}, u32[]{:S(2)}, u32[]{:S(2)}) collective-permute-start(bf16[2,2,2,32,512]{4,3,2,1,0:T(8,128)(2,1)S(1)} %pad_maximum_fusion.2.refs_0_), channel_id=1, source_target_pairs={{0,8},{2,10},{4,12},{6,14},{8,16},{10,18},{12,20},{14,22},{16,24},... | collective-permute-start | bytes 786440 | tf_op jit(solution)/shard_map/ppermute | solution.py:507
  90.2 18.4 %collective-permute-start.15 = (bf16[2,2,2,32,512]{4,3,2,1,0:T(8,128)(2,1)S(1)}, bf16[2,2,2,32,512]{4,3,2,1,0:T(8,128)(2,1)S(1)}, u32[]{:S(2)}, u32[]{:S(2)}) collective-permute-start(bf16[2,2,2,32,512]{4,3,2,1,0:T(8,128)(2,1)S(1)} %pad_maximum_fusion.2.refs_0_), channel_id=1, source_target_pairs={{0,24},{2,26},{4,28},{6,30},{8,0},{10,2},{12,4},{14,6},{16,8},{18,... | collective-permute-start | bytes 786440 | tf_op jit(solution)/shard_map/ppermute | solution.py:507
  108.7 18.6 %all-to-all-start.1 = ((bf16[16,64,128]{2,1,0:T(8,128)(2,1)}), bf16[16,64,128]{2,1,0:T(8,128)(2,1)S(1)}, u32[]{:S(2)}, u32[]{:S(2)}) async-start(bf16[16,64,128]{2,1,0:T(8,128)(2,1)} %bitcast.153), calls=%async_computation.1 | async-start | bytes 524288 | tf_op jit(solution)/shard_map/all_to_all | solution.py:753
  116.7 96.9 %all-gather.7.cloned.1.call-start = ((), (), s32[]{:S(2)}) async-start(), calls=%async_computation.6 | async-start | bytes 6488064 | tf_op jit(solution)/shard_map/all_gather | solution.py:763
  116.9 20.7 %collective-permute-start.19 = (bf16[2,2,2,32,512]{4,3,2,1,0:T(8,128)(2,1)S(1)}, bf16[2,2,2,32,512]{4,3,2,1,0:T(8,128)(2,1)S(1)}, u32[]{:S(2)}, u32[]{:S(2)}) collective-permute-start(bf16[2,2,2,32,512]{4,3,2,1,0:T(8,128)(2,1)S(1)} %pad_maximum_fusion.2.refs_0_), channel_id=1, source_target_pairs={{0,16},{2,18},{4,20},{6,22},{8,24},{10,26},{12,28},{14,30},{16,0},... | collective-permute-start | bytes 786440 | tf_op jit(solution)/shard_map/ppermute | solution.py:507
  169.1 18.5 %collective-permute-start.20 = (bf16[128,1024]{1,0:T(8,128)(2,1)S(1)}, bf16[128,1024]{1,0:T(8,128)(2,1)S(1)}, u32[]{:S(2)}, u32[]{:S(2)}) collective-permute-start(bf16[128,1024]{1,0:T(8,128)(2,1)S(1)} %copy-done.58), channel_id=1, source_target_pairs={{0,2},{2,0},{4,6},{6,4},{8,10},{10,8},{12,14},{14,12},{16,18},{18,... | collective-permute-start | bytes 786440 | tf_op jit(solution)/shard_map/ppermute | solution.py:502
  190.8 21.7 %collective-permute-start.35 = (bf16[1024,1024]{1,0:T(8,128)(2,1)S(1)}, bf16[1024,1024]{1,0:T(8,128)(2,1)}, u32[]{:S(2)}, u32[]{:S(2)}) collective-permute-start(bf16[1024,1024]{1,0:T(8,128)(2,1)S(1)} %bitcast.143), channel_id=1, source_target_pairs={{0,2},{2,0},{4,6},{6,4},{8,10},{10,8},{12,14},{14,12},{16,18},{18,... | collective-permute-start | bytes 6291464 | tf_op jit(solution)/shard_map/ppermute | solution.py:502
  194.7 17.7 %collective-permute-start.37 = (bf16[2,4,32,1024]{3,2,1,0:T(8,128)(2,1)}, bf16[2,4,32,1024]{3,2,1,0:T(8,128)(2,1)S(1)}, u32[]{:S(2)}, u32[]{:S(2)}) collective-permute-start(bf16[2,4,32,1024]{3,2,1,0:T(8,128)(2,1)} %get-tuple-element.260), channel_id=1, source_target_pairs={{0,2},{2,0},{4,6},{6,4},{8,10},{10,8},{12,14},{14,12},{16,18},{18,... | collective-permute-start | bytes 1572872 | tf_op jit(solution)/shard_map/ppermute | solution.py:502
  194.7 17.7 %all-to-all-start.2 = ((bf16[16,64,128]{2,1,0:T(8,128)(2,1)}), bf16[16,64,128]{2,1,0:T(8,128)(2,1)}, u32[]{:S(2)}, u32[]{:S(2)}) async-start(bf16[16,64,128]{2,1,0:T(8,128)(2,1)} %bitcast.53), calls=%async_computation.2 | async-start | bytes 524288 | tf_op jit(solution)/shard_map/all_to_all | solution.py:824
  201.7 30.7 %collective-permute-start.41 = (bf16[256,512]{1,0:T(8,128)(2,1)}, bf16[256,512]{1,0:T(8,128)(2,1)}, u32[]{:S(2)}, u32[]{:S(2)}) collective-permute-start(bf16[256,512]{1,0:T(8,128)(2,1)} %get-tuple-element.273), channel_id=1, source_target_pairs={{0,16},{2,18},{4,20},{6,22},{8,24},{10,26},{12,28},{14,30},{16,0},... | collective-permute-start | bytes 786440 | tf_op jit(solution)/shard_map/ppermute | solution.py:507
  204.4 27.9 %collective-permute-start.40 = (bf16[256,512]{1,0:T(8,128)(2,1)}, bf16[256,512]{1,0:T(8,128)(2,1)}, u32[]{:S(2)}, u32[]{:S(2)}) collective-permute-start(bf16[256,512]{1,0:T(8,128)(2,1)} %get-tuple-element.271), channel_id=1, source_target_pairs={{0,24},{2,26},{4,28},{6,30},{8,0},{10,2},{12,4},{14,6},{16,8},{18,... | collective-permute-start | bytes 786440 | tf_op jit(solution)/shard_map/ppermute | solution.py:507
  205.9 26.5 %collective-permute-start.39 = (bf16[256,512]{1,0:T(8,128)(2,1)}, bf16[256,512]{1,0:T(8,128)(2,1)}, u32[]{:S(2)}, u32[]{:S(2)}) collective-permute-start(bf16[256,512]{1,0:T(8,128)(2,1)} %get-tuple-element.269), channel_id=1, source_target_pairs={{0,8},{2,10},{4,12},{6,14},{8,16},{10,18},{12,20},{14,22},{16,24},... | collective-permute-start | bytes 786440 | tf_op jit(solution)/shard_map/ppermute | solution.py:507
  214.9 17.5 %collective-permute-start.38 = (bf16[2,4,32,1024]{3,2,1,0:T(8,128)(2,1)S(1)}, bf16[2,4,32,1024]{3,2,1,0:T(8,128)(2,1)}, u32[]{:S(2)}, u32[]{:S(2)}) collective-permute-start(bf16[2,4,32,1024]{3,2,1,0:T(8,128)(2,1)S(1)} %add.294), channel_id=1, source_target_pairs={{0,4},{2,6},{4,0},{6,2},{8,12},{10,14},{12,8},{14,10},{16,20},{18,... | collective-permute-start | bytes 1572872 | tf_op jit(solution)/shard_map/ppermute | solution.py:502
  234.1 42.0 %collective-permute-start.43 = (bf16[128,1024]{1,0:T(8,128)(2,1)}, bf16[128,1024]{1,0:T(8,128)(2,1)}, u32[]{:S(2)}, u32[]{:S(2)}) collective-permute-start(bf16[128,1024]{1,0:T(8,128)(2,1)} %add_convert_fusion.2), channel_id=1, source_target_pairs={{0,4},{2,6},{4,0},{6,2},{8,12},{10,14},{12,8},{14,10},{16,20},{18,... | collective-permute-start | bytes 786440 | tf_op jit(solution)/shard_map/ppermute | solution.py:502
  238.0 38.1 %collective-permute-start.42 = (bf16[128,1024]{1,0:T(8,128)(2,1)}, bf16[128,1024]{1,0:T(8,128)(2,1)}, u32[]{:S(2)}, u32[]{:S(2)}) collective-permute-start(bf16[128,1024]{1,0:T(8,128)(2,1)} %add_convert_fusion.3), channel_id=1, source_target_pairs={{0,4},{2,6},{4,0},{6,2},{8,12},{10,14},{12,8},{14,10},{16,20},{18,... | collective-permute-start | bytes 786440 | tf_op jit(solution)/shard_map/ppermute | solution.py:502
  238.0 38.1 %all-to-all-start.3 = ((bf16[16,192,128]{2,1,0:T(8,128)(2,1)}), bf16[16,192,128]{2,1,0:T(8,128)(2,1)}, u32[]{:S(2)}, u32[]{:S(2)}) async-start(bf16[16,192,128]{2,1,0:T(8,128)(2,1)} %bitcast.56), calls=%async_computation.3 | async-start | bytes 1572864 | tf_op jit(solution)/shard_map/all_to_all | solution.py:845
  276.1 26.6 %collective-permute-start.52 = (bf16[128,1024]{1,0:T(8,128)(2,1)}, bf16[128,1024]{1,0:T(8,128)(2,1)S(1)}, u32[]{:S(2)}, u32[]{:S(2)}) collective-permute-start(bf16[128,1024]{1,0:T(8,128)(2,1)} %get-tuple-element.311), channel_id=1, source_target_pairs={{0,8},{2,10},{4,12},{6,14},{8,16},{10,18},{12,20},{14,22},{16,24},... | collective-permute-start | bytes 786440 | tf_op jit(solution)/shard_map/ppermute | solution.py:507
  277.6 26.0 %collective-permute-start.53 = (bf16[128,1024]{1,0:T(8,128)(2,1)}, bf16[128,1024]{1,0:T(8,128)(2,1)}, u32[]{:S(2)}, u32[]{:S(2)}) collective-permute-start(bf16[128,1024]{1,0:T(8,128)(2,1)} %get-tuple-element.313), channel_id=1, source_target_pairs={{0,24},{2,26},{4,28},{6,30},{8,0},{10,2},{12,4},{14,6},{16,8},{18,... | collective-permute-start | bytes 786440 | tf_op jit(solution)/shard_map/ppermute | solution.py:507
  281.1 30.3 %collective-permute-start.54 = (bf16[128,1024]{1,0:T(8,128)(2,1)}, bf16[128,1024]{1,0:T(8,128)(2,1)}, u32[]{:S(2)}, u32[]{:S(2)}) collective-permute-start(bf16[128,1024]{1,0:T(8,128)(2,1)} %get-tuple-element.315), channel_id=1, source_target_pairs={{0,16},{2,18},{4,20},{6,22},{8,24},{10,26},{12,28},{14,30},{16,0},... | collective-permute-start | bytes 786440 | tf_op jit(solution)/shard_map/ppermute | solution.py:507
  285.7 33.9 %all-to-all-start.4 = ((bf16[32,32,192]{2,1,0:T(8,128)(2,1)}), bf16[32,32,192]{2,1,0:T(8,128)(2,1)S(1)}, u32[]{:S(2)}, u32[]{:S(2)}) async-start(bf16[32,32,192]{2,1,0:T(8,128)(2,1)} %bitcast.57), calls=%async_computation.4 | async-start | bytes 1048576 | tf_op jit(solution)/shard_map/all_to_all | solution.py:867
  297.0 16.3 %collective-permute-start.46 = (bf16[32,1024]{1,0:T(8,128)(2,1)S(1)}, bf16[32,1024]{1,0:T(8,128)(2,1)S(1)}, u32[]{:S(2)}, u32[]{:S(2)}) collective-permute-start(bf16[32,1024]{1,0:T(8,128)(2,1)S(1)} %get-tuple-element.331), channel_id=1, source_target_pairs={{0,8},{2,10},{4,12},{6,14},{8,16},{10,18},{12,20},{14,22},{16,24},... | collective-permute-start | bytes 196616 | tf_op jit(solution)/shard_map/ppermute | solution.py:507
  302.7 16.3 %collective-permute-start.48 = (bf16[32,1024]{1,0:T(8,128)(2,1)S(1)}, bf16[32,1024]{1,0:T(8,128)(2,1)S(1)}, u32[]{:S(2)}, u32[]{:S(2)}) collective-permute-start(bf16[32,1024]{1,0:T(8,128)(2,1)S(1)} %get-tuple-element.332), channel_id=1, source_target_pairs={{0,16},{2,18},{4,20},{6,22},{8,24},{10,26},{12,28},{14,30},{16,0},... | collective-permute-start | bytes 196616 | tf_op jit(solution)/shard_map/ppermute | solution.py:507
  (94 other events, 1006.1 us)
Sparse Core Ops, SparseCore 0:
  11.1 69.1 all-gather.4
  86.7 27.7 all-gather.8
  137.8 75.8 all-gather.6

commit v3 on v2

--- a/solution.py
+++ b/solution.py
@@ -30,12 +30,17 @@
     )
 
 
-def masked_scores(keys, queries, key_ids, query_ids, first):
+def masked_scores(keys, queries, key_ids, query_ids, row, first):
     scores = contract(keys, queries, 0, 0)
-    slots = lax.broadcasted_iota(jnp.int32, scores.shape, 0)
+    slots = row + lax.broadcasted_iota(jnp.int32, scores.shape, 0)
     columns = first + lax.broadcasted_iota(jnp.int32, scores.shape, 1)
     allowed = (key_ids == query_ids) | (slots == columns)
     return jnp.where(allowed, scores, MASKED)
+
+
+def chunks(length, step):
+    step = min(step, length)
+    return [slice(row, row + step) for row in range(0, length, step)]
 
 
 def load_heads(own_ref, other_ref, held, key_id_ref, key_column):
@@ -58,18 +63,30 @@
     block = attended_ref.shape[1]
     first = pl.multiple_of(step * block, block)
     queries = held[:HDIM, pl.ds(first, block)]
-    scores = masked_scores(
-        held[HDIM : 2 * HDIM, :], queries, key_column[...], query_id_ref[...], first
-    )
-    highest = jnp.max(scores, axis=0, keepdims=True)
-    expo = jnp.exp(scores - highest)
-    totals = jnp.sum(expo, axis=0, keepdims=True)
-    attended = contract(held[2 * HDIM :, :], expo.astype(BF16), 1, 0) / totals
+    scores, highest = [], None
+    parts = chunks(held.shape[1], 512)
+    for part in parts:
+        scores.append(
+            masked_scores(
+                held[HDIM : 2 * HDIM, part], queries, key_column[part], query_id_ref[...],
+                part.start, first,
+            )
+        )
+        top = jnp.max(scores[-1], axis=0, keepdims=True)
+        highest = top if highest is None else jnp.maximum(highest, top)
+    totals = attended = None
+    for part, score in zip(parts, scores):
+        expo = jnp.exp(score - highest)
+        total = jnp.sum(expo, axis=0, keepdims=True)
+        term = contract(held[2 * HDIM :, part], expo.astype(BF16), 1, 0)
+        totals = total if totals is None else totals + total
+        attended = term if attended is None else attended + term
+    attended = attended / totals
     attended_ref[...] = attended
     log_ref[...] = highest + jnp.log(totals)
     low = attended.astype(BF16)
-    for x in range(2):
-        mixed_ref[0, x, 0] = low[:, x * tokens : (x + 1) * tokens]
+    for index in range(block // tokens):
+        mixed_ref[index // 2, index % 2, 0] = low[:, index * tokens : (index + 1) * tokens]
 
 
 def backward_kernel(
@@ -90,21 +107,33 @@
     block = attended_ref.shape[1]
     first = pl.multiple_of(step * block, block)
     queries = held[:HDIM, pl.ds(first, block)]
-    keys = held[HDIM : 2 * HDIM, :]
-    grads = jnp.concatenate([grad_ref[0, x, 0] for x in range(2)], axis=1)
-    scores = masked_scores(keys, queries, key_column[...], query_id_ref[...], first)
-    probs = jnp.exp(scores - log_ref[...])
+    count = block // tokens
+    grads = jnp.concatenate(
+        [grad_ref[index // 2, index % 2, 0] for index in range(count)], axis=1
+    )
+    logs = log_ref[...]
     delta = jnp.sum(grads.astype(F32) * attended_ref[...], axis=0, keepdims=True)
-    dprob = contract(held[2 * HDIM :, :], grads, 0, 0)
-    dscore = (probs * (dprob - delta)).astype(BF16)
-    dq = (contract(keys, dscore, 1, 0) * SCALING).astype(BF16)
-    dk_sum[...] += contract(queries, dscore, 1, 1)
-    dv_sum[...] += contract(grads, probs.astype(BF16), 1, 1)
-    side = step // groups
+    dq = None
+    for part in chunks(held.shape[1], 1024):
+        keys = held[HDIM : 2 * HDIM, part]
+        scores = masked_scores(
+            keys, queries, key_column[part], query_id_ref[...], part.start, first
+        )
+        probs = jnp.exp(scores - logs)
+        dprob = contract(held[2 * HDIM :, part], grads, 0, 0)
+        dscore = (probs * (dprob - delta)).astype(BF16)
+        term = contract(keys, dscore, 1, 0)
+        dq = term if dq is None else dq + term
+        dk_sum[:, part] += contract(queries, dscore, 1, 1)
+        dv_sum[:, part] += contract(grads, probs.astype(BF16), 1, 1)
+    dq = (dq * SCALING).astype(BF16)
+    per_side = half // block
+    side = step // per_side
     core = jnp.where(side == 0, core_ref[0], 1 - core_ref[0])
-    for x in range(2):
-        out_ref[step % groups, x, core, :HDIM, :] = dq[:, x * tokens : (x + 1) * tokens]
-    inside = pl.multiple_of((step % groups) * block, block)
+    for index in range(count):
+        group = step % per_side * (count // 2) + index // 2
+        out_ref[group, index % 2, core, :HDIM, :] = dq[:, index * tokens : (index + 1) * tokens]
+    inside = pl.multiple_of((step % per_side) * block, block)
 
     @pl.when(side == 0)
     def _():
@@ -127,15 +156,15 @@
                     for x in range(2):
                         at = side_at * half + (2 * group + x) * tokens
                         out_ref[group, x, to_core, rows, :] = low[:, at : at + tokens]
-        if steps < 2 * groups:
+        if steps < 2 * (half // block):
             other_grad_ref[:HDIM, :] = jnp.zeros((HDIM, half), BF16)
             for group in range(groups):
                 for x in range(2):
                     out_ref[group, x, 1 - core_ref[0], :HDIM, :] = jnp.zeros((HDIM, tokens), BF16)
 
 
-def side_core(step, groups, core):
-    return jnp.where(step < groups, core, 1 - core)
+def side_core(step, per_side, core):
+    return jnp.where(step < per_side, core, 1 - core)
 
 
 def attention_specs(length, block, tokens, groups):
@@ -144,17 +173,18 @@
     part = pl.BlockSpec((HDIM, block), lambda i, core: (0, i))
     row = pl.BlockSpec((1, block), lambda i, core: (0, i))
     column = pl.BlockSpec((1, length), lambda i, core: (0, 0))
+    per_side = half // block
     tile = pl.BlockSpec(
-        (1, 2, 1, HDIM, tokens),
-        lambda i, core: (i % groups, 0, side_core(i, groups, core[0]), 0, 0),
+        (groups // per_side, 2, 1, HDIM, tokens),
+        lambda i, core: (i % per_side, 0, side_core(i, per_side, core[0]), 0, 0),
     )
     return whole, part, row, column, tile
 
 
 def attention_forward(core, own, other, key_ids, query_ids, tokens, splits):
     length = 2 * own.shape[1]
-    block = 2 * tokens
-    groups = length // (2 * block)
+    groups = length // (4 * tokens)
+    block = 4 * tokens if groups % 2 == 0 else 2 * tokens
     count = length // splits
     whole, part, row, column, tile = attention_specs(length, block, tokens, groups)
     return pl.pallas_call(
@@ -181,8 +211,8 @@
 def attention_backward(core, own, other, key_ids, query_ids, attended, logs, grads, tokens, splits):
     length = 2 * own.shape[1]
     half = length // 2
-    block = 2 * tokens
-    groups = length // (2 * block)
+    groups = length // (4 * tokens)
+    block = 4 * tokens if groups % 2 == 0 else 2 * tokens
     count = length // splits
     whole, part, row, column, tile = attention_specs(length, block, tokens, groups)
     return pl.pallas_call(
@@ -215,6 +245,21 @@
     )(core, own, other, key_ids, query_ids, attended, logs, grads)
 
 
+def standard_kernel(patches_ref, out_ref):
+    out_ref[...] = standardize(patches_ref[...].astype(F32))[0].astype(BF16)
+
+
+def standard_patches(patches):
+    return pl.pallas_call(
+        standard_kernel,
+        grid=(1,),
+        in_specs=[whole(patches)],
+        out_specs=whole(patches),
+        out_shape=jax.ShapeDtypeStruct(patches.shape, BF16),
+        cost_estimate=SMALL,
+    )(patches)
+
+
 def project_kernel(layout, tokens, where_ref, mine_w_ref, theirs_w_ref, *refs):
     pieces, (mine_ref, theirs_ref, all_ref) = refs[:-3], refs[-3:]
     for index, (source, row) in enumerate(layout):
@@ -319,40 +364,70 @@
     return outs[0], outs[1], list(outs[2 : 2 + count]), list(outs[2 + count :])
 
 
-def mlp_weight_kernel(counts, toggles, blocks, at_ref, *refs):
+def mlp_weight_kernel(counts, sizes, toggles, at_ref, *refs):
+    halves, batches, lines, hidden_rows = sizes
     hats, pres, hiddens = (
         refs[: counts[0]], refs[counts[0] : sum(counts[:2])], refs[sum(counts[:2]) : sum(counts)]
     )
     refs = refs[sum(counts) :]
-    all_ref, up_refs, down_refs = refs[0], refs[1 : 1 + blocks], refs[1 + blocks : 1 + 2 * blocks]
-    hat_held, hidden_held = refs[1 + 2 * blocks :]
-    hat_held[...] = together(hats)
-    hidden_held[...] = together(hiddens)
-    pre_grad = together(pres)
+    all_ref, out_refs, (up_held, down_held) = refs[0], refs[1:-2], refs[-2:]
     upstream = jnp.concatenate([all_ref[at_ref[0] ^ toggle] for toggle in toggles], axis=0)
-    for index in range(blocks):
-        for held, other, out_ref in (
-            (hat_held, pre_grad, up_refs[index]), (hidden_held, upstream, down_refs[index])
-        ):
-            wide = out_ref.shape[0]
-            columns = pl.ds(pl.multiple_of(at_ref[1 + index] * wide, wide), wide)
-            out_ref[...] = contract(held[:, columns], other, 0, 0).astype(BF16)
-
-
-def mlp_weight_terms(numbers, blocks, hats, toggles, pres, hiddens, upstream_all):
-    tokens = sum(hat.shape[0] for hat in hats)
+    up = contract(together(hats), together(pres), 0, 0).astype(BF16)
+    up_held[...] = up.reshape(up_held.shape)
+    down = contract(together(hiddens), upstream, 0, 0).astype(BF16)
+    down_held[...] = down.reshape(down_held.shape)
+    units = up_held.shape[-1]
+    for hop, out_ref in enumerate(out_refs):
+        b = at_ref[1 + halves + hop]
+        for step in range(halves):
+            g = at_ref[1 + step]
+            for quad in range(QUAD):
+                for z in range(2):
+                    first = (2 * quad + z) * lines
+                    out_ref[step, first : first + lines] = up_held[g, z, quad, b]
+            for part in range(2):
+                first = EIGHT * lines + part * hidden_rows
+                columns = slice(part * units, (part + 1) * units)
+                out_ref[step, first : first + hidden_rows] = down_held[g, b, :, columns]
+
+
+def mlp_weight_terms(numbers, sizes, hats, toggles, pres, hiddens, upstream_all):
+    halves, batches, lines, hidden_rows = sizes
     width, units = hats[0].shape[1], pres[0].shape[1]
     counts = (len(hats), len(pres), len(hiddens))
+    out = jax.ShapeDtypeStruct((halves, EIGHT * lines + 2 * hidden_rows, units), BF16)
     outs = whole_call(
-        functools.partial(mlp_weight_kernel, counts, toggles, blocks),
+        functools.partial(mlp_weight_kernel, counts, sizes, toggles),
         numbers,
         [*hats, *pres, *hiddens, upstream_all],
-        [jax.ShapeDtypeStruct((width // blocks, units), BF16)] * blocks
-        + [jax.ShapeDtypeStruct((units // blocks, width), BF16)] * blocks,
-        [pltpu.VMEM((tokens, width), BF16), pltpu.VMEM((tokens, units), BF16)],
+        [out] * batches,
+        [
+            pltpu.VMEM((halves, 2, QUAD, batches, lines, units), BF16),
+            pltpu.VMEM((halves, batches, hidden_rows, width), BF16),
+        ],
         LARGE,
     )
-    return list(outs[:blocks]), list(outs[blocks:])
+    return list(outs)
+
+
+def two_sums_kernel(count, *refs):
+    for index in range(count):
+        total = refs[index][...] + refs[count + index][...].astype(F32)
+        refs[2 * count + index][...] = total.astype(BF16)
+
+
+def two_sums(left, right, gate):
+    arrays = [*left, after(right[0], gate), *right[1:]]
+    outs = [jax.ShapeDtypeStruct(term.shape, BF16) for term in left]
+    return pl.pallas_call(
+        functools.partial(two_sums_kernel, len(left)),
+        grid=(1,),
+        in_specs=[whole(array) for array in arrays],
+        out_specs=[whole(out) for out in outs],
+        out_shape=outs,
+        compiler_params=pltpu.CompilerParams(vmem_limit_bytes=VMEM_LIMIT),
+        cost_estimate=LARGE,
+    )(*arrays)
 
 
 def out_weight_kernel(order, at_ref, mixed_ref, grad_ref, *refs):
@@ -377,13 +452,12 @@
         [mixed, grad],
         [jax.ShapeDtypeStruct((2, len(order), lines, width), BF16)] * 4,
         [pltpu.VMEM(shape, BF16)],
-        LARGE,
-    )
-
-
-def finish_input_kernel(got_ref, weight_ref, hat_ref, inverse_ref, middle_ref, out_ref, total):
+    )
+
+
+def finish_input_kernel(got_ref, weight_ref, patches_ref, middle_ref, out_ref, total):
     step = pl.program_id(0)
-    term = contract(got_ref[...], weight_ref[...], 0, 1)
+    term = contract(weight_ref[...], got_ref[...], 1, 0)
 
     @pl.when(step == 0)
     def _():
@@ -395,15 +469,16 @@
 
     @pl.when(step == pl.num_programs(0) - 1)
     def _():
-        grad = standardize_back(total[...], hat_ref[...], inverse_ref[...])
+        hat, inverse = standardize(patches_ref[...].astype(F32))
+        grad = standardize_back(total[...].T, hat, inverse)
         out_ref[...] = (middle_ref[...] + grad).astype(BF16)
 
 
-def finish_input(got, weight, hat, inverse, middle_grad):
+def finish_input(got, weight, patches, middle_grad):
     columns, tokens = got.shape
     width = weight.shape[0]
     block = columns // 4
-    rows = [hat, inverse, middle_grad]
+    rows = [patches, middle_grad]
     return pl.pallas_call(
         finish_input_kernel,
         grid=(4,),
@@ -414,7 +489,7 @@
         ],
         out_specs=pl.BlockSpec((tokens, width), lambda i: (0, 0)),
         out_shape=jax.ShapeDtypeStruct((tokens, width), BF16),
-        scratch_shapes=[pltpu.VMEM((tokens, width), F32)],
+        scratch_shapes=[pltpu.VMEM((width, tokens), F32)],
         compiler_params=pltpu.CompilerParams(vmem_limit_bytes=VMEM_LIMIT),
         cost_estimate=LARGE,
     )(got, weight, *rows)
@@ -432,16 +507,16 @@
             first = (kind * HEADS + head) * HDIM
             columns = slice(first, first + HDIM)
             part = term[:, kind * HDIM : (kind + 1) * HDIM]
-            out_ref[:, columns] = part * gains
+            out_ref[:, columns] = part * gains[:, :HDIM]
             part = part * weight_ref[:, columns].astype(F32)
             total = part if total is None else total + part
-    gain_grad_ref[...] = jnp.sum(total, axis=1, keepdims=True)
+    gain_grad_ref[...] = jnp.sum(total.T, axis=0, keepdims=True)
 
 
 def finish_qkv(gains, terms, weight):
     lines, columns = weight.shape
     outs = [
-        jax.ShapeDtypeStruct((lines, columns), F32), jax.ShapeDtypeStruct((lines, 1), F32)
+        jax.ShapeDtypeStruct((lines, columns), F32), jax.ShapeDtypeStruct((1, lines), F32)
     ]
     arrays = [gains, terms, weight]
     return pl.pallas_call(
@@ -456,24 +531,24 @@
 
 
 def finish_up_kernel(sizes, at_ref, gain_ref, near_ref, far_ref, weight_ref, out_ref, gain_grad_ref):
-    groups, batches = sizes
-    chunk = near_ref.shape[-1] // (groups * (batches // 2))
+    halves, batches = sizes
+    chunk = near_ref.shape[-1] // (halves * batches)
     gains = gain_ref[...]
     total = None
-    for y, ref in enumerate((near_ref, far_ref)):
+    for z, ref in enumerate((near_ref, far_ref)):
         for x in range(2):
             for core in range(2):
                 quad = 2 * (at_ref[0] ^ x) + (at_ref[1] ^ core)
                 term = ref[x, core].astype(F32)
-                for index in range(groups * (batches // 2)):
-                    group, pair = index // (batches // 2), index % (batches // 2)
-                    block = (QUAD * group + quad) * batches + 2 * pair + (at_ref[2] ^ y)
+                for index in range(halves * batches):
+                    group = 2 * (index // batches) + (at_ref[2] ^ z)
+                    block = (QUAD * group + quad) * batches + index % batches
                     columns = pl.ds(pl.multiple_of(block * chunk, chunk), chunk)
                     part = term[:, index * chunk : (index + 1) * chunk]
                     out_ref[:, columns] = part * gains
                     part = part * weight_ref[:, columns].astype(F32)
                     total = part if total is None else total + part
-    gain_grad_ref[...] = jnp.sum(total, axis=1, keepdims=True)
+    gain_grad_ref[...] = jnp.sum(total.T, axis=0, keepdims=True)
 
 
 def finish_up(at, gains, near, far, weight, sizes):
@@ -482,7 +557,7 @@
         functools.partial(finish_up_kernel, sizes),
         at,
         [gains, near, far, weight],
-        [jax.ShapeDtypeStruct((lines, columns), F32), jax.ShapeDtypeStruct((lines, 1), F32)],
+        [jax.ShapeDtypeStruct((lines, columns), F32), jax.ShapeDtypeStruct((1, lines), F32)],
     )
 
 
@@ -533,6 +608,56 @@
             right, left = right[: self.split], left[self.split :]
         self.right, self.left = self.shift(right, 1), self.shift(left, -1)
         return [self.right, self.left]
+
+
+class Reduce:
+    def __init__(self, block_at, ring, shift):
+        self.block_at, self.ring, self.shift = block_at, ring, shift
+        self.distance = ring // 2
+        self.got = self.half = None
+        if ring == 1:
+            self.sum = block_at(0)
+
+    def step(self, *gates):
+        distance, shift, block_at = self.distance, self.shift, self.block_at
+        if distance == 0:
+            return []
+        self.distance -= 1
+        if self.ring == 2:
+            self.got = [shift(after(block_at(1).astype(BF16), *gates), 1)]
+        elif self.got is None and self.ring % 2 == 0:
+            far = block_at(distance).astype(BF16)
+            self.half = far.shape[0] // 2
+            self.got = [
+                shift(after(far[: self.half], *gates), 1),
+                shift(after(far[self.half :], *gates), -1),
+            ]
+        else:
+            terms = [block_at(distance), block_at(-distance)]
+            if self.half is not None:
+                at = self.half
+                terms = [
+                    jnp.concatenate([terms[0][:at] + self.got[0], terms[0][at:]]),
+                    jnp.concatenate([terms[1][:at], terms[1][at:] + self.got[1]]),
+                ]
+                self.half = None
+            elif self.got is not None:
+                terms = [term + got for term, got in zip(terms, self.got)]
+            self.got = [
+                shift(after(term.astype(BF16), *gates), way)
+                for term, way in zip(terms, (1, -1))
+            ]
+        if self.distance == 0:
+            self.sum = block_at(0)
+            for got in self.got:
+                self.sum = self.sum + got
+        return self.got
+
+    def finish(self, *gates):
+        new = []
+        while self.distance > 0:
+            new = self.step(*gates)
+        return new
 
 
 def standardize(values):
@@ -574,14 +699,18 @@
     splits = seqs // HEADS
     lines = qkv_weight.shape[0]
     hidden_rows = down_weight.shape[0]
-    units = hidden_rows * groups * pairs
+    halves = groups // 2
+    units = hidden_rows * halves * batches
     at_seq = lax.axis_index("seq")
     at_batch = lax.axis_index("batch")
     group, at_x, at_core = at_seq // QUAD, (at_seq // 2) % 2, at_seq % 2
     pair, at_y = at_batch // 2, at_batch % 2
+    half_group, at_z = group // 2, group % 2
     quad = at_seq % QUAD
     along_groups = shifter("seq", seqs, QUAD)
     along_pairs = shifter("batch", batches, 2)
+    along_halves = shifter("seq", seqs, 2 * QUAD)
+    along_batch = shifter("batch", batches, 1)
     distances = sorted(range(groups), key=lambda step: min(step, groups - step))
     hops = [(step, hop) for hop in range(pairs) for step in distances]
 
@@ -590,6 +719,9 @@
 
     def flip_core(array, *gates):
         return flip(after(array, *gates), "seq", 1, seqs)
+
+    def flip_z(array, *gates):
+        return flip(after(array, *gates), "seq", QUAD, seqs)
 
     def flip_y(array, *gates):
         return flip(after(array, *gates), "batch", 1, batches)
@@ -604,56 +736,56 @@
         array = along_groups(array, step) if step else array
         return along_pairs(array, hop) if hop else array
 
-    def fetch(block, *gates):
+    def from_halves(block, *gates):
         block = after(block, *gates)
-        return [shifted(block, step, hop) for step, hop in hops[1:]]
-
-    def owners(hop_list=hops):
-        return [((group - step) % groups, (pair - hop) % pairs) for step, hop in hop_list]
+        return [along_halves(block, step) for step in range(1, halves)]
+
+    def from_batch(block, *gates):
+        block = after(block, *gates)
+        return [along_batch(block, hop) for hop in range(1, batches)]
 
     def deliver(terms, *gates):
         return [
             shifted(after(term, *gates), step, hop) for term, (step, hop) in zip(terms[1:], hops[1:])
         ]
 
-    def in_order(terms):
-        return [
-            pick(pick(terms, (group + step) % groups, 0), (pair + hop) % pairs, 0)
-            for step, hop in hops
-        ]
-
     out_full = lax.all_gather(out_weight, EVERY, axis=0, tiled=True)
     at, plan = [], []
-    for index, (g, p) in enumerate(owners()):
-        first = len(at)
-        at += [g, p]
-        for row, (y, x, c) in enumerate(
-            (y, x, c) for y in range(2) for x in range(2) for c in range(2)
-        ):
-            plan.append((index, (y, x, c), None, 0, (first, len(at), first + 1, len(at) + 1)))
-            at += [quad ^ (2 * x + c), at_y ^ y]
-        plan.append((len(hops) + index, slice(None), None, 1, (first, first + 1)))
+    for step in range(halves):
+        for hop in range(batches):
+            index = step * batches + hop
+            first = len(at)
+            at += [(half_group - step) % halves, (at_batch - hop) % batches]
+            for block in range(EIGHT):
+                z, x, c = block // 4, block // 2 % 2, block % 2
+                where = (first, len(at), len(at) + 1, first + 1)
+                plan.append((index, (z, x, c), None, 0, where))
+                at += [at_z ^ z, quad ^ (2 * x + c)]
+            plan.append((halves * batches + index, slice(None), None, 1, (first, first + 1)))
     place_numbers = jnp.stack(at).astype(jnp.int32)
     order = [(3 + 2 * index, 4 + 2 * index) for index in range(len(hops))]
     at = [at_x, at_core, at_y]
     for step, hop in hops:
         at += [(group + step) % groups, (pair + hop) % pairs]
     out_numbers = jnp.stack(at).astype(jnp.int32)
-    place_at = (4 * at_x + 2 * at_core + at_y).astype(jnp.int32)[None]
-    group_numbers = [(group + step) % groups for step in distances]
+    place_at = (4 * at_z + 2 * at_x + at_core).astype(jnp.int32)[None]
+    group_numbers = [(half_group + step) % halves for step in range(halves)]
+    group_numbers += [(at_batch + hop) % batches for hop in range(batches)]
     group_numbers = jnp.stack([place_at[0], *group_numbers]).astype(jnp.int32)
     core = at_core.astype(jnp.int32)[None]
-    sides = jnp.stack([at_x, at_core, at_y]).astype(jnp.int32)
+    sides = jnp.stack([at_x, at_core, at_z]).astype(jnp.int32)
     numbers = [place_numbers, out_numbers, place_at, group_numbers, core, sides]
 
     inputs = patches[0].astype(F32)
-    first_hat, first_inverse = standardize(inputs)
-    own = first_hat.astype(BF16)
+    own = standard_patches(patches[0])
     first_rows = first_gain.astype(F32)[:, None]
     second_rows = second_gain.astype(F32)[:, None]
+    wide_gains = [
+        jnp.broadcast_to(gains, (lines, 128)) for gains in (first_rows, second_rows)
+    ]
     ring = Ring(own, groups, along_groups, tokens // 2)
     rounds = [[own], ring.step()]
-    beside = []
+    beside = [flip_x(own)]
     qkv_rows = after(qkv_weight, own).astype(F32) * first_rows
     qkv_rows = qkv_rows.reshape(lines, 3, HEADS, HDIM).transpose(2, 0, 1, 3)
     scales = jnp.array([SCALING, 1.0, 1.0], F32)[:, None]
@@ -662,20 +794,21 @@
         (HEADS, splits * batches, lines, 3 * HDIM),
     ).reshape(devices, lines, 3 * HDIM)
     eights = [
-        [(QUAD * g + q) * batches + 2 * p + y for q in range(QUAD) for y in range(2)]
-        for g in range(groups)
-        for p in range(pairs)
+        [((2 * g + z) * QUAD + q) * batches + b for z in range(2) for q in range(QUAD)]
+        for g in range(halves)
+        for b in range(batches)
     ]
     qkv_part = qkv_rows.astype(BF16).transpose(1, 0, 2, 3).reshape(lines, 3 * width)
     up_rows = (after(up_weight, own).astype(F32) * second_rows).astype(BF16)
-    up_rows = up_rows.reshape(lines, groups, 2, 2, pairs, 2, hidden_rows)
-    up_rows = up_rows.transpose(2, 3, 5, 0, 1, 4, 6).reshape(2, 2, 2, lines, units)
+    up_rows = up_rows.reshape(lines, halves, 2, 2, 2, batches, hidden_rows)
+    up_rows = up_rows.transpose(3, 4, 2, 0, 1, 5, 6).reshape(2, 2, 2, lines, units)
     up_kept = pick(up_rows, at_core, 1)
     up_core = flip_core(pick(up_rows, 1 - at_core, 1))
-    rounds[1], up_core = join(rounds[1], up_core)
+    head_weight = lax.all_to_all(sent, EVERY, split_axis=0, concat_axis=0, tiled=True)
+    rounds[1], beside, up_core = join(rounds[1], beside, up_core)
 
     while ring.taken < groups // 2:
-        beside.append(flip_x(rows(*sum(rounds if len(rounds) == 2 else rounds[-1:], []))))
+        beside.append(flip_x(rows(*rounds[-1])))
         rounds.append(ring.step(*rounds[-1]))
     up_rows = jnp.stack([up_kept, up_core], axis=1)
     up_kept, up_x = pick(up_rows, at_x, 0), flip_x(pick(up_rows, 1 - at_x, 0), *rounds[1])
@@ -687,12 +820,10 @@
 
     ids = by_side(segment_ids[0])
     key_ids = jnp.where(by_side(kept_mask[0]) == 1, ids, -1)[None]
-    head_weight = lax.all_to_all(
-        after(sent, *rounds[1]), EVERY, split_axis=0, concat_axis=0, tiled=True
-    )
     farthest = rounds[-1]
-    rounds, beside, up_x, head_weight, ids, key_ids, numbers = join(
-        rounds, beside, up_x, head_weight, ids, key_ids, numbers
+    down_rows = [[down_weight, *from_batch(down_weight, *rounds[1])]]
+    rounds, beside, up_x, head_weight, ids, key_ids, numbers, down_rows = join(
+        rounds, beside, up_x, head_weight, ids, key_ids, numbers, down_rows
     )
 
     place_numbers, out_numbers, place_at, group_numbers, core, sides = numbers
@@ -701,16 +832,15 @@
     head_weight = head_weight.reshape(width, 3 * HDIM).T
     near_weight = flip_core(head_weight)
     up_rows = jnp.stack([up_kept, up_x], axis=0)
-    up_kept, up_y = pick(up_rows, at_y, 2), flip_y(pick(up_rows, 1 - at_y, 2))
-    down_around = fetch(down_weight, *farthest)
-    beside, near_weight, up_y, down_around[:-1] = join(
-        beside, near_weight, up_y, down_around[:-1]
-    )
-    up_packed = jnp.stack([up_kept, up_y], axis=0)
-    up_around = fetch(up_packed)
+    up_kept, up_z = pick(up_rows, at_z, 2), flip_z(pick(up_rows, 1 - at_z, 2))
+    down_far = from_halves(down_weight, *farthest)
+    beside, near_weight, up_z = join(beside, near_weight, up_z)
+    up_packed = jnp.stack([up_kept, up_z], axis=0)
+    up_far = from_halves(up_packed)
+    up_rows = [[up_packed, *from_batch(up_packed)]]
 
     pieces, layout, where = [own], [(0, 0)], [2 * group + at_x]
-    flipped = [(1, 0, 2 * group + 1 - at_x)]
+    flipped = [(0, 0, 2 * group + 1 - at_x)]
     for number in range(1, len(rounds)):
         steps = [number] if 2 * number == groups else [-number, number]
         spots = [2 * ((group + step) % groups) for step in steps]
@@ -720,11 +850,8 @@
             layout += [(len(pieces) + index, 0) for index in range(len(steps))]
         where += [spot + at_x for spot in spots]
         pieces += rounds[number]
-        first = tokens if number == 1 and groups > 2 else 0
-        flipped += [
-            (number, first + row * tokens, spot + 1 - at_x) for row, spot in enumerate(spots)
-        ]
-    layout += [(len(pieces) + number - 1, row) for number, row, spot in flipped]
+        flipped += [(number, row * tokens, spot + 1 - at_x) for row, spot in enumerate(spots)]
+    layout += [(len(pieces) + number, row) for number, row, spot in flipped]
     where += [spot for number, row, spot in flipped]
     pieces += beside
     where = jnp.stack(where).astype(jnp.int32)
@@ -733,6 +860,8 @@
     )
 
     other = flip_core(theirs)
+    first_own = first_own.reshape(length // 2, width)
+    first_other = flip_core(first_own)
     upstream = cotangent[0]
     upstream_all = lax.all_gather(
         after(upstream, mine), EVERY, axis=0, axis_index_groups=eights
@@ -746,151 +875,169 @@
     if splits > 1:
         filled = (jnp.arange(seqs, dtype=jnp.int32) % 2 == at_core)[:, None, None]
         mixed_blocks = jnp.where(filled, mixed_blocks, 0)
-    mixed_blocks, down_around, up_around[:-1] = join(
-        mixed_blocks, down_around, up_around[:-1]
-    )
+    mixed_blocks, down_rows, up_rows, down_far, first_other = join(
+        mixed_blocks, down_rows, up_rows, down_far, first_other
+    )
+    down_rows += [[block, *from_batch(block)] for block in down_far]
 
     mixed = lax.all_to_all(mixed_blocks, "seq", split_axis=0, concat_axis=0, tiled=True)
     if splits > 1:
         mixed = mixed.reshape(HEADS, splits, HDIM, tokens).sum(1)
-    mixed, out_full = join(mixed.reshape(width, tokens), out_full)
+    mixed, out_full, up_far, wide_gains = join(
+        mixed.reshape(width, tokens), out_full, up_far, wide_gains
+    )
+    up_rows += [[block, *from_batch(block)] for block in up_far]
+
+    qkv_full = lax.all_gather(after(qkv_part, mixed_blocks), EVERY, axis=0, tiled=True)
 
     middle = inputs + contract(mixed, out_full, 0, 0)
     second_hat, second_inverse = standardize(middle)
     second = second_hat.astype(BF16)
-    second_x, second_y, second_core = flip_x(second), flip_y(second), flip_core(second)
-    second_core, up_around, upstream_all = join(second_core, up_around, upstream_all)
-    qkv_full = lax.all_gather(after(qkv_part, second_core), EVERY, axis=0, tiled=True)
+    second_x, second_z, second_core = flip_x(second), flip_z(second), flip_core(second)
+    second_x, second_z, second_core, up_rows, down_rows, upstream_all = join(
+        second_x, second_z, second_core, up_rows, down_rows, upstream_all
+    )
+    second_xz = flip_x(second_z)
+    second_x_core, second_z_core = flip_core(second_x), flip_core(second_z)
     up_part, down_part = place(
         place_numbers,
-        [up_packed, *up_around, down_weight, *down_around],
+        sum(up_rows + down_rows, []),
         plan,
-        [(groups, QUAD, pairs, 2, lines, units), (groups, pairs, hidden_rows, width)],
+        [(halves, 2, QUAD, batches, lines, units), (halves, batches, hidden_rows, width)],
     )
     up_part = up_part.reshape(width, units)
     down_part = down_part.reshape(units, width)
 
     weights = (place_at, upstream_all, up_part, down_part)
-    hidden_near, pre_near, sum_near, grad_near = mlp([second, second_core], (0, 2), *weights)
-    second_x, second_y, grad_near = join(second_x, second_y, grad_near)
-    second_xy = flip_x(second_y)
-    second_x_core, second_y_core = flip_core(second_x), flip_core(second_y)
+    hidden_near, pre_near, sum_near, grad_near = mlp([second, second_core], (0, 1), *weights)
+    second_x_core, second_z_core, grad_near = join(second_x_core, second_z_core, grad_near)
     hidden_mid, pre_mid, sum_mid, grad_mid = mlp(
-        [second_x, second_y, second_x_core, second_y_core], (4, 1, 6, 3), *weights
-    )
-    second_xy, grad_mid = join(second_xy, grad_mid)
-    second_xy_core = flip_core(second_xy)
-    hidden_far, pre_far, sum_far, grad_far = mlp([second_xy, second_xy_core], (5, 7), *weights)
+        [second_x, second_z, second_x_core, second_z_core], (2, 4, 3, 5), *weights
+    )
+    second_xz, grad_mid = join(second_xz, grad_mid)
+    second_xz_core = flip_core(second_xz)
+    hidden_far, pre_far, sum_far, grad_far = mlp([second_xz, second_xz_core], (6, 7), *weights)
 
     far_sum = grad_far[0] + flip_core(grad_far[1])
     far_x = flip_x(far_sum.astype(BF16))
     x_sum = grad_mid[0] + flip_core(grad_mid[2])
-    y_sum = grad_mid[1] + flip_core(grad_mid[3])
+    z_sum = grad_mid[1] + flip_core(grad_mid[3])
     near_sum = grad_near[0] + flip_core(grad_near[1])
-    mid_x = flip_x(x_sum.astype(BF16), far_x)
-    mid_y = flip_y((y_sum + far_x).astype(BF16))
-    sum_other = [flip_core(term, far_sum) for term in (sum_near[1], *sum_mid[2:], sum_far[1])]
     seconds = [
-        second, second_core, second_x, second_y, second_x_core, second_y_core, second_xy,
-        second_xy_core,
+        second, second_core, second_x, second_z, second_x_core, second_z_core, second_xz,
+        second_xz_core,
     ]
-    toggles = (0, 2, 4, 1, 6, 3, 5, 7)
+    toggles = (0, 1, 2, 4, 3, 5, 6, 7)
     hiddens = [hidden_near, hidden_mid, hidden_far]
     pres = [pre_near, pre_mid, after(pre_far, far_sum)]
-    if pairs == 1:
-        up_terms, down_terms = mlp_weight_terms(
-            group_numbers, len(hops), seconds, toggles, pres, hiddens, upstream_all
+    if lines % 16 == 0 and hidden_rows % 16 == 0:
+        mlp_terms = mlp_weight_terms(
+            group_numbers, (halves, batches, lines, hidden_rows), seconds, toggles, pres, hiddens,
+            upstream_all,
         )
     else:
         up_terms = contract(rows(*seconds), rows(*pres), 0, 0).astype(BF16)
-        up_terms = up_terms.reshape(groups, QUAD, pairs, 2, lines, units).swapaxes(1, 2)
+        up_terms = up_terms.reshape(halves, 2, QUAD, batches, lines, units)
+        up_terms = up_terms.transpose(3, 0, 2, 1, 4, 5).reshape(batches, halves, -1, units)
         sorted_places = jnp.stack([place_at[0] ^ toggle for toggle in toggles])
         down_terms = jnp.take(upstream_all, sorted_places, axis=0).reshape(-1, width)
         down_terms = contract(rows(*hiddens), down_terms, 0, 0).astype(BF16)
-        down_terms = down_terms.reshape(groups, pairs, hidden_rows, width)
-        up_terms, down_terms = in_order(up_terms), in_order(down_terms)
-    mid_x, mid_y, up_terms, down_terms, sum_other = join(
-        mid_x, mid_y, up_terms, down_terms, sum_other
-    )
-    second_grad = near_sum + mid_x + mid_y
+        down_terms = down_terms.reshape(halves, batches, hidden_rows, 2, units)
+        down_terms = down_terms.transpose(1, 0, 3, 2, 4).reshape(batches, halves, -1, units)
+        mlp_terms = jnp.roll(
+            jnp.concatenate([up_terms, down_terms], axis=2), (-at_batch, -half_group), (0, 1)
+        )
+        mlp_terms = [mlp_terms[hop] for hop in range(batches)]
+    sum_other = [flip_core(term, far_sum) for term in (sum_near[1], *sum_mid[2:])]
+    sum_other.append(flip_core(sum_far[1], mlp_terms[0]))
+    far_x, sum_other[3] = join(far_x, sum_other[3])
+    mid_x = flip_x(x_sum.astype(BF16), far_x)
+    mid_z = flip_z((z_sum + far_x).astype(BF16))
+    over_batch = Reduce(lambda hop: mlp_terms[hop % batches], batches, along_batch)
+    over_batch.step()
+    mid_x, mid_z = join(mid_x, mid_z)
+    second_grad = near_sum + mid_x + mid_z
 
     middle_grad = upstream.astype(F32) + standardize_back(second_grad, second_hat, second_inverse)
     middle_low = middle_grad.astype(BF16)
     mixed_grad = contract(out_full, middle_low, 1, 1).astype(BF16)
-    up_got = deliver(up_terms, second_grad)
     sent = jnp.broadcast_to(
         mixed_grad.reshape(HEADS, 1, HDIM, tokens), (HEADS, splits, HDIM, tokens)
     ).reshape(seqs, HDIM, tokens)
     grads = lax.all_to_all(sent, "seq", split_axis=0, concat_axis=0, tiled=True)
-    out_kept, out_kept_x, out_sent, out_sent_x = out_weight_terms(
-        out_numbers, order, after(mixed, sent), middle_low,
-        (groups, 2, 2, pairs, 2, lines, width),
-    )
-    out_core, out_core_x = flip_core(out_sent), flip_core(out_sent_x)
-    first_own = first_own.reshape(length // 2, width)
-    first_other = flip_core(first_own, sent)
-    grads, first_other, out_core, out_core_x, qkv_full = join(
-        grads, first_other, out_core, out_core_x, qkv_full
-    )
+    far_part, x_part, z_part = two_sums(
+        [sum_far[0], *sum_mid[:2]], [sum_other[3], *sum_other[1:3]], sent
+    )
+    while over_batch.distance > 0:
+        over_batch.step()
+    grads, over_batch.got, qkv_full = join(grads, over_batch.got, qkv_full)
+    over_batch.sum = sum(over_batch.got, over_batch.block_at(0))
+    over_halves = Reduce(lambda step: over_batch.sum[step % halves], halves, along_halves)
 
     grads = grads.reshape(groups, 2, 2, HDIM, tokens)
-    out_x = flip_x(out_kept_x + out_core_x)
+    far_x, mid_x = flip_x(far_part), flip_x(x_part)
+    last_step = over_halves.finish(grads)
     project_grad, own_grad, other_grad = attention_backward(
         core, mine, other, key_ids, query_ids, attended, logs, grads, tokens, splits
     )
-    project_grad, own_grad, other_grad, out_x, up_got = join(
-        project_grad, own_grad, other_grad, out_x, up_got
+    project_grad, own_grad, other_grad, far_x, mid_x = join(
+        project_grad, own_grad, other_grad, far_x, mid_x
     )
 
     got = lax.all_to_all(
         project_grad.reshape(seqs, 3 * HDIM, tokens), "seq", split_axis=0, concat_axis=0, tiled=True
     )
-    up_sum = sum(up_got, up_terms[0]).astype(BF16).reshape(2, 2, 2, lines, units)
+    mlp_sum = sum(last_step, over_halves.block_at(0)).astype(BF16)
+    up_sum = mlp_sum[: EIGHT * lines].reshape(2, 2, 2, lines, units)
     up_kept, up_core = pick(up_sum, at_core, 1), flip_core(pick(up_sum, 1 - at_core, 1))
     up_rows = jnp.stack([up_kept, up_core], axis=1)
     up_kept, up_x = pick(up_rows, at_x, 0), flip_x(pick(up_rows, 1 - at_x, 0))
-    up_rows = jnp.stack([up_kept, up_x], axis=0)
-    up_kept, up_y = pick(up_rows, at_y, 2), flip_y(pick(up_rows, 1 - at_y, 2))
-    out_sum = out_kept + out_core + out_x
-    out_sum = out_sum[0] + flip_y(out_sum[1], got)
-    far_x = flip_x((sum_far[0] + after(sum_other[3], project_grad)).astype(BF16))
-    mid_x = flip_x((sum_mid[0] + after(sum_other[1], project_grad)).astype(BF16))
-    out_got = deliver([out_sum[index] for index in range(len(hops))])
+    out_kept, out_kept_x, out_sent, out_sent_x = out_weight_terms(
+        out_numbers, order, after(mixed, project_grad), middle_low,
+        (groups, 2, 2, pairs, 2, lines, width),
+    )
+    out_core, out_core_x = flip_core(out_sent), flip_core(out_sent_x)
+    out_x = flip_x(out_kept_x + out_core_x)
     qkv_terms = contract(first_own, own_grad, 0, 1)
     qkv_terms = qkv_terms + contract(first_other, other_grad, 0, 1)
     if splits > 1:
         got = got.reshape(HEADS, splits, 3 * HDIM, tokens).sum(1)
     qkv_terms = after(qkv_terms, got)
-    got, far_x, mid_x = join(got, far_x, mid_x)
-    down_got = deliver(down_terms, got)
+    mid_z = flip_z(z_part + far_x)
+    got, up_x, out_x, mid_z = join(got, up_x, out_x, mid_z)
 
     qkv_terms = lax.all_to_all(
         qkv_terms.astype(BF16).reshape(devices, lines, 3 * HDIM),
         EVERY, split_axis=0, concat_axis=0, tiled=True,
     )
-    mid_y = flip_y((sum_mid[1] + sum_other[2] + far_x).astype(BF16))
 
     input_grad = finish_input(
-        got.reshape(3 * width, tokens), qkv_full, first_hat, first_inverse, middle_grad
-    )
-    block_output = middle + (sum_near[0] + sum_other[0] + mid_x + mid_y)
+        got.reshape(3 * width, tokens), qkv_full, patches[0], middle_grad
+    )
+    up_rows = jnp.stack([up_kept, up_x], axis=0)
+    up_kept, up_z = pick(up_rows, at_z, 2), flip_z(pick(up_rows, 1 - at_z, 2))
+    out_sum = out_kept + out_core + out_x
+    out_sum = out_sum[0] + flip_y(out_sum[1])
+    out_got = deliver([out_sum[index] for index in range(len(hops))])
+    block_output = middle + (sum_near[0] + sum_other[0] + mid_x + mid_z)
     block_output = block_output.astype(BF16)
     qkv_terms, input_grad, block_output = join(qkv_terms, input_grad, block_output)
-    qkv_sum, first_gain_grad = finish_qkv(first_rows, qkv_terms, qkv_weight)
+    qkv_sum, first_gain_grad = finish_qkv(wide_gains[0], qkv_terms, qkv_weight)
     if hidden_rows % 128 == 0:
         up_sum, second_gain_grad = finish_up(
-            sides, second_rows, up_kept, up_y,
-            up_weight, (groups, batches),
+            sides, wide_gains[1], up_kept, up_z,
+            up_weight, (halves, batches),
         )
     else:
-        up_sum = jnp.stack([up_kept, up_y], axis=2)
-        for axis, at in ((0, at_x), (1, at_core), (2, at_y)):
+        up_sum = jnp.stack([up_kept, up_z], axis=2)
+        for axis, at in ((0, at_x), (1, at_core), (2, at_z)):
             up_sum = jnp.where(at == 0, up_sum, jnp.flip(up_sum, axis))
-        up_sum = up_sum.astype(F32).reshape(2, 2, 2, lines, groups, pairs, hidden_rows)
-        up_sum = up_sum.transpose(3, 4, 0, 1, 5, 2, 6).reshape(lines, -1)
+        up_sum = up_sum.astype(F32).reshape(2, 2, 2, lines, halves, batches, hidden_rows)
+        up_sum = up_sum.transpose(3, 4, 2, 0, 1, 5, 6).reshape(lines, -1)
         second_gain_grad = jnp.sum(up_weight.astype(F32) * up_sum, axis=1)
         up_sum = up_sum * second_rows
-    down_sum = sum(down_got, down_terms[0]).astype(F32).reshape(hidden_rows, width)
+    down_sum = mlp_sum[EIGHT * lines :].astype(F32).reshape(2, hidden_rows, units)
+    down_sum = jnp.concatenate([down_sum[0], down_sum[1]], axis=1)
     out_sum = sum(out_got, out_sum[0]).astype(F32)
 
     return (

time: 332 us -> 282 us (0.85)
  starting transfers between devices: 97 us -> 74.3 us
  waiting for transfers between devices: 89.4 us -> 72.3 us
  other arithmetic: 32.3 us -> 20 us
    ppermute x19 -> x15, waiting for transfers between devices: 39.7 us -> 22.2 us  [shift(): lax.ppermute(array, axis, [(i, (i + step * stride) % size) for i in range...]
    all_to_all x1, starting transfers between devices: 15.4 us -> 4.15 us  [local(): lax.all_to_all(project_grad.reshape(seqs, 3 * HDIM, tokens), 'seq', split...]
    ppermute x19 -> x15, starting transfers between devices: 36.2 us -> 27.4 us  [shift(): lax.ppermute(array, axis, [(i, (i + step * stride) % size) for i in range...]
    all_to_all x1, waiting for transfers between devices: 7.4 us -> 0.01 us  [local(): lax.all_to_all(mixed_blocks, 'seq', split_axis=0, concat_axis=0, tiled=True)]
    convert_element_type x5 -> x4, other arithmetic: 6.61 us -> 0.81 us  [the longest x1 0.66 us: local(): second_rows = second_gain.astype(F32)[:, None]]
    pallas_call x0 -> x2, Pallas kernels: none -> 4.54 us  [the longest x1 2.64 us: two_sums(): pl.pallas_call(functools.partial(two_sums_kernel, len(left)), grid=(1,),...]
    all_to_all x1, starting transfers between devices: 8.05 us -> 4.11 us  [local(): lax.all_to_all(mixed_blocks, 'seq', split_axis=0, concat_axis=0, tiled=True)]
    ppermute x36 -> x37, waiting for transfers between devices: 34.5 us -> 38.4 us  [flip(): return lax.ppermute(array, axis, [(i, i ^ bit) for i in range(size)])]
  transfers between devices with their start and end apart: 63 -> 60, of which waited for: 23 -> 20; matrix products, arithmetic and copies ran while one was open for 14% -> 13% of each run, Pallas kernels for 22% -> 26%
where the time goes in v3:
time: 282 us; the launch traced here: 281 us
  Pallas kernels  76 us (27%)
  starting transfers between devices  74.3 us (26%)
  waiting for transfers between devices  72.3 us (26%)
  other arithmetic  20 us (7%)
  local copies, waits for them, and re-layouts  17.2 us (6%)
  between operations  14.7 us (5%)
  matrix products  6.47 us (2%)
    ppermute x37, waiting for transfers between devices, flip(): return lax.ppermute(array, axis, [(i, i ^ bit) for i in range(size)])  38.4 us
    pallas_call x8, Pallas kernels, whole_call(): pl.pallas_call(kernel, grid=(1,), in_specs=[pl.BlockSpec(memory_space=plt...  36 us
    ppermute x15, starting transfers between devices, shift(): lax.ppermute(array, axis, [(i, (i + step * stride) % size) for i in range...  27.4 us
    ppermute x37, starting transfers between devices, flip(): return lax.ppermute(array, axis, [(i, i ^ bit) for i in range(size)])  24.5 us
    ppermute x15, waiting for transfers between devices, shift(): lax.ppermute(array, axis, [(i, (i + step * stride) % size) for i in range...  22.2 us
    pallas_call x1, Pallas kernels, attention_backward(): pl.pallas_call(functools.partial(backward_kernel, tokens), grid_spec=pltp...  15.5 us
    pallas_call x1, Pallas kernels, attention_forward(): pl.pallas_call(functools.partial(forward_kernel, tokens), grid_spec=pltpu...  11.1 us
    all_to_all x1, waiting for transfers between devices, local(): grads = lax.all_to_all(sent, 'seq', split_axis=0, concat_axis=0, tiled=True)  7.29 us
  transfers between devices with their start and end apart: 60, of which 20 were waited for; matrix products, arithmetic and copies ran while one was open for 13% of the time, Pallas kernels for 26%

profile of v3, /device:TPU:0, one launch (start us, length us, event | category | flops | bytes accessed | tf_op | source)
XLA Modules:
  0.0 281.0 jit_solution(17937420552886880197)
XLA Ops:
  9.8 3.0 %collective-permute-start = (bf16[128,1024]{1,0:T(8,128)(2,1)}, bf16[128,1024]{1,0:T(8,128)(2,1)S(1)}, u32[]{:S(2)}, u32[]{:S(2)}) collective-permute-start(bf16[128,1024]{1,0:T(8,128)(2,1)} %shard_map.170.refs_0_), channel_id=1, source_target_pairs={{0,8},{2,10},{4,12},{6,14},{8,16},{10,18},{12,20},{14,22},{16,24},... | collective-permute-start | bytes 786440 | tf_op jit(solution)/shard_map/ppermute | solution.py:582
  20.9 3.2 %all-to-all-start = ((bf16[32,32,192]{2,1,0:T(8,128)(2,1)}), bf16[32,32,192]{2,1,0:T(8,128)(2,1)S(1)}, u32[]{:S(2)}, u32[]{:S(2)}) async-start(bf16[32,32,192]{2,1,0:T(8,128)(2,1)} %bitcast.14), calls=%async_computation | async-start | bytes 1048576 | tf_op jit(solution)/shard_map/all_to_all | solution.py:807
  24.2 2.6 collective-permute-done.1.refs_2_
  30.8 2.8 collective-permute-start.5
  41.6 7.1 %collective-permute-done.7 = bf16[2,2,32,512]{3,2,0,1:T(8,128)(2,1)S(1)} collective-permute-done((bf16[2,2,32,512]{3,2,0,1:T(8,128)(2,1)}, bf16[2,2,32,512]{3,2,0,1:T(8,128)(2,1)S(1)}, u32[]{:S(2)}, u32[]{:S(2)}) %collective-permute-start.7) | collective-permute-done | bytes 131104 | tf_op jit(solution)/shard_map/ppermute | solution.py:577
  53.9 3.3 %collective-permute-done.11 = bf16[2,2,32,512]{3,2,1,0:T(8,128)(2,1)S(1)} collective-permute-done((bf16[2,2,32,512]{3,2,1,0:T(8,128)(2,1)S(1)}, bf16[2,2,32,512]{3,2,1,0:T(8,128)(2,1)S(1)}, u32[]{:S(2)}, u32[]{:S(2)}) %collective-permute-start.11) | collective-permute-done | bytes 131104 | tf_op jit(solution)/shard_map/ppermute | solution.py:577
  59.6 5.2 %shard_map.171 = (bf16[192,1024]{1,0:T(8,128)(2,1)}, bf16[192,1024]{1,0:T(8,128)(2,1)}, bf16[8,128,1024]{2,1,0:T(8,128)(2,1)}) custom-call(s32[8]{0:T(128)} %stack.92.where_ref, bf16[192,1024]{1,0:T(8,128)(2,1)} %bitcast.142, bf16[192,1024]{1,0:T(8,128)(2,1)} %copy-done.25, bf16[128,1024]{1,0:T(8,128)(2,1)} %shard_map.170.refs_0_, ...), custom_call_target="tpu_custom_call" | custom-call | flops 1 | bytes 1 | tf_op jit(solution)/shard_map/pallas_call | solution.py:299
  70.5 11.1 %shard_map.172 = (bf16[4,2,2,64,128]{4,3,2,1,0:T(8,128)(2,1)}, f32[64,2048]{1,0:T(8,128)}, f32[1,2048]{1,0:T(1,128)}) custom-call(s32[1]{0:T(128)} %bitcast.34.core_ref, bf16[192,1024]{1,0:T(8,128)(2,1)} %get-tuple-element.176.own_ref, bf16[192,1024]{1,0:T(8,128)(2,1)} %collective-permute-done.12.other_ref, s32[1,2048]{1,0:T(1,128)} %bitcast.158, ...), custom_call_target="tpu_custom_call" | custom-call | flops 1 | bytes 1 | tf_op jit(solution)/shard_map/pallas_call | solution.py:190
  83.0 4.1 %all-to-all-start.1 = ((bf16[16,64,128]{2,1,0:T(8,128)(2,1)}), bf16[16,64,128]{2,1,0:T(8,128)(2,1)S(1)}, u32[]{:S(2)}, u32[]{:S(2)}) async-start(bf16[16,64,128]{2,1,0:T(8,128)(2,1)} %bitcast.151), calls=%async_computation.1 | async-start | bytes 524288 | tf_op jit(solution)/shard_map/all_to_all | solution.py:883
  87.1 2.9 %collective-permute-start.16 = (bf16[2,2,2,32,512]{4,3,2,1,0:T(8,128)(2,1)S(1)}, bf16[2,2,2,32,512]{4,3,2,1,0:T(8,128)(2,1)S(1)}, u32[]{:S(2)}, u32[]{:S(2)}) collective-permute-start(bf16[2,2,2,32,512]{4,3,2,1,0:T(8,128)(2,1)S(1)} %pad_maximum_fusion.3.refs_0_), channel_id=1, source_target_pairs={{0,16},{2,18},{4,20},{6,22},{8,24},{10,26},{12,28},{14,30},{16,0},... | collective-permute-start | bytes 786440 | tf_op jit(solution)/shard_map/ppermute | solution.py:582
  91.2 14.5 %collective-permute-done.16.refs_2_ = bf16[2,2,2,32,512]{4,3,2,1,0:T(8,128)(2,1)S(1)} collective-permute-done((bf16[2,2,2,32,512]{4,3,2,1,0:T(8,128)(2,1)S(1)}, bf16[2,2,2,32,512]{4,3,2,1,0:T(8,128)(2,1)S(1)}, u32[]{:S(2)}, u32[]{:S(2)}) %collective-permute-start.16) | collective-permute-done | bytes 262176 | tf_op jit(solution)/shard_map/ppermute | solution.py:582
  109.7 3.1 %collective-permute-start.17 = (bf16[128,1024]{1,0:T(8,128)(2,1)S(1)}, bf16[128,1024]{1,0:T(8,128)(2,1)S(1)}, u32[]{:S(2)}, u32[]{:S(2)}) collective-permute-start(bf16[128,1024]{1,0:T(8,128)(2,1)S(1)} %fusion.1.refs_0_), channel_id=1, source_target_pairs={{0,4},{2,6},{4,0},{6,2},{8,12},{10,14},{12,8},{14,10},{16,20},{18,... | collective-permute-start | bytes 786440 | tf_op jit(solution)/shard_map/ppermute | solution.py:577
  116.0 2.4 collective-permute-done.17.refs_0_.refs_2_
  120.6 3.7 %collective-permute-done.20.refs_3_ = bf16[2,2,2,32,512]{4,3,2,1,0:T(8,128)(2,1)S(1)} collective-permute-done((bf16[2,2,2,32,512]{4,3,2,1,0:T(8,128)(2,1)S(1)}, bf16[2,2,2,32,512]{4,3,2,1,0:T(8,128)(2,1)S(1)}, u32[]{:S(2)}, u32[]{:S(2)}) %collective-permute-start.20) | collective-permute-done | bytes 262176 | tf_op jit(solution)/shard_map/ppermute | solution.py:582
  125.2 3.0 %shard_map.173 = (bf16[2,2,4,2,32,512]{5,4,3,2,1,0:T(8,128)(2,1)}, bf16[2,2,128,1024]{3,2,1,0:T(8,128)(2,1)}) custom-call(s32[72]{0:T(128)} %stack.105.at_ref, bf16[2,2,2,32,512]{4,3,2,1,0:T(8,128)(2,1)} %copy-done.12, bf16[2,2,2,32,512]{4,3,2,1,0:T(8,128)(2,1)} %collective-permute-done.13.refs_1_, bf16[2,2,2,32,512]{4,3,2,1,0:T(8,128)(2,1)} %copy-done.31, ...), custom_call_target="tpu_custom_call" | custom-call | flops 1 | bytes 1 | tf_op jit(solution)/shard_map/pallas_call | solution.py:299
  128.2 4.8 %shard_map.174 = (bf16[256,512]{1,0:T(8,128)(2,1)}, bf16[256,512]{1,0:T(8,128)(2,1)}, f32[128,1024]{1,0:T(8,128)}, bf16[128,1024]{1,0:T(8,128)(2,1)}, f32[128,1024]{1,0:T(8,128)}, /*index=5*/bf16[128,1024]{1,0:T(8,128)(2,1)}) custom-call(s32[1]{0:T(128)} %bitcast.39.place_ref, bf16[128,1024]{1,0:T(8,128)(2,1)} %copy-done.11, bf16[128,1024]{1,0:T(8,128)(2,1)} %copy-done.29, ...), custom_call_target="tpu_custom_call" | custom-call | flops 1 | bytes 1 | tf_op jit(solution)/shard_map/pallas_call | solution.py:299
  133.9 6.3 %shard_map.175 = (bf16[512,512]{1,0:T(8,128)(2,1)}, bf16[512,512]{1,0:T(8,128)(2,1)}, f32[128,1024]{1,0:T(8,128)}, f32[128,1024]{1,0:T(8,128)}, bf16[128,1024]{1...) custom-call(s32[1]{0:T(128)} %bitcast.39.place_ref, ...), custom_call_target="tpu_custom_call" | custom-call | flops 1 | bytes 1 | tf_op jit(solution)/shard_map/pallas_call | solution.py:299
  142.5 4.8 %shard_map.176 = (bf16[256,512]{1,0:T(8,128)(2,1)}, bf16[256,512]{1,0:T(8,128)(2,1)}, f32[128,1024]{1,0:T(8,128)}, bf16[128,1024]{1,0:T(8,128)(2,1)}, f32[128,1024]{1,0:T(8,128)}, /*index=5*/bf16[128,1024]{1,0:T(8,128)(2,1)}) custom-call(s32[1]{0:T(128)} %bitcast.39.place_ref, bf16[128,1024]{1,0:T(8,128)(2,1)} %copy-done.30, bf16[128,1024]{1,0:T(8,128)(2,1)} %copy-done.33, ...), custom_call_target="tpu_custom_call" | custom-call | flops 1 | bytes 1 | tf_op jit(solution)/shard_map/pallas_call | solution.py:299
  151.9 6.7 %shard_map.177 = (bf16[2,512,512]{2,1,0:T(8,128)(2,1)}, bf16[2,512,512]{2,1,0:T(8,128)(2,1)}) custom-call(s32[5]{0:T(128)} %stack.115.at_ref, bf16[128,1024]{1,0:T(8,128)(2,1)} %copy-done.11, bf16[128,1024]{1,0:T(8,128)(2,1)} %copy-done.29, bf16[128,1024]{1,0:T(8,128)(2,1)} %copy-done.36, bf16[128,1024]{1,0:T(8,128)(2,1)} %copy-done.37, ...), custom_call_target="tpu_custom_call" | custom-call | flops 30000001024 | bytes 1 | tf_op jit(solution)/shard_map/pallas_call | solution.py:299
  161.8 2.5 collective-permute-start.34
  164.5 11.2 %collective-permute-done.31 = bf16[128,1024]{1,0:T(8,128)(2,1)S(1)} collective-permute-done((bf16[128,1024]{1,0:T(8,128)(2,1)S(1)}, bf16[128,1024]{1,0:T(8,128)(2,1)S(1)}, u32[]{:S(2)}, u32[]{:S(2)}) %collective-permute-start.31) | collective-permute-done | bytes 262176 | tf_op jit(solution)/shard_map/ppermute | solution.py:577
  179.0 4.5 %all-to-all-start.2 = ((bf16[16,64,128]{2,1,0:T(8,128)(2,1)}), bf16[16,64,128]{2,1,0:T(8,128)(2,1)S(1)}, u32[]{:S(2)}, u32[]{:S(2)}) async-start(bf16[16,64,128]{2,1,0:T(8,128)(2,1)} %bitcast.56), calls=%async_computation.2 | async-start | bytes 524288 | tf_op jit(solution)/shard_map/all_to_all | solution.py:967
  184.3 2.6 shard_map.179
  188.9 7.3 %all-to-all-done.2 = bf16[16,64,128]{2,1,0:T(8,128)(2,1)S(1)} async-done(((bf16[16,64,128]{2,1,0:T(8,128)(2,1)}), bf16[16,64,128]{2,1,0:T(8,128)(2,1)S(1)}, u32[]{:S(2)}, u32[]{:S(2)}) %all-to-all-start.2) | async-done | bytes 262176 | tf_op jit(solution)/shard_map/all_to_all | solution.py:967
  198.3 15.5 %shard_map.178 = (bf16[4,2,2,192,128]{4,3,2,1,0:T(8,128)(2,1)}, bf16[192,1024]{1,0:T(8,128)(2,1)}, bf16[192,1024]{1,0:T(8,128)(2,1)}) custom-call(s32[1]{0:T(128)} %bitcast.34.core_ref, bf16[192,1024]{1,0:T(8,128)(2,1)} %get-tuple-element.176.own_ref, bf16[192,1024]{1,0:T(8,128)(2,1)} %collective-permute-done.12.other_ref, s32[1,2048]{1,0:T(1,128)} %bitcast.159, ...), custom_call_target="tpu_custom_call" | custom-call | flops 30000001024 | bytes 1 | tf_op jit(solution)/shard_map/pallas_call | solution.py:218
  213.8 4.2 %all-to-all-start.3 = ((bf16[16,192,128]{2,1,0:T(8,128)(2,1)}), bf16[16,192,128]{2,1,0:T(8,128)(2,1)S(1)}, u32[]{:S(2)}, u32[]{:S(2)}) async-start(bf16[16,192,128]{2,1,0:T(8,128)(2,1)} %bitcast.149), calls=%async_computation.3 | async-start | bytes 1572864 | tf_op jit(solution)/shard_map/all_to_all | solution.py:987
  218.0 3.1 %shard_map.180 = (bf16[2,4,32,1024]{3,2,1,0:T(8,128)(2,1)}, bf16[2,4,32,1024]{3,2,1,0:T(8,128)(2,1)}, bf16[2,4,32,1024]{3,2,1,0:T(8,128)(2,1)}, bf16[2,4,32,1024]{3,2,1,0:T(8,128)(2,1)}) custom-call(s32[11]{0:T(128)} %stack.112.at_ref, bf16[1024,128]{1,0:T(8,128)(2,1)} %bitcast.137, bf16[128,1024]{1,0:T(8,128)(2,1)} %copy-done.1), custom_call_target="tpu_custom_call" | custom-call | flops 1 | bytes 1 | tf_op jit(solution)/shard_map/pallas_call | solution.py:299
  233.4 3.6 %all-to-all-done.3 = bf16[16,192,128]{2,1,0:T(8,128)(2,1)S(1)} async-done(((bf16[16,192,128]{2,1,0:T(8,128)(2,1)}), bf16[16,192,128]{2,1,0:T(8,128)(2,1)S(1)}, u32[]{:S(2)}, u32[]{:S(2)}) %all-to-all-start.3) | async-done | bytes 786464 | tf_op jit(solution)/shard_map/all_to_all | solution.py:987
  238.2 6.4 %all-to-all-start.4 = ((bf16[32,32,192]{2,1,0:T(8,128)(2,1)}), bf16[32,32,192]{2,1,0:T(8,128)(2,1)S(1)}, u32[]{:S(2)}, u32[]{:S(2)}) async-start(bf16[32,32,192]{2,1,0:T(8,128)(2,1)} %bitcast.60), calls=%async_computation.4 | async-start | bytes 1048576 | tf_op jit(solution)/shard_map/all_to_all | solution.py:1009
  244.6 5.7 %collective-permute-done.41 = bf16[2,2,32,512]{3,2,0,1:T(8,128)(2,1)} collective-permute-done((bf16[2,2,32,512]{3,2,0,1:T(8,128)(2,1)}, bf16[2,2,32,512]{3,2,0,1:T(8,128)(2,1)}, u32[]{:S(2)}, u32[]{:S(2)}) %collective-permute-start.41) | collective-permute-done | bytes 131104 | tf_op jit(solution)/shard_map/ppermute | solution.py:577
  253.5 6.5 %shard_map.181 = bf16[128,1024]{1,0:T(8,128)(2,1)} custom-call(bf16[3072,128]{1,0:T(8,128)(2,1)} %bitcast.148, bf16[1024,3072]{1,0:T(8,128)(2,1)} %all-gather.7.cloned.1.call-done.weight_ref, bf16[128,1024]{1,0:T(8,128)(2,1)} %bitcast.147, f32[128,1024]{1,0:T(8,128)} %get-tuple-element.299.middle_ref), custom_call_target="tpu_custom_call" | custom-call | flops 30000001024 | bytes 1 | tf_op jit(solution)/shard_map/pallas_call | solution.py:482
  260.5 3.1 %collective-permute-start.50 = (bf16[32,1024]{1,0:T(8,128)(2,1)S(1)}, bf16[32,1024]{1,0:T(8,128)(2,1)S(1)}, u32[]{:S(2)}, u32[]{:S(2)}) collective-permute-start(bf16[32,1024]{1,0:T(8,128)(2,1)S(1)} %get-tuple-element.312), channel_id=1, source_target_pairs={{0,16},{2,18},{4,20},{6,22},{8,24},{10,26},{12,28},{14,30},{16,0},... | collective-permute-start | bytes 196616 | tf_op jit(solution)/shard_map/ppermute | solution.py:582
  (285 shorter events, 95.7 us)
Async XLA Ops:
  7.2 98.5 %all-gather.5.cloned.1.call-start = ((), (), s32[]{:S(2)}) async-start(), calls=%async_computation.5 | async-start | bytes 2162688 | tf_op jit(solution)/shard_map/all_gather | solution.py:752
  9.8 14.3 %collective-permute-start = (bf16[128,1024]{1,0:T(8,128)(2,1)}, bf16[128,1024]{1,0:T(8,128)(2,1)S(1)}, u32[]{:S(2)}, u32[]{:S(2)}) collective-permute-start(bf16[128,1024]{1,0:T(8,128)(2,1)} %shard_map.170.refs_0_), channel_id=1, source_target_pairs={{0,8},{2,10},{4,12},{6,14},{8,16},{10,18},{12,20},{14,22},{16,24},... | collective-permute-start | bytes 786440 | tf_op jit(solution)/shard_map/ppermute | solution.py:582
  12.9 13.9 %collective-permute-start.1 = (bf16[128,1024]{1,0:T(8,128)(2,1)}, bf16[128,1024]{1,0:T(8,128)(2,1)S(1)}, u32[]{:S(2)}, u32[]{:S(2)}) collective-permute-start(bf16[128,1024]{1,0:T(8,128)(2,1)} %shard_map.170.refs_0_), channel_id=1, source_target_pairs={{0,24},{2,26},{4,28},{6,30},{8,0},{10,2},{12,4},{14,6},{16,8},{18,... | collective-permute-start | bytes 786440 | tf_op jit(solution)/shard_map/ppermute | solution.py:582
  20.9 27.8 %all-to-all-start = ((bf16[32,32,192]{2,1,0:T(8,128)(2,1)}), bf16[32,32,192]{2,1,0:T(8,128)(2,1)S(1)}, u32[]{:S(2)}, u32[]{:S(2)}) async-start(bf16[32,32,192]{2,1,0:T(8,128)(2,1)} %bitcast.14), calls=%async_computation | async-start | bytes 1048576 | tf_op jit(solution)/shard_map/all_to_all | solution.py:807
  24.1 100.2 %all-gather.9.cloned.1.call-start = ((), (), s32[]{:S(2)}) async-start(), calls=%async_computation.7 | async-start | bytes 2359296 | tf_op jit(solution)/shard_map/all_gather | solution.py:866
  26.8 21.9 %collective-permute-start.6 = (bf16[256,1024]{1,0:T(8,128)(2,1)S(1)}, bf16[256,1024]{1,0:T(8,128)(2,1)S(1)}, u32[]{:S(2)}, u32[]{:S(2)}) collective-permute-start(bf16[256,1024]{1,0:T(8,128)(2,1)S(1)} %pad_maximum_fusion), channel_id=1, source_target_pairs={{0,4},{2,6},{4,0},{6,2},{8,12},{10,14},{12,8},{14,10},{16,20},{18,... | collective-permute-start | bytes 1572872 | tf_op jit(solution)/shard_map/ppermute | solution.py:577
  33.6 15.1 %collective-permute-start.8 = (bf16[128,1024]{1,0:T(8,128)(2,1)}, bf16[128,1024]{1,0:T(8,128)(2,1)S(1)}, u32[]{:S(2)}, u32[]{:S(2)}) collective-permute-start(bf16[128,1024]{1,0:T(8,128)(2,1)} %refs_4_), channel_id=1, source_target_pairs={{0,1},{1,0},{2,3},{3,2},{4,5},{5,4},{6,7},{7,6},{8,9},{9,8},{10,11... | collective-permute-start | bytes 786440 | tf_op jit(solution)/shard_map/ppermute | solution.py:582
  64.8 131.5 %all-gather.7.cloned.1.call-start = ((), (), s32[]{:S(2)}) async-start(), calls=%async_computation.6 | async-start | bytes 6488064 | tf_op jit(solution)/shard_map/all_gather | solution.py:891
  64.8 16.8 %collective-permute-start.15 = (bf16[1024,1024]{1,0:T(8,128)(2,1)}, bf16[1024,1024]{1,0:T(8,128)(2,1)S(1)}, u32[]{:S(2)}, u32[]{:S(2)}) collective-permute-start(bf16[1024,1024]{1,0:T(8,128)(2,1)} %bitcast.138), channel_id=1, source_target_pairs={{0,2},{2,0},{4,6},{6,4},{8,10},{10,8},{12,14},{14,12},{16,18},{18,... | collective-permute-start | bytes 6291464 | tf_op jit(solution)/shard_map/ppermute | solution.py:577
  65.4 16.2 %collective-permute-start.14 = (bf16[128,1024]{1,0:T(8,128)(2,1)}, bf16[128,1024]{1,0:T(8,128)(2,1)}, u32[]{:S(2)}, u32[]{:S(2)}) collective-permute-start(bf16[128,1024]{1,0:T(8,128)(2,1)} %refs_4_), channel_id=1, source_target_pairs={{0,16},{2,18},{4,20},{6,22},{8,24},{10,26},{12,28},{14,30},{16,0},... | collective-permute-start | bytes 786440 | tf_op jit(solution)/shard_map/ppermute | solution.py:582
  67.6 14.0 %collective-permute-start.13 = (bf16[2,2,2,32,512]{4,3,2,1,0:T(8,128)(2,1)S(1)}, bf16[2,2,2,32,512]{4,3,2,1,0:T(8,128)(2,1)}, u32[]{:S(2)}, u32[]{:S(2)}) collective-permute-start(bf16[2,2,2,32,512]{4,3,2,1,0:T(8,128)(2,1)S(1)} %pad_maximum_fusion.3.refs_0_), channel_id=1, source_target_pairs={{0,1},{1,0},{2,3},{3,2},{4,5},{5,4},{6,7},{7,6},{8,9},{9,8},{10,11... | collective-permute-start | bytes 786440 | tf_op jit(solution)/shard_map/ppermute | solution.py:582
  83.0 22.7 %all-to-all-start.1 = ((bf16[16,64,128]{2,1,0:T(8,128)(2,1)}), bf16[16,64,128]{2,1,0:T(8,128)(2,1)S(1)}, u32[]{:S(2)}, u32[]{:S(2)}) async-start(bf16[16,64,128]{2,1,0:T(8,128)(2,1)} %bitcast.151), calls=%async_computation.1 | async-start | bytes 524288 | tf_op jit(solution)/shard_map/all_to_all | solution.py:883
  87.1 18.6 %collective-permute-start.16 = (bf16[2,2,2,32,512]{4,3,2,1,0:T(8,128)(2,1)S(1)}, bf16[2,2,2,32,512]{4,3,2,1,0:T(8,128)(2,1)S(1)}, u32[]{:S(2)}, u32[]{:S(2)}) collective-permute-start(bf16[2,2,2,32,512]{4,3,2,1,0:T(8,128)(2,1)S(1)} %pad_maximum_fusion.3.refs_0_), channel_id=1, source_target_pairs={{0,16},{2,18},{4,20},{6,22},{8,24},{10,26},{12,28},{14,30},{16,0},... | collective-permute-start | bytes 786440 | tf_op jit(solution)/shard_map/ppermute | solution.py:582
  90.0 26.0 %collective-permute-start.21 = (bf16[128,1024]{1,0:T(8,128)(2,1)}, bf16[128,1024]{1,0:T(8,128)(2,1)S(1)}, u32[]{:S(2)}, u32[]{:S(2)}) collective-permute-start(bf16[128,1024]{1,0:T(8,128)(2,1)} %collective-permute-done.14.refs_6_), channel_id=1, source_target_pairs={{0,1},{1,0},{2,3},{3,2},{4,5},{5,4},{6,7},{7,6},{8,9},{9,8},{10,11... | collective-permute-start | bytes 786440 | tf_op jit(solution)/shard_map/ppermute | solution.py:582
  124.8 15.4 %collective-permute-start.25 = (bf16[128,1024]{1,0:T(8,128)(2,1)S(1)}, bf16[128,1024]{1,0:T(8,128)(2,1)S(1)}, u32[]{:S(2)}, u32[]{:S(2)}) collective-permute-start(bf16[128,1024]{1,0:T(8,128)(2,1)S(1)} %collective-permute-done.18.refs_1_.refs_3_), channel_id=1, source_target_pairs={{0,4},{2,6},{4,0},{6,2},{8,12},{10,14},{12,8},{14,10},{16,20},{18,... | collective-permute-start | bytes 786440 | tf_op jit(solution)/shard_map/ppermute | solution.py:577
  161.2 14.5 %collective-permute-start.31 = (bf16[128,1024]{1,0:T(8,128)(2,1)S(1)}, bf16[128,1024]{1,0:T(8,128)(2,1)S(1)}, u32[]{:S(2)}, u32[]{:S(2)}) collective-permute-start(bf16[128,1024]{1,0:T(8,128)(2,1)S(1)} %add_convert_fusion.2), channel_id=1, source_target_pairs={{0,4},{2,6},{4,0},{6,2},{8,12},{10,14},{12,8},{14,10},{16,20},{18,... | collective-permute-start | bytes 786440 | tf_op jit(solution)/shard_map/ppermute | solution.py:577
  161.6 14.1 %collective-permute-start.33 = (bf16[128,1024]{1,0:T(8,128)(2,1)S(1)}, bf16[128,1024]{1,0:T(8,128)(2,1)S(1)}, u32[]{:S(2)}, u32[]{:S(2)}) collective-permute-start(bf16[128,1024]{1,0:T(8,128)(2,1)S(1)} %add_convert_fusion.1), channel_id=1, source_target_pairs={{0,8},{2,10},{4,12},{6,14},{8,0},{10,2},{12,4},{14,6},{16,24},{18,... | collective-permute-start | bytes 786440 | tf_op jit(solution)/shard_map/ppermute | solution.py:577
  161.7 14.5 %collective-permute-start.24 = (bf16[128,1024]{1,0:T(8,128)(2,1)S(1)}, bf16[128,1024]{1,0:T(8,128)(2,1)S(1)}, u32[]{:S(2)}, u32[]{:S(2)}) collective-permute-start(bf16[128,1024]{1,0:T(8,128)(2,1)S(1)} %copy-done.51), channel_id=1, source_target_pairs={{0,2},{2,0},{4,6},{6,4},{8,10},{10,8},{12,14},{14,12},{16,18},{18,... | collective-permute-start | bytes 786440 | tf_op jit(solution)/shard_map/ppermute | solution.py:577
  161.8 34.4 %collective-permute-start.34 = (bf16[2,512,512]{2,1,0:T(8,128)(2,1)}, bf16[2,512,512]{2,1,0:T(8,128)(2,1)}, u32[]{:S(2)}, u32[]{:S(2)}) collective-permute-start(bf16[2,512,512]{2,1,0:T(8,128)(2,1)} %get-tuple-element.245), channel_id=1, source_target_pairs={{0,1},{1,0},{2,3},{3,2},{4,5},{5,4},{6,7},{7,6},{8,9},{9,8},{10,11... | collective-permute-start | bytes 3145736 | tf_op jit(solution)/shard_map/ppermute | solution.py:582
  164.3 19.1 %collective-permute-start.35 = (bf16[128,1024]{1,0:T(8,128)(2,1)S(1)}, bf16[128,1024]{1,0:T(8,128)(2,1)S(1)}, u32[]{:S(2)}, u32[]{:S(2)}) collective-permute-start(bf16[128,1024]{1,0:T(8,128)(2,1)S(1)} %copy-done.50), channel_id=1, source_target_pairs={{0,2},{2,0},{4,6},{6,4},{8,10},{10,8},{12,14},{14,12},{16,18},{18,... | collective-permute-start | bytes 786440 | tf_op jit(solution)/shard_map/ppermute | solution.py:577
  175.7 89.9 %collective-permute-start.45 = (bf16[128,1024]{1,0:T(8,128)(2,1)}, bf16[128,1024]{1,0:T(8,128)(2,1)}, u32[]{:S(2)}, u32[]{:S(2)}) collective-permute-start(bf16[128,1024]{1,0:T(8,128)(2,1)} %get-tuple-element.279), channel_id=1, source_target_pairs={{0,2},{2,0},{4,6},{6,4},{8,10},{10,8},{12,14},{14,12},{16,18},{18,... | collective-permute-start | bytes 786440 | tf_op jit(solution)/shard_map/ppermute | solution.py:577
  179.0 17.2 %all-to-all-start.2 = ((bf16[16,64,128]{2,1,0:T(8,128)(2,1)}), bf16[16,64,128]{2,1,0:T(8,128)(2,1)S(1)}, u32[]{:S(2)}, u32[]{:S(2)}) async-start(bf16[16,64,128]{2,1,0:T(8,128)(2,1)} %bitcast.56), calls=%async_computation.2 | async-start | bytes 524288 | tf_op jit(solution)/shard_map/all_to_all | solution.py:967
  186.9 26.9 %collective-permute-start.37 = (bf16[128,1024]{1,0:T(8,128)(2,1)}, bf16[128,1024]{1,0:T(8,128)(2,1)}, u32[]{:S(2)}, u32[]{:S(2)}) collective-permute-start(bf16[128,1024]{1,0:T(8,128)(2,1)} %get-tuple-element.260), channel_id=1, source_target_pairs={{0,4},{2,6},{4,0},{6,2},{8,12},{10,14},{12,8},{14,10},{16,20},{18,... | collective-permute-start | bytes 786440 | tf_op jit(solution)/shard_map/ppermute | solution.py:577
  188.8 25.0 %collective-permute-start.38 = (bf16[128,1024]{1,0:T(8,128)(2,1)}, bf16[128,1024]{1,0:T(8,128)(2,1)}, u32[]{:S(2)}, u32[]{:S(2)}) collective-permute-start(bf16[128,1024]{1,0:T(8,128)(2,1)} %get-tuple-element.261), channel_id=1, source_target_pairs={{0,4},{2,6},{4,0},{6,2},{8,12},{10,14},{12,8},{14,10},{16,20},{18,... | collective-permute-start | bytes 786440 | tf_op jit(solution)/shard_map/ppermute | solution.py:577
  197.9 29.5 %collective-permute-start.39 = (bf16[512,512]{1,0:T(8,128)(2,1)S(1)}, bf16[512,512]{1,0:T(8,128)(2,1)S(1)}, u32[]{:S(2)}, u32[]{:S(2)}) collective-permute-start(bf16[512,512]{1,0:T(8,128)(2,1)S(1)} %slice_bitcast_fusion), channel_id=1, source_target_pairs={{0,16},{2,18},{4,20},{6,22},{8,24},{10,26},{12,28},{14,30},{16,0},... | collective-permute-start | bytes 1572872 | tf_op jit(solution)/shard_map/ppermute | solution.py:582
  213.8 23.3 %all-to-all-start.3 = ((bf16[16,192,128]{2,1,0:T(8,128)(2,1)}), bf16[16,192,128]{2,1,0:T(8,128)(2,1)S(1)}, u32[]{:S(2)}, u32[]{:S(2)}) async-start(bf16[16,192,128]{2,1,0:T(8,128)(2,1)} %bitcast.149), calls=%async_computation.3 | async-start | bytes 1572864 | tf_op jit(solution)/shard_map/all_to_all | solution.py:987
  223.3 21.3 %collective-permute-start.44 = (bf16[128,1024]{1,0:T(8,128)(2,1)}, bf16[128,1024]{1,0:T(8,128)(2,1)}, u32[]{:S(2)}, u32[]{:S(2)}) collective-permute-start(bf16[128,1024]{1,0:T(8,128)(2,1)} %add.285), channel_id=1, source_target_pairs={{0,8},{2,10},{4,12},{6,14},{8,0},{10,2},{12,4},{14,6},{16,24},{18,... | collective-permute-start | bytes 786440 | tf_op jit(solution)/shard_map/ppermute | solution.py:577
  225.0 25.3 %collective-permute-start.46 = (bf16[2,4,32,1024]{3,2,1,0:T(8,128)(2,1)}, bf16[2,4,32,1024]{3,2,1,0:T(8,128)(2,1)}, u32[]{:S(2)}, u32[]{:S(2)}) collective-permute-start(bf16[2,4,32,1024]{3,2,1,0:T(8,128)(2,1)} %get-tuple-element.289), channel_id=1, source_target_pairs={{0,2},{2,0},{4,6},{6,4},{8,10},{10,8},{12,14},{14,12},{16,18},{18,... | collective-permute-start | bytes 1572872 | tf_op jit(solution)/shard_map/ppermute | solution.py:577
  229.8 20.5 %collective-permute-start.43 = (bf16[2,4,32,1024]{3,2,1,0:T(8,128)(2,1)S(1)}, bf16[2,4,32,1024]{3,2,1,0:T(8,128)(2,1)S(1)}, u32[]{:S(2)}, u32[]{:S(2)}) collective-permute-start(bf16[2,4,32,1024]{3,2,1,0:T(8,128)(2,1)S(1)} %add.284), channel_id=1, source_target_pairs={{0,4},{2,6},{4,0},{6,2},{8,12},{10,14},{12,8},{14,10},{16,20},{18,... | collective-permute-start | bytes 1572872 | tf_op jit(solution)/shard_map/ppermute | solution.py:577
  232.0 18.3 %collective-permute-start.41 = (bf16[2,2,32,512]{3,2,0,1:T(8,128)(2,1)}, bf16[2,2,32,512]{3,2,0,1:T(8,128)(2,1)}, u32[]{:S(2)}, u32[]{:S(2)}) collective-permute-start(bf16[2,2,32,512]{3,2,0,1:T(8,128)(2,1)} %get-tuple-element.310), channel_id=1, source_target_pairs={{0,4},{2,6},{4,0},{6,2},{8,12},{10,14},{12,8},{14,10},{16,20},{18,... | collective-permute-start | bytes 393224 | tf_op jit(solution)/shard_map/ppermute | solution.py:577
  238.2 33.1 %all-to-all-start.4 = ((bf16[32,32,192]{2,1,0:T(8,128)(2,1)}), bf16[32,32,192]{2,1,0:T(8,128)(2,1)S(1)}, u32[]{:S(2)}, u32[]{:S(2)}) async-start(bf16[32,32,192]{2,1,0:T(8,128)(2,1)} %bitcast.60), calls=%async_computation.4 | async-start | bytes 1048576 | tf_op jit(solution)/shard_map/all_to_all | solution.py:1009
  253.1 14.5 %collective-permute-start.51 = (bf16[2,2,32,512]{3,2,1,0:T(8,128)(2,1)S(1)}, bf16[2,2,32,512]{3,2,1,0:T(8,128)(2,1)S(1)}, u32[]{:S(2)}, u32[]{:S(2)}) collective-permute-start(bf16[2,2,32,512]{3,2,1,0:T(8,128)(2,1)S(1)} %get-tuple-element.307), channel_id=1, source_target_pairs={{0,8},{2,10},{4,12},{6,14},{8,0},{10,2},{12,4},{14,6},{16,24},{18,... | collective-permute-start | bytes 393224 | tf_op jit(solution)/shard_map/ppermute | solution.py:577
  (85 other events, 856.7 us)
Sparse Core Ops, SparseCore 0:
  11.1 67.3 all-gather.4
  80.1 28.8 all-gather.8
  111.9 84.0 all-gather.6

commit v4 on v3

--- a/solution.py
+++ b/solution.py
@@ -457,47 +457,47 @@
 
 def finish_input_kernel(got_ref, weight_ref, patches_ref, middle_ref, out_ref, total):
     step = pl.program_id(0)
-    term = contract(weight_ref[...], got_ref[...], 1, 0)
-
-    @pl.when(step == 0)
-    def _():
-        total[...] = term
-
-    @pl.when(step > 0)
-    def _():
-        total[...] += term
+    total[step] = contract(weight_ref[...], got_ref[...], 1, 0).T
 
     @pl.when(step == pl.num_programs(0) - 1)
     def _():
+        grad = jnp.concatenate([total[index] for index in range(total.shape[0])], axis=1)
         hat, inverse = standardize(patches_ref[...].astype(F32))
-        grad = standardize_back(total[...].T, hat, inverse)
+        grad = standardize_back(grad, hat, inverse)
         out_ref[...] = (middle_ref[...] + grad).astype(BF16)
 
 
 def finish_input(got, weight, patches, middle_grad):
     columns, tokens = got.shape
     width = weight.shape[0]
-    block = columns // 4
+    block = width // 4
     rows = [patches, middle_grad]
     return pl.pallas_call(
         finish_input_kernel,
         grid=(4,),
         in_specs=[
-            pl.BlockSpec((block, tokens), lambda i: (i, 0)),
-            pl.BlockSpec((width, block), lambda i: (0, i)),
+            whole(got),
+            pl.BlockSpec((block, columns), lambda i: (i, 0)),
             *[whole(array) for array in rows],
         ],
         out_specs=pl.BlockSpec((tokens, width), lambda i: (0, 0)),
         out_shape=jax.ShapeDtypeStruct((tokens, width), BF16),
-        scratch_shapes=[pltpu.VMEM((width, tokens), F32)],
+        scratch_shapes=[pltpu.VMEM((4, tokens, block), F32)],
         compiler_params=pltpu.CompilerParams(vmem_limit_bytes=VMEM_LIMIT),
         cost_estimate=LARGE,
     )(got, weight, *rows)
 
 
+def as_column(row_ref):
+    row = row_ref[...].astype(F32)
+    size = (row.shape[1], row.shape[1])
+    same = lax.broadcasted_iota(jnp.int32, size, 0) == lax.broadcasted_iota(jnp.int32, size, 1)
+    return jnp.sum(jnp.where(same, row, 0.0), axis=1, keepdims=True)
+
+
 def finish_qkv_kernel(gain_ref, terms_ref, weight_ref, out_ref, gain_grad_ref):
     copies = terms_ref.shape[0] // HEADS
-    gains = gain_ref[...]
+    gains = as_column(gain_ref)
     total = None
     for head in range(HEADS):
         term = terms_ref[head * copies].astype(F32)
@@ -507,7 +507,7 @@
             first = (kind * HEADS + head) * HDIM
             columns = slice(first, first + HDIM)
             part = term[:, kind * HDIM : (kind + 1) * HDIM]
-            out_ref[:, columns] = part * gains[:, :HDIM]
+            out_ref[:, columns] = part * gains
             part = part * weight_ref[:, columns].astype(F32)
             total = part if total is None else total + part
     gain_grad_ref[...] = jnp.sum(total.T, axis=0, keepdims=True)
@@ -533,7 +533,7 @@
 def finish_up_kernel(sizes, at_ref, gain_ref, near_ref, far_ref, weight_ref, out_ref, gain_grad_ref):
     halves, batches = sizes
     chunk = near_ref.shape[-1] // (halves * batches)
-    gains = gain_ref[...]
+    gains = as_column(gain_ref)
     total = None
     for z, ref in enumerate((near_ref, far_ref)):
         for x in range(2):
@@ -780,9 +780,6 @@
     own = standard_patches(patches[0])
     first_rows = first_gain.astype(F32)[:, None]
     second_rows = second_gain.astype(F32)[:, None]
-    wide_gains = [
-        jnp.broadcast_to(gains, (lines, 128)) for gains in (first_rows, second_rows)
-    ]
     ring = Ring(own, groups, along_groups, tokens // 2)
     rounds = [[own], ring.step()]
     beside = [flip_x(own)]
@@ -798,7 +795,6 @@
         for g in range(halves)
         for b in range(batches)
     ]
-    qkv_part = qkv_rows.astype(BF16).transpose(1, 0, 2, 3).reshape(lines, 3 * width)
     up_rows = (after(up_weight, own).astype(F32) * second_rows).astype(BF16)
     up_rows = up_rows.reshape(lines, halves, 2, 2, 2, batches, hidden_rows)
     up_rows = up_rows.transpose(3, 4, 2, 0, 1, 5, 6).reshape(2, 2, 2, lines, units)
@@ -810,9 +806,6 @@
     while ring.taken < groups // 2:
         beside.append(flip_x(rows(*rounds[-1])))
         rounds.append(ring.step(*rounds[-1]))
-    up_rows = jnp.stack([up_kept, up_core], axis=1)
-    up_kept, up_x = pick(up_rows, at_x, 0), flip_x(pick(up_rows, 1 - at_x, 0), *rounds[1])
-
     def by_side(row):
         row = row.reshape(2 * groups, 2, tokens)
         sides = [pick(row, side, 1) for side in (at_core, 1 - at_core)]
@@ -822,22 +815,19 @@
     key_ids = jnp.where(by_side(kept_mask[0]) == 1, ids, -1)[None]
     farthest = rounds[-1]
     down_rows = [[down_weight, *from_batch(down_weight, *rounds[1])]]
-    rounds, beside, up_x, head_weight, ids, key_ids, numbers, down_rows = join(
-        rounds, beside, up_x, head_weight, ids, key_ids, numbers, down_rows
+    beside.append(flip_x(rows(*rounds[-1])))
+    head_weight, ids, key_ids, numbers, rounds = join(
+        head_weight, ids, key_ids, numbers, rounds
     )
 
     place_numbers, out_numbers, place_at, group_numbers, core, sides = numbers
 
-    beside.append(flip_x(rows(*rounds[-1])))
     head_weight = head_weight.reshape(width, 3 * HDIM).T
     near_weight = flip_core(head_weight)
-    up_rows = jnp.stack([up_kept, up_x], axis=0)
-    up_kept, up_z = pick(up_rows, at_z, 2), flip_z(pick(up_rows, 1 - at_z, 2))
+    up_rows = jnp.stack([up_kept, up_core], axis=1)
+    up_kept, up_x = pick(up_rows, at_x, 0), flip_x(pick(up_rows, 1 - at_x, 0))
     down_far = from_halves(down_weight, *farthest)
-    beside, near_weight, up_z = join(beside, near_weight, up_z)
-    up_packed = jnp.stack([up_kept, up_z], axis=0)
-    up_far = from_halves(up_packed)
-    up_rows = [[up_packed, *from_batch(up_packed)]]
+    beside, near_weight = join(beside, near_weight)
 
     pieces, layout, where = [own], [(0, 0)], [2 * group + at_x]
     flipped = [(0, 0, 2 * group + 1 - at_x)]
@@ -860,6 +850,9 @@
     )
 
     other = flip_core(theirs)
+    other, up_x = join(other, up_x)
+    up_rows = jnp.stack([up_kept, up_x], axis=0)
+    up_kept, up_z = pick(up_rows, at_z, 2), flip_z(pick(up_rows, 1 - at_z, 2))
     first_own = first_own.reshape(length // 2, width)
     first_other = flip_core(first_own)
     upstream = cotangent[0]
@@ -875,20 +868,23 @@
     if splits > 1:
         filled = (jnp.arange(seqs, dtype=jnp.int32) % 2 == at_core)[:, None, None]
         mixed_blocks = jnp.where(filled, mixed_blocks, 0)
-    mixed_blocks, down_rows, up_rows, down_far, first_other = join(
-        mixed_blocks, down_rows, up_rows, down_far, first_other
-    )
+    mixed_blocks, down_rows, up_z, down_far, first_other = join(
+        mixed_blocks, down_rows, up_z, down_far, first_other
+    )
+    up_packed = jnp.stack([up_kept, up_z], axis=0)
+    up_far = from_halves(up_packed)
+    up_rows = [[up_packed, *from_batch(up_packed)]]
     down_rows += [[block, *from_batch(block)] for block in down_far]
 
     mixed = lax.all_to_all(mixed_blocks, "seq", split_axis=0, concat_axis=0, tiled=True)
     if splits > 1:
         mixed = mixed.reshape(HEADS, splits, HDIM, tokens).sum(1)
-    mixed, out_full, up_far, wide_gains = join(
-        mixed.reshape(width, tokens), out_full, up_far, wide_gains
-    )
+    mixed, out_full = join(mixed.reshape(width, tokens), out_full)
     up_rows += [[block, *from_batch(block)] for block in up_far]
 
-    qkv_full = lax.all_gather(after(qkv_part, mixed_blocks), EVERY, axis=0, tiled=True)
+    qkv_part = after(qkv_rows.astype(BF16), mixed_blocks).transpose(1, 0, 2, 3)
+    qkv_part = qkv_part.reshape(lines, 3 * width)
+    qkv_full = lax.all_gather(qkv_part, EVERY, axis=0, tiled=True)
 
     middle = inputs + contract(mixed, out_full, 0, 0)
     second_hat, second_inverse = standardize(middle)
@@ -910,12 +906,14 @@
 
     weights = (place_at, upstream_all, up_part, down_part)
     hidden_near, pre_near, sum_near, grad_near = mlp([second, second_core], (0, 1), *weights)
-    second_x_core, second_z_core, grad_near = join(second_x_core, second_z_core, grad_near)
+    second_x_core, second_z_core, second_xz, grad_near = join(
+        second_x_core, second_z_core, second_xz, grad_near
+    )
+    second_xz_core = flip_core(second_xz)
     hidden_mid, pre_mid, sum_mid, grad_mid = mlp(
         [second_x, second_z, second_x_core, second_z_core], (2, 4, 3, 5), *weights
     )
-    second_xz, grad_mid = join(second_xz, grad_mid)
-    second_xz_core = flip_core(second_xz)
+    second_xz_core, grad_mid = join(second_xz_core, grad_mid)
     hidden_far, pre_far, sum_far, grad_far = mlp([second_xz, second_xz_core], (6, 7), *weights)
 
     far_sum = grad_far[0] + flip_core(grad_far[1])
@@ -971,8 +969,13 @@
     while over_batch.distance > 0:
         over_batch.step()
     grads, over_batch.got, qkv_full = join(grads, over_batch.got, qkv_full)
-    over_batch.sum = sum(over_batch.got, over_batch.block_at(0))
-    over_halves = Reduce(lambda step: over_batch.sum[step % halves], halves, along_halves)
+    over_halves = Reduce(
+        lambda step: sum(
+            [got[step % halves] for got in over_batch.got], over_batch.block_at(0)[step % halves]
+        ),
+        halves,
+        along_halves,
+    )
 
     grads = grads.reshape(groups, 2, 2, HDIM, tokens)
     far_x, mid_x = flip_x(far_part), flip_x(x_part)
@@ -1022,10 +1025,10 @@
     block_output = middle + (sum_near[0] + sum_other[0] + mid_x + mid_z)
     block_output = block_output.astype(BF16)
     qkv_terms, input_grad, block_output = join(qkv_terms, input_grad, block_output)
-    qkv_sum, first_gain_grad = finish_qkv(wide_gains[0], qkv_terms, qkv_weight)
+    qkv_sum, first_gain_grad = finish_qkv(first_gain.reshape(1, lines), qkv_terms, qkv_weight)
     if hidden_rows % 128 == 0:
         up_sum, second_gain_grad = finish_up(
-            sides, wide_gains[1], up_kept, up_z,
+            sides, second_gain.reshape(1, lines), up_kept, up_z,
             up_weight, (halves, batches),
         )
     else:

time: 282 us -> 280 us (level)
    ppermute x37, waiting for transfers between devices: 38.4 us -> 34.2 us  [flip(): return lax.ppermute(array, axis, [(i, i ^ bit) for i in range(size)])]
    unnamed x114 -> x92, local copies, waits for them, and re-layouts: 6.83 us -> 7.29 us
  transfers between devices with their start and end apart: 60 -> 60, of which waited for: 20 -> 17; matrix products, arithmetic and copies ran while one was open for 13% -> 12% of each run, Pallas kernels for 26% -> 26%
where the time goes in v4:
time: 280 us; the launch traced here: 279 us
  Pallas kernels  76 us (27%)
  starting transfers between devices  75.4 us (27%)
  waiting for transfers between devices  71.1 us (25%)
  other arithmetic  22 us (8%)
  local copies, waits for them, and re-layouts  14.7 us (5%)
  between operations  14.6 us (5%)
  matrix products  4.81 us (2%)
    pallas_call x8, Pallas kernels, whole_call(): pl.pallas_call(kernel, grid=(1,), in_specs=[pl.BlockSpec(memory_space=plt...  36 us
    ppermute x37, waiting for transfers between devices, flip(): return lax.ppermute(array, axis, [(i, i ^ bit) for i in range(size)])  34.2 us
    ppermute x15, starting transfers between devices, shift(): lax.ppermute(array, axis, [(i, (i + step * stride) % size) for i in range...  28.4 us
    ppermute x37, starting transfers between devices, flip(): return lax.ppermute(array, axis, [(i, i ^ bit) for i in range(size)])  25.3 us
    ppermute x15, waiting for transfers between devices, shift(): lax.ppermute(array, axis, [(i, (i + step * stride) % size) for i in range...  23.2 us
    pallas_call x1, Pallas kernels, attention_backward(): pl.pallas_call(functools.partial(backward_kernel, tokens), grid_spec=pltp...  15.6 us
    pallas_call x1, Pallas kernels, attention_forward(): pl.pallas_call(functools.partial(forward_kernel, tokens), grid_spec=pltpu...  11 us
    unnamed x92, local copies, waits for them, and re-layouts  7.29 us
  transfers between devices with their start and end apart: 60, of which 17 were waited for; matrix products, arithmetic and copies ran while one was open for 12% of the time, Pallas kernels for 26%

profile of v4, /device:TPU:0, one launch (start us, length us, event | category | flops | bytes accessed | tf_op | source)
XLA Modules:
  0.0 278.6 jit_solution(5304207571041396427)
XLA Ops:
  9.8 3.0 %collective-permute-start = (bf16[128,1024]{1,0:T(8,128)(2,1)}, bf16[128,1024]{1,0:T(8,128)(2,1)S(1)}, u32[]{:S(2)}, u32[]{:S(2)}) collective-permute-start(bf16[128,1024]{1,0:T(8,128)(2,1)} %shard_map.170.refs_0_), channel_id=1, source_target_pairs={{0,8},{2,10},{4,12},{6,14},{8,16},{10,18},{12,20},{14,22},{16,24},... | collective-permute-start | bytes 786440 | tf_op jit(solution)/shard_map/ppermute | solution.py:582
  20.1 3.1 %all-to-all-start = ((bf16[32,32,192]{2,1,0:T(8,128)(2,1)}), bf16[32,32,192]{2,1,0:T(8,128)(2,1)S(1)}, u32[]{:S(2)}, u32[]{:S(2)}) async-start(bf16[32,32,192]{2,1,0:T(8,128)(2,1)} %bitcast.10), calls=%async_computation | async-start | bytes 1048576 | tf_op jit(solution)/shard_map/all_to_all | solution.py:803
  28.8 3.4 %collective-permute-start.5 = (bf16[64,1024]{1,0:T(8,128)(2,1)S(1)}, bf16[64,1024]{1,0:T(8,128)(2,1)S(1)}, u32[]{:S(2)}, u32[]{:S(2)}) collective-permute-start(bf16[64,1024]{1,0:T(8,128)(2,1)S(1)} %slice.51), channel_id=1, source_target_pairs={{0,24},{2,26},{4,28},{6,30},{8,0},{10,2},{12,4},{14,6},{16,8},{18,... | collective-permute-start | bytes 393224 | tf_op jit(solution)/shard_map/ppermute | solution.py:582
  37.1 3.4 %collective-permute-done.4.refs_3_ = bf16[64,1024]{1,0:T(8,128)(2,1)S(1)} collective-permute-done((bf16[64,1024]{1,0:T(8,128)(2,1)S(1)}, bf16[64,1024]{1,0:T(8,128)(2,1)S(1)}, u32[]{:S(2)}, u32[]{:S(2)}) %collective-permute-start.4) | collective-permute-done | bytes 131104 | tf_op jit(solution)/shard_map/ppermute | solution.py:582
  46.1 7.8 %collective-permute-done.7.refs_7_ = bf16[128,1024]{1,0:T(8,128)(2,1)} collective-permute-done((bf16[128,1024]{1,0:T(8,128)(2,1)}, bf16[128,1024]{1,0:T(8,128)(2,1)}, u32[]{:S(2)}, u32[]{:S(2)}) %collective-permute-start.7) | collective-permute-done | bytes 262176 | tf_op jit(solution)/shard_map/ppermute | solution.py:577
  55.4 5.1 %shard_map.171 = (bf16[192,1024]{1,0:T(8,128)(2,1)}, bf16[192,1024]{1,0:T(8,128)(2,1)}, bf16[8,128,1024]{2,1,0:T(8,128)(2,1)}) custom-call(s32[8]{0:T(128)} %stack.92.where_ref, bf16[192,1024]{1,0:T(8,128)(2,1)} %bitcast.143, bf16[192,1024]{1,0:T(8,128)(2,1)} %copy-done.22, bf16[128,1024]{1,0:T(8,128)(2,1)} %shard_map.170.refs_0_, ...), custom_call_target="tpu_custom_call" | custom-call | flops 1 | bytes 1 | tf_op jit(solution)/shard_map/pallas_call | solution.py:299
  64.6 4.3 %collective-permute-start.13 = (bf16[128,1024]{1,0:T(8,128)(2,1)S(1)}, bf16[128,1024]{1,0:T(8,128)(2,1)}, u32[]{:S(2)}, u32[]{:S(2)}) collective-permute-start(bf16[128,1024]{1,0:T(8,128)(2,1)S(1)} %copy-done.26), channel_id=1, source_target_pairs={{0,16},{2,18},{4,20},{6,22},{8,24},{10,26},{12,28},{14,30},{16,0},... | collective-permute-start | bytes 786440 | tf_op jit(solution)/shard_map/ppermute | solution.py:582
  69.6 2.6 collective-permute-start.12
  72.2 11.0 %shard_map.172 = (bf16[4,2,2,64,128]{4,3,2,1,0:T(8,128)(2,1)}, f32[64,2048]{1,0:T(8,128)}, f32[1,2048]{1,0:T(1,128)}) custom-call(s32[1]{0:T(128)} %bitcast.30.core_ref, bf16[192,1024]{1,0:T(8,128)(2,1)} %get-tuple-element.162.own_ref, bf16[192,1024]{1,0:T(8,128)(2,1)} %copy-done.25, s32[1,2048]{1,0:T(1,128)} %bitcast.160, s32[1,2048]{1,0:T(1,128)} %bitcast.162), custom_call_target="tpu_custom_call" | custom-call | flops 1 | bytes 1 | tf_op jit(solution)/shard_map/pallas_call | solution.py:190
  85.3 3.9 %all-to-all-start.1 = ((bf16[16,64,128]{2,1,0:T(8,128)(2,1)}), bf16[16,64,128]{2,1,0:T(8,128)(2,1)S(1)}, u32[]{:S(2)}, u32[]{:S(2)}) async-start(bf16[16,64,128]{2,1,0:T(8,128)(2,1)} %bitcast.152), calls=%async_computation.1 | async-start | bytes 524288 | tf_op jit(solution)/shard_map/all_to_all | solution.py:879
  90.2 2.9 %collective-permute-start.19 = (bf16[2,2,2,32,512]{4,3,2,1,0:T(8,128)(2,1)S(1)}, bf16[2,2,2,32,512]{4,3,2,1,0:T(8,128)(2,1)}, u32[]{:S(2)}, u32[]{:S(2)}) collective-permute-start(bf16[2,2,2,32,512]{4,3,2,1,0:T(8,128)(2,1)S(1)} %pad_maximum_fusion.3.refs_0_), channel_id=1, source_target_pairs={{0,16},{2,18},{4,20},{6,22},{8,24},{10,26},{12,28},{14,30},{16,0},... | collective-permute-start | bytes 786440 | tf_op jit(solution)/shard_map/ppermute | solution.py:582
  95.1 15.1 %collective-permute-done.19.refs_2_ = bf16[2,2,2,32,512]{4,3,2,1,0:T(8,128)(2,1)} collective-permute-done((bf16[2,2,2,32,512]{4,3,2,1,0:T(8,128)(2,1)S(1)}, bf16[2,2,2,32,512]{4,3,2,1,0:T(8,128)(2,1)}, u32[]{:S(2)}, u32[]{:S(2)}) %collective-permute-start.19) | collective-permute-done | bytes 262176 | tf_op jit(solution)/shard_map/ppermute | solution.py:582
  115.9 2.4 collective-permute-done.20.refs_3_
  118.3 3.8 %collective-permute-done.15.refs_0_.refs_2_ = bf16[128,1024]{1,0:T(8,128)(2,1)S(1)} collective-permute-done((bf16[128,1024]{1,0:T(8,128)(2,1)S(1)}, bf16[128,1024]{1,0:T(8,128)(2,1)S(1)}, u32[]{:S(2)}, u32[]{:S(2)}) %collective-permute-start.15) | collective-permute-done | bytes 262176 | tf_op jit(solution)/shard_map/ppermute | solution.py:577
  126.5 3.0 %shard_map.173 = (bf16[2,2,4,2,32,512]{5,4,3,2,1,0:T(8,128)(2,1)}, bf16[2,2,128,1024]{3,2,1,0:T(8,128)(2,1)}) custom-call(s32[72]{0:T(128)} %stack.103.at_ref, bf16[2,2,2,32,512]{4,3,2,1,0:T(8,128)(2,1)} %copy-done.10, bf16[2,2,2,32,512]{4,3,2,1,0:T(8,128)(2,1)} %collective-permute-done.18.refs_1_, ...), custom_call_target="tpu_custom_call" | custom-call | flops 1 | bytes 1 | tf_op jit(solution)/shard_map/pallas_call | solution.py:299
  129.5 4.8 %shard_map.174 = (bf16[256,512]{1,0:T(8,128)(2,1)}, bf16[256,512]{1,0:T(8,128)(2,1)}, f32[128,1024]{1,0:T(8,128)}, bf16[128,1024]{1,0:T(8,128)(2,1)}, f32[128,1024]{1,0:T(8,128)}, /*index=5*/bf16[128,1024]{1,0:T(8,128)(2,1)}) custom-call(s32[1]{0:T(128)} %bitcast.35.place_ref, bf16[128,1024]{1,0:T(8,128)(2,1)} %copy-done.9, bf16[128,1024]{1,0:T(8,128)(2,1)} %copy-done.28, ...), custom_call_target="tpu_custom_call" | custom-call | flops 1 | bytes 1 | tf_op jit(solution)/shard_map/pallas_call | solution.py:299
  135.2 6.4 %shard_map.175 = (bf16[512,512]{1,0:T(8,128)(2,1)}, bf16[512,512]{1,0:T(8,128)(2,1)}, f32[128,1024]{1,0:T(8,128)}, f32[128,1024]{1,0:T(8,128)}, bf16[128,1024]{1...) custom-call(s32[1]{0:T(128)} %bitcast.35.place_ref, ...), custom_call_target="tpu_custom_call" | custom-call | flops 1 | bytes 1 | tf_op jit(solution)/shard_map/pallas_call | solution.py:299
  142.3 4.8 %shard_map.176 = (bf16[256,512]{1,0:T(8,128)(2,1)}, bf16[256,512]{1,0:T(8,128)(2,1)}, f32[128,1024]{1,0:T(8,128)}, bf16[128,1024]{1,0:T(8,128)(2,1)}, f32[128,1024]{1,0:T(8,128)}, /*index=5*/bf16[128,1024]{1,0:T(8,128)(2,1)}) custom-call(s32[1]{0:T(128)} %bitcast.35.place_ref, bf16[128,1024]{1,0:T(8,128)(2,1)} %copy-done.29, bf16[128,1024]{1,0:T(8,128)(2,1)} %copy-done.30, ...), custom_call_target="tpu_custom_call" | custom-call | flops 1 | bytes 1 | tf_op jit(solution)/shard_map/pallas_call | solution.py:299
  150.7 6.7 %shard_map.177 = (bf16[2,512,512]{2,1,0:T(8,128)(2,1)}, bf16[2,512,512]{2,1,0:T(8,128)(2,1)}) custom-call(s32[5]{0:T(128)} %stack.113.at_ref, bf16[128,1024]{1,0:T(8,128)(2,1)} %copy-done.9, bf16[128,1024]{1,0:T(8,128)(2,1)} %copy-done.28, bf16[128,1024]{1,0:T(8,128)(2,1)} %copy-done.32, bf16[128,1024]{1,0:T(8,128)(2,1)} %copy-done.33, ...), custom_call_target="tpu_custom_call" | custom-call | flops 30000001024 | bytes 1 | tf_op jit(solution)/shard_map/pallas_call | solution.py:299
  163.0 11.4 %collective-permute-done.31 = bf16[128,1024]{1,0:T(8,128)(2,1)S(1)} collective-permute-done((bf16[128,1024]{1,0:T(8,128)(2,1)S(1)}, bf16[128,1024]{1,0:T(8,128)(2,1)S(1)}, u32[]{:S(2)}, u32[]{:S(2)}) %collective-permute-start.31) | collective-permute-done | bytes 262176 | tf_op jit(solution)/shard_map/ppermute | solution.py:577
  177.7 4.1 %all-to-all-start.2 = ((bf16[16,64,128]{2,1,0:T(8,128)(2,1)}), bf16[16,64,128]{2,1,0:T(8,128)(2,1)S(1)}, u32[]{:S(2)}, u32[]{:S(2)}) async-start(bf16[16,64,128]{2,1,0:T(8,128)(2,1)} %bitcast.56), calls=%async_computation.2 | async-start | bytes 524288 | tf_op jit(solution)/shard_map/all_to_all | solution.py:965
  182.5 2.6 shard_map.179
  187.2 5.5 %all-to-all-done.2 = bf16[16,64,128]{2,1,0:T(8,128)(2,1)S(1)} async-done(((bf16[16,64,128]{2,1,0:T(8,128)(2,1)}), bf16[16,64,128]{2,1,0:T(8,128)(2,1)S(1)}, u32[]{:S(2)}, u32[]{:S(2)}) %all-to-all-start.2) | async-done | bytes 262176 | tf_op jit(solution)/shard_map/all_to_all | solution.py:965
  196.4 15.6 %shard_map.178 = (bf16[4,2,2,192,128]{4,3,2,1,0:T(8,128)(2,1)}, bf16[192,1024]{1,0:T(8,128)(2,1)}, bf16[192,1024]{1,0:T(8,128)(2,1)}) custom-call(s32[1]{0:T(128)} %bitcast.30.core_ref, bf16[192,1024]{1,0:T(8,128)(2,1)} %get-tuple-element.162.own_ref, bf16[192,1024]{1,0:T(8,128)(2,1)} %copy-done.25, s32[1,2048]{1,0:T(1,128)} %bitcast.161, ...), custom_call_target="tpu_custom_call" | custom-call | flops 30000001024 | bytes 1 | tf_op jit(solution)/shard_map/pallas_call | solution.py:218
  212.0 4.4 %all-to-all-start.3 = ((bf16[16,192,128]{2,1,0:T(8,128)(2,1)}), bf16[16,192,128]{2,1,0:T(8,128)(2,1)}, u32[]{:S(2)}, u32[]{:S(2)}) async-start(bf16[16,192,128]{2,1,0:T(8,128)(2,1)} %bitcast.150), calls=%async_computation.3 | async-start | bytes 1572864 | tf_op jit(solution)/shard_map/all_to_all | solution.py:990
  216.4 3.1 %shard_map.180 = (bf16[2,4,32,1024]{3,2,1,0:T(8,128)(2,1)}, bf16[2,4,32,1024]{3,2,1,0:T(8,128)(2,1)}, bf16[2,4,32,1024]{3,2,1,0:T(8,128)(2,1)}, bf16[2,4,32,1024]{3,2,1,0:T(8,128)(2,1)}) custom-call(s32[11]{0:T(128)} %stack.110.at_ref, bf16[1024,128]{1,0:T(8,128)(2,1)} %bitcast.138, bf16[128,1024]{1,0:T(8,128)(2,1)} %copy-done.1), custom_call_target="tpu_custom_call" | custom-call | flops 1 | bytes 1 | tf_op jit(solution)/shard_map/pallas_call | solution.py:299
  230.0 5.6 %all-to-all-done.3 = bf16[16,192,128]{2,1,0:T(8,128)(2,1)} async-done(((bf16[16,192,128]{2,1,0:T(8,128)(2,1)}), bf16[16,192,128]{2,1,0:T(8,128)(2,1)}, u32[]{:S(2)}, u32[]{:S(2)}) %all-to-all-start.3) | async-done | bytes 786464 | tf_op jit(solution)/shard_map/all_to_all | solution.py:990
  236.5 6.1 %all-to-all-start.4 = ((bf16[32,32,192]{2,1,0:T(8,128)(2,1)}), bf16[32,32,192]{2,1,0:T(8,128)(2,1)S(1)}, u32[]{:S(2)}, u32[]{:S(2)}) async-start(bf16[32,32,192]{2,1,0:T(8,128)(2,1)} %bitcast.61), calls=%async_computation.4 | async-start | bytes 1048576 | tf_op jit(solution)/shard_map/all_to_all | solution.py:1012
  242.6 4.0 %collective-permute-done.41 = bf16[2,2,32,512]{3,2,0,1:T(8,128)(2,1)S(1)} collective-permute-done((bf16[2,2,32,512]{3,2,0,1:T(8,128)(2,1)S(1)}, bf16[2,2,32,512]{3,2,0,1:T(8,128)(2,1)S(1)}, u32[]{:S(2)}, u32[]{:S(2)}) %collective-permute-start.41) | collective-permute-done | bytes 131104 | tf_op jit(solution)/shard_map/ppermute | solution.py:577
  250.0 6.4 %shard_map.181 = bf16[128,1024]{1,0:T(8,128)(2,1)} custom-call(bf16[3072,128]{1,0:T(8,128)(2,1)} %bitcast.68.got_ref, bf16[1024,3072]{1,0:T(8,128)(2,1)} %all-gather.7.cloned.1.call-done.weight_ref, bf16[128,1024]{1,0:T(8,128)(2,1)} %bitcast.149, f32[128,1024]{1,0:T(8,128)} %get-tuple-element.283.middle_ref), custom_call_target="tpu_custom_call" | custom-call | flops 30000001024 | bytes 1 | tf_op jit(solution)/shard_map/pallas_call | solution.py:475
  258.0 3.5 %collective-permute-start.50 = (bf16[32,1024]{1,0:T(8,128)(2,1)S(1)}, bf16[32,1024]{1,0:T(8,128)(2,1)S(1)}, u32[]{:S(2)}, u32[]{:S(2)}) collective-permute-start(bf16[32,1024]{1,0:T(8,128)(2,1)S(1)} %get-tuple-element.296), channel_id=1, source_target_pairs={{0,16},{2,18},{4,20},{6,22},{8,24},{10,26},{12,28},{14,30},{16,0},... | collective-permute-start | bytes 196616 | tf_op jit(solution)/shard_map/ppermute | solution.py:582
  269.7 2.4 shard_map.182
  (260 shorter events, 91.9 us)
Async XLA Ops:
  7.2 104.5 %all-gather.5.cloned.1.call-start = ((), (), s32[]{:S(2)}) async-start(), calls=%async_computation.5 | async-start | bytes 2162688 | tf_op jit(solution)/shard_map/all_gather | solution.py:752
  9.8 15.6 %collective-permute-start = (bf16[128,1024]{1,0:T(8,128)(2,1)}, bf16[128,1024]{1,0:T(8,128)(2,1)S(1)}, u32[]{:S(2)}, u32[]{:S(2)}) collective-permute-start(bf16[128,1024]{1,0:T(8,128)(2,1)} %shard_map.170.refs_0_), channel_id=1, source_target_pairs={{0,8},{2,10},{4,12},{6,14},{8,16},{10,18},{12,20},{14,22},{16,24},... | collective-permute-start | bytes 786440 | tf_op jit(solution)/shard_map/ppermute | solution.py:582
  12.8 14.6 %collective-permute-start.1 = (bf16[128,1024]{1,0:T(8,128)(2,1)}, bf16[128,1024]{1,0:T(8,128)(2,1)S(1)}, u32[]{:S(2)}, u32[]{:S(2)}) collective-permute-start(bf16[128,1024]{1,0:T(8,128)(2,1)} %shard_map.170.refs_0_), channel_id=1, source_target_pairs={{0,24},{2,26},{4,28},{6,30},{8,0},{10,2},{12,4},{14,6},{16,8},{18,... | collective-permute-start | bytes 786440 | tf_op jit(solution)/shard_map/ppermute | solution.py:582
  14.9 12.6 %collective-permute-start.2 = (bf16[128,1024]{1,0:T(8,128)(2,1)}, bf16[128,1024]{1,0:T(8,128)(2,1)S(1)}, u32[]{:S(2)}, u32[]{:S(2)}) collective-permute-start(bf16[128,1024]{1,0:T(8,128)(2,1)} %shard_map.170.refs_0_), channel_id=1, source_target_pairs={{0,4},{2,6},{4,0},{6,2},{8,12},{10,14},{12,8},{14,10},{16,20},{18,... | collective-permute-start | bytes 786440 | tf_op jit(solution)/shard_map/ppermute | solution.py:577
  20.1 22.6 %all-to-all-start = ((bf16[32,32,192]{2,1,0:T(8,128)(2,1)}), bf16[32,32,192]{2,1,0:T(8,128)(2,1)S(1)}, u32[]{:S(2)}, u32[]{:S(2)}) async-start(bf16[32,32,192]{2,1,0:T(8,128)(2,1)} %bitcast.10), calls=%async_computation | async-start | bytes 1048576 | tf_op jit(solution)/shard_map/all_to_all | solution.py:803
  23.2 100.9 %all-gather.9.cloned.1.call-start = ((), (), s32[]{:S(2)}) async-start(), calls=%async_computation.7 | async-start | bytes 2359296 | tf_op jit(solution)/shard_map/all_gather | solution.py:859
  32.2 21.7 %collective-permute-start.6 = (bf16[256,1024]{1,0:T(8,128)(2,1)S(1)}, bf16[256,1024]{1,0:T(8,128)(2,1)S(1)}, u32[]{:S(2)}, u32[]{:S(2)}) collective-permute-start(bf16[256,1024]{1,0:T(8,128)(2,1)S(1)} %pad_maximum_fusion), channel_id=1, source_target_pairs={{0,4},{2,6},{4,0},{6,2},{8,12},{10,14},{12,8},{14,10},{16,20},{18,... | collective-permute-start | bytes 1572872 | tf_op jit(solution)/shard_map/ppermute | solution.py:577
  60.6 132.1 %all-gather.7.cloned.1.call-start = ((), (), s32[]{:S(2)}) async-start(), calls=%async_computation.6 | async-start | bytes 6488064 | tf_op jit(solution)/shard_map/all_gather | solution.py:887
  60.6 22.6 %collective-permute-start.14 = (bf16[1024,1024]{1,0:T(8,128)(2,1)}, bf16[1024,1024]{1,0:T(8,128)(2,1)S(1)}, u32[]{:S(2)}, u32[]{:S(2)}) collective-permute-start(bf16[1024,1024]{1,0:T(8,128)(2,1)} %bitcast.139), channel_id=1, source_target_pairs={{0,2},{2,0},{4,6},{6,4},{8,10},{10,8},{12,14},{14,12},{16,18},{18,... | collective-permute-start | bytes 6291464 | tf_op jit(solution)/shard_map/ppermute | solution.py:577
  63.8 19.4 %collective-permute-start.11 = (bf16[128,1024]{1,0:T(8,128)(2,1)S(1)}, bf16[128,1024]{1,0:T(8,128)(2,1)}, u32[]{:S(2)}, u32[]{:S(2)}) collective-permute-start(bf16[128,1024]{1,0:T(8,128)(2,1)S(1)} %copy-done.26), channel_id=1, source_target_pairs={{0,1},{1,0},{2,3},{3,2},{4,5},{5,4},{6,7},{7,6},{8,9},{9,8},{10,11... | collective-permute-start | bytes 786440 | tf_op jit(solution)/shard_map/ppermute | solution.py:582
  64.6 18.7 %collective-permute-start.13 = (bf16[128,1024]{1,0:T(8,128)(2,1)S(1)}, bf16[128,1024]{1,0:T(8,128)(2,1)}, u32[]{:S(2)}, u32[]{:S(2)}) collective-permute-start(bf16[128,1024]{1,0:T(8,128)(2,1)S(1)} %copy-done.26), channel_id=1, source_target_pairs={{0,16},{2,18},{4,20},{6,22},{8,24},{10,26},{12,28},{14,30},{16,0},... | collective-permute-start | bytes 786440 | tf_op jit(solution)/shard_map/ppermute | solution.py:582
  69.6 13.6 %collective-permute-start.12 = (bf16[2,2,32,512]{3,2,1,0:T(8,128)(2,1)S(1)}, bf16[2,2,32,512]{3,2,1,0:T(8,128)(2,1)S(1)}, u32[]{:S(2)}, u32[]{:S(2)}) collective-permute-start(bf16[2,2,32,512]{3,2,1,0:T(8,128)(2,1)S(1)} %get-tuple-element.301), channel_id=1, source_target_pairs={{0,8},{2,10},{4,12},{6,14},{8,0},{10,2},{12,4},{14,6},{16,24},{18,... | collective-permute-start | bytes 393224 | tf_op jit(solution)/shard_map/ppermute | solution.py:577
  85.3 26.4 %all-to-all-start.1 = ((bf16[16,64,128]{2,1,0:T(8,128)(2,1)}), bf16[16,64,128]{2,1,0:T(8,128)(2,1)S(1)}, u32[]{:S(2)}, u32[]{:S(2)}) async-start(bf16[16,64,128]{2,1,0:T(8,128)(2,1)} %bitcast.152), calls=%async_computation.1 | async-start | bytes 524288 | tf_op jit(solution)/shard_map/all_to_all | solution.py:879
  90.2 20.0 %collective-permute-start.19 = (bf16[2,2,2,32,512]{4,3,2,1,0:T(8,128)(2,1)S(1)}, bf16[2,2,2,32,512]{4,3,2,1,0:T(8,128)(2,1)}, u32[]{:S(2)}, u32[]{:S(2)}) collective-permute-start(bf16[2,2,2,32,512]{4,3,2,1,0:T(8,128)(2,1)S(1)} %pad_maximum_fusion.3.refs_0_), channel_id=1, source_target_pairs={{0,16},{2,18},{4,20},{6,22},{8,24},{10,26},{12,28},{14,30},{16,0},... | collective-permute-start | bytes 786440 | tf_op jit(solution)/shard_map/ppermute | solution.py:582
  93.1 22.8 %collective-permute-start.18 = (bf16[2,2,2,32,512]{4,3,2,1,0:T(8,128)(2,1)S(1)}, bf16[2,2,2,32,512]{4,3,2,1,0:T(8,128)(2,1)}, u32[]{:S(2)}, u32[]{:S(2)}) collective-permute-start(bf16[2,2,2,32,512]{4,3,2,1,0:T(8,128)(2,1)S(1)} %pad_maximum_fusion.3.refs_0_), channel_id=1, source_target_pairs={{0,1},{1,0},{2,3},{3,2},{4,5},{5,4},{6,7},{7,6},{8,9},{9,8},{10,11... | collective-permute-start | bytes 786440 | tf_op jit(solution)/shard_map/ppermute | solution.py:582
  94.6 21.3 %collective-permute-start.21 = (bf16[128,1024]{1,0:T(8,128)(2,1)}, bf16[128,1024]{1,0:T(8,128)(2,1)}, u32[]{:S(2)}, u32[]{:S(2)}) collective-permute-start(bf16[128,1024]{1,0:T(8,128)(2,1)} %collective-permute-done.13.refs_6_), channel_id=1, source_target_pairs={{0,1},{1,0},{2,3},{3,2},{4,5},{5,4},{6,7},{7,6},{8,9},{9,8},{10,11... | collective-permute-start | bytes 786440 | tf_op jit(solution)/shard_map/ppermute | solution.py:582
  160.1 14.3 %collective-permute-start.31 = (bf16[128,1024]{1,0:T(8,128)(2,1)S(1)}, bf16[128,1024]{1,0:T(8,128)(2,1)S(1)}, u32[]{:S(2)}, u32[]{:S(2)}) collective-permute-start(bf16[128,1024]{1,0:T(8,128)(2,1)S(1)} %add_convert_fusion.2), channel_id=1, source_target_pairs={{0,4},{2,6},{4,0},{6,2},{8,12},{10,14},{12,8},{14,10},{16,20},{18,... | collective-permute-start | bytes 786440 | tf_op jit(solution)/shard_map/ppermute | solution.py:577
  162.4 12.5 %collective-permute-start.25 = (bf16[128,1024]{1,0:T(8,128)(2,1)S(1)}, bf16[128,1024]{1,0:T(8,128)(2,1)S(1)}, u32[]{:S(2)}, u32[]{:S(2)}) collective-permute-start(bf16[128,1024]{1,0:T(8,128)(2,1)S(1)} %copy-done.43), channel_id=1, source_target_pairs={{0,2},{2,0},{4,6},{6,4},{8,10},{10,8},{12,14},{14,12},{16,18},{18,... | collective-permute-start | bytes 786440 | tf_op jit(solution)/shard_map/ppermute | solution.py:577
  162.5 30.2 %collective-permute-start.34 = (bf16[2,512,512]{2,1,0:T(8,128)(2,1)}, bf16[2,512,512]{2,1,0:T(8,128)(2,1)}, u32[]{:S(2)}, u32[]{:S(2)}) collective-permute-start(bf16[2,512,512]{2,1,0:T(8,128)(2,1)} %get-tuple-element.231), channel_id=1, source_target_pairs={{0,1},{1,0},{2,3},{3,2},{4,5},{5,4},{6,7},{7,6},{8,9},{9,8},{10,11... | collective-permute-start | bytes 3145736 | tf_op jit(solution)/shard_map/ppermute | solution.py:582
  162.6 19.2 %collective-permute-start.35 = (bf16[128,1024]{1,0:T(8,128)(2,1)}, bf16[128,1024]{1,0:T(8,128)(2,1)S(1)}, u32[]{:S(2)}, u32[]{:S(2)}) collective-permute-start(bf16[128,1024]{1,0:T(8,128)(2,1)} %get-tuple-element.243), channel_id=1, source_target_pairs={{0,2},{2,0},{4,6},{6,4},{8,10},{10,8},{12,14},{14,12},{16,18},{18,... | collective-permute-start | bytes 786440 | tf_op jit(solution)/shard_map/ppermute | solution.py:577
  174.4 89.1 %collective-permute-start.45 = (bf16[128,1024]{1,0:T(8,128)(2,1)}, bf16[128,1024]{1,0:T(8,128)(2,1)}, u32[]{:S(2)}, u32[]{:S(2)}) collective-permute-start(bf16[128,1024]{1,0:T(8,128)(2,1)} %get-tuple-element.265), channel_id=1, source_target_pairs={{0,2},{2,0},{4,6},{6,4},{8,10},{10,8},{12,14},{14,12},{16,18},{18,... | collective-permute-start | bytes 786440 | tf_op jit(solution)/shard_map/ppermute | solution.py:577
  177.7 15.0 %all-to-all-start.2 = ((bf16[16,64,128]{2,1,0:T(8,128)(2,1)}), bf16[16,64,128]{2,1,0:T(8,128)(2,1)S(1)}, u32[]{:S(2)}, u32[]{:S(2)}) async-start(bf16[16,64,128]{2,1,0:T(8,128)(2,1)} %bitcast.56), calls=%async_computation.2 | async-start | bytes 524288 | tf_op jit(solution)/shard_map/all_to_all | solution.py:965
  185.2 26.8 %collective-permute-start.37 = (bf16[128,1024]{1,0:T(8,128)(2,1)}, bf16[128,1024]{1,0:T(8,128)(2,1)}, u32[]{:S(2)}, u32[]{:S(2)}) collective-permute-start(bf16[128,1024]{1,0:T(8,128)(2,1)} %get-tuple-element.246), channel_id=1, source_target_pairs={{0,4},{2,6},{4,0},{6,2},{8,12},{10,14},{12,8},{14,10},{16,20},{18,... | collective-permute-start | bytes 786440 | tf_op jit(solution)/shard_map/ppermute | solution.py:577
  187.1 24.9 %collective-permute-start.38 = (bf16[128,1024]{1,0:T(8,128)(2,1)}, bf16[128,1024]{1,0:T(8,128)(2,1)}, u32[]{:S(2)}, u32[]{:S(2)}) collective-permute-start(bf16[128,1024]{1,0:T(8,128)(2,1)} %get-tuple-element.247), channel_id=1, source_target_pairs={{0,4},{2,6},{4,0},{6,2},{8,12},{10,14},{12,8},{14,10},{16,20},{18,... | collective-permute-start | bytes 786440 | tf_op jit(solution)/shard_map/ppermute | solution.py:577
  194.0 29.9 %collective-permute-start.39 = (bf16[512,512]{1,0:T(8,128)(2,1)S(1)}, bf16[512,512]{1,0:T(8,128)(2,1)}, u32[]{:S(2)}, u32[]{:S(2)}) collective-permute-start(bf16[512,512]{1,0:T(8,128)(2,1)S(1)} %add_bitcast_fusion), channel_id=1, source_target_pairs={{0,16},{2,18},{4,20},{6,22},{8,24},{10,26},{12,28},{14,30},{16,0},... | collective-permute-start | bytes 1572872 | tf_op jit(solution)/shard_map/ppermute | solution.py:582
  212.0 23.5 %all-to-all-start.3 = ((bf16[16,192,128]{2,1,0:T(8,128)(2,1)}), bf16[16,192,128]{2,1,0:T(8,128)(2,1)}, u32[]{:S(2)}, u32[]{:S(2)}) async-start(bf16[16,192,128]{2,1,0:T(8,128)(2,1)} %bitcast.150), calls=%async_computation.3 | async-start | bytes 1572864 | tf_op jit(solution)/shard_map/all_to_all | solution.py:990
  221.6 21.0 %collective-permute-start.44 = (bf16[128,1024]{1,0:T(8,128)(2,1)}, bf16[128,1024]{1,0:T(8,128)(2,1)}, u32[]{:S(2)}, u32[]{:S(2)}) collective-permute-start(bf16[128,1024]{1,0:T(8,128)(2,1)} %add.297), channel_id=1, source_target_pairs={{0,8},{2,10},{4,12},{6,14},{8,0},{10,2},{12,4},{14,6},{16,24},{18,... | collective-permute-start | bytes 786440 | tf_op jit(solution)/shard_map/ppermute | solution.py:577
  223.3 23.3 %collective-permute-start.46 = (bf16[2,4,32,1024]{3,2,1,0:T(8,128)(2,1)}, bf16[2,4,32,1024]{3,2,1,0:T(8,128)(2,1)}, u32[]{:S(2)}, u32[]{:S(2)}) collective-permute-start(bf16[2,4,32,1024]{3,2,1,0:T(8,128)(2,1)} %get-tuple-element.274), channel_id=1, source_target_pairs={{0,2},{2,0},{4,6},{6,4},{8,10},{10,8},{12,14},{14,12},{16,18},{18,... | collective-permute-start | bytes 1572872 | tf_op jit(solution)/shard_map/ppermute | solution.py:577
  226.9 19.7 %collective-permute-start.43 = (bf16[2,4,32,1024]{3,2,1,0:T(8,128)(2,1)S(1)}, bf16[2,4,32,1024]{3,2,1,0:T(8,128)(2,1)S(1)}, u32[]{:S(2)}, u32[]{:S(2)}) collective-permute-start(bf16[2,4,32,1024]{3,2,1,0:T(8,128)(2,1)S(1)} %add.296), channel_id=1, source_target_pairs={{0,4},{2,6},{4,0},{6,2},{8,12},{10,14},{12,8},{14,10},{16,20},{18,... | collective-permute-start | bytes 1572872 | tf_op jit(solution)/shard_map/ppermute | solution.py:577
  228.5 18.1 %collective-permute-start.41 = (bf16[2,2,32,512]{3,2,0,1:T(8,128)(2,1)S(1)}, bf16[2,2,32,512]{3,2,0,1:T(8,128)(2,1)S(1)}, u32[]{:S(2)}, u32[]{:S(2)}) collective-permute-start(bf16[2,2,32,512]{3,2,0,1:T(8,128)(2,1)S(1)} %get-tuple-element.294), channel_id=1, source_target_pairs={{0,4},{2,6},{4,0},{6,2},{8,12},{10,14},{12,8},{14,10},{16,20},{18,... | collective-permute-start | bytes 393224 | tf_op jit(solution)/shard_map/ppermute | solution.py:577
  236.5 32.4 %all-to-all-start.4 = ((bf16[32,32,192]{2,1,0:T(8,128)(2,1)}), bf16[32,32,192]{2,1,0:T(8,128)(2,1)S(1)}, u32[]{:S(2)}, u32[]{:S(2)}) async-start(bf16[32,32,192]{2,1,0:T(8,128)(2,1)} %bitcast.61), calls=%async_computation.4 | async-start | bytes 1048576 | tf_op jit(solution)/shard_map/all_to_all | solution.py:1012
  248.6 16.9 %collective-permute-start.51 = (bf16[2,2,32,512]{3,2,1,0:T(8,128)(2,1)S(1)}, bf16[2,2,32,512]{3,2,1,0:T(8,128)(2,1)S(1)}, u32[]{:S(2)}, u32[]{:S(2)}) collective-permute-start(bf16[2,2,32,512]{3,2,1,0:T(8,128)(2,1)S(1)} %get-tuple-element.291), channel_id=1, source_target_pairs={{0,8},{2,10},{4,12},{6,14},{8,0},{10,2},{12,4},{14,6},{16,24},{18,... | collective-permute-start | bytes 393224 | tf_op jit(solution)/shard_map/ppermute | solution.py:577
  (74 other events, 585.1 us)
Sparse Core Ops, SparseCore 0:
  11.1 66.6 all-gather.4
  79.4 29.3 all-gather.8
  111.7 74.3 all-gather.6

commit v5 on v4

--- a/solution.py
+++ b/solution.py
@@ -916,8 +916,8 @@
     second_xz_core, grad_mid = join(second_xz_core, grad_mid)
     hidden_far, pre_far, sum_far, grad_far = mlp([second_xz, second_xz_core], (6, 7), *weights)
 
-    far_sum = grad_far[0] + flip_core(grad_far[1])
-    far_x = flip_x(far_sum.astype(BF16))
+    far_sum = (grad_far[0] + flip_core(grad_far[1])).astype(BF16)
+    far_x = flip_x(far_sum)
     x_sum = grad_mid[0] + flip_core(grad_mid[2])
     z_sum = grad_mid[1] + flip_core(grad_mid[3])
     near_sum = grad_near[0] + flip_core(grad_near[1])

time: 280 us -> 280 us (level)
  no operation moved by 1% of the time
where the time goes in v5:
time: 280 us; the launch traced here: 279 us
  Pallas kernels  76 us (27%)
  starting transfers between devices  75.4 us (27%)
  waiting for transfers between devices  71.1 us (25%)
  other arithmetic  22 us (8%)
  local copies, waits for them, and re-layouts  14.7 us (5%)
  between operations  14.6 us (5%)
  matrix products  4.81 us (2%)
    pallas_call x8, Pallas kernels, whole_call(): pl.pallas_call(kernel, grid=(1,), in_specs=[pl.BlockSpec(memory_space=plt...  36 us
    ppermute x37, waiting for transfers between devices, flip(): return lax.ppermute(array, axis, [(i, i ^ bit) for i in range(size)])  34.2 us
    ppermute x15, starting transfers between devices, shift(): lax.ppermute(array, axis, [(i, (i + step * stride) % size) for i in range...  28.4 us
    ppermute x37, starting transfers between devices, flip(): return lax.ppermute(array, axis, [(i, i ^ bit) for i in range(size)])  25.3 us
    ppermute x15, waiting for transfers between devices, shift(): lax.ppermute(array, axis, [(i, (i + step * stride) % size) for i in range...  23.2 us
    pallas_call x1, Pallas kernels, attention_backward(): pl.pallas_call(functools.partial(backward_kernel, tokens), grid_spec=pltp...  15.6 us
    pallas_call x1, Pallas kernels, attention_forward(): pl.pallas_call(functools.partial(forward_kernel, tokens), grid_spec=pltpu...  11 us
    unnamed x92, local copies, waits for them, and re-layouts  7.29 us
  transfers between devices with their start and end apart: 60, of which 17 were waited for; matrix products, arithmetic and copies ran while one was open for 12% of the time, Pallas kernels for 26%

profile of v5, /device:TPU:0, one launch (start us, length us, event | category | flops | bytes accessed | tf_op | source)
XLA Modules:
  0.0 278.6 jit_solution(5304207571041396427)
XLA Ops:
  9.8 3.0 %collective-permute-start = (bf16[128,1024]{1,0:T(8,128)(2,1)}, bf16[128,1024]{1,0:T(8,128)(2,1)S(1)}, u32[]{:S(2)}, u32[]{:S(2)}) collective-permute-start(bf16[128,1024]{1,0:T(8,128)(2,1)} %shard_map.170.refs_0_), channel_id=1, source_target_pairs={{0,8},{2,10},{4,12},{6,14},{8,16},{10,18},{12,20},{14,22},{16,24},... | collective-permute-start | bytes 786440 | tf_op jit(solution)/shard_map/ppermute | solution.py:582
  20.1 3.1 %all-to-all-start = ((bf16[32,32,192]{2,1,0:T(8,128)(2,1)}), bf16[32,32,192]{2,1,0:T(8,128)(2,1)S(1)}, u32[]{:S(2)}, u32[]{:S(2)}) async-start(bf16[32,32,192]{2,1,0:T(8,128)(2,1)} %bitcast.10), calls=%async_computation | async-start | bytes 1048576 | tf_op jit(solution)/shard_map/all_to_all | solution.py:803
  28.8 3.4 %collective-permute-start.5 = (bf16[64,1024]{1,0:T(8,128)(2,1)S(1)}, bf16[64,1024]{1,0:T(8,128)(2,1)S(1)}, u32[]{:S(2)}, u32[]{:S(2)}) collective-permute-start(bf16[64,1024]{1,0:T(8,128)(2,1)S(1)} %slice.51), channel_id=1, source_target_pairs={{0,24},{2,26},{4,28},{6,30},{8,0},{10,2},{12,4},{14,6},{16,8},{18,... | collective-permute-start | bytes 393224 | tf_op jit(solution)/shard_map/ppermute | solution.py:582
  37.1 3.4 %collective-permute-done.4.refs_3_ = bf16[64,1024]{1,0:T(8,128)(2,1)S(1)} collective-permute-done((bf16[64,1024]{1,0:T(8,128)(2,1)S(1)}, bf16[64,1024]{1,0:T(8,128)(2,1)S(1)}, u32[]{:S(2)}, u32[]{:S(2)}) %collective-permute-start.4) | collective-permute-done | bytes 131104 | tf_op jit(solution)/shard_map/ppermute | solution.py:582
  46.1 7.8 %collective-permute-done.7.refs_7_ = bf16[128,1024]{1,0:T(8,128)(2,1)} collective-permute-done((bf16[128,1024]{1,0:T(8,128)(2,1)}, bf16[128,1024]{1,0:T(8,128)(2,1)}, u32[]{:S(2)}, u32[]{:S(2)}) %collective-permute-start.7) | collective-permute-done | bytes 262176 | tf_op jit(solution)/shard_map/ppermute | solution.py:577
  55.4 5.1 %shard_map.171 = (bf16[192,1024]{1,0:T(8,128)(2,1)}, bf16[192,1024]{1,0:T(8,128)(2,1)}, bf16[8,128,1024]{2,1,0:T(8,128)(2,1)}) custom-call(s32[8]{0:T(128)} %stack.92.where_ref, bf16[192,1024]{1,0:T(8,128)(2,1)} %bitcast.143, bf16[192,1024]{1,0:T(8,128)(2,1)} %copy-done.22, bf16[128,1024]{1,0:T(8,128)(2,1)} %shard_map.170.refs_0_, ...), custom_call_target="tpu_custom_call" | custom-call | flops 1 | bytes 1 | tf_op jit(solution)/shard_map/pallas_call | solution.py:299
  64.6 4.3 %collective-permute-start.13 = (bf16[128,1024]{1,0:T(8,128)(2,1)S(1)}, bf16[128,1024]{1,0:T(8,128)(2,1)}, u32[]{:S(2)}, u32[]{:S(2)}) collective-permute-start(bf16[128,1024]{1,0:T(8,128)(2,1)S(1)} %copy-done.26), channel_id=1, source_target_pairs={{0,16},{2,18},{4,20},{6,22},{8,24},{10,26},{12,28},{14,30},{16,0},... | collective-permute-start | bytes 786440 | tf_op jit(solution)/shard_map/ppermute | solution.py:582
  69.6 2.6 collective-permute-start.12
  72.2 11.0 %shard_map.172 = (bf16[4,2,2,64,128]{4,3,2,1,0:T(8,128)(2,1)}, f32[64,2048]{1,0:T(8,128)}, f32[1,2048]{1,0:T(1,128)}) custom-call(s32[1]{0:T(128)} %bitcast.30.core_ref, bf16[192,1024]{1,0:T(8,128)(2,1)} %get-tuple-element.162.own_ref, bf16[192,1024]{1,0:T(8,128)(2,1)} %copy-done.25, s32[1,2048]{1,0:T(1,128)} %bitcast.160, s32[1,2048]{1,0:T(1,128)} %bitcast.162), custom_call_target="tpu_custom_call" | custom-call | flops 1 | bytes 1 | tf_op jit(solution)/shard_map/pallas_call | solution.py:190
  85.3 3.9 %all-to-all-start.1 = ((bf16[16,64,128]{2,1,0:T(8,128)(2,1)}), bf16[16,64,128]{2,1,0:T(8,128)(2,1)S(1)}, u32[]{:S(2)}, u32[]{:S(2)}) async-start(bf16[16,64,128]{2,1,0:T(8,128)(2,1)} %bitcast.152), calls=%async_computation.1 | async-start | bytes 524288 | tf_op jit(solution)/shard_map/all_to_all | solution.py:879
  90.2 2.9 %collective-permute-start.19 = (bf16[2,2,2,32,512]{4,3,2,1,0:T(8,128)(2,1)S(1)}, bf16[2,2,2,32,512]{4,3,2,1,0:T(8,128)(2,1)}, u32[]{:S(2)}, u32[]{:S(2)}) collective-permute-start(bf16[2,2,2,32,512]{4,3,2,1,0:T(8,128)(2,1)S(1)} %pad_maximum_fusion.3.refs_0_), channel_id=1, source_target_pairs={{0,16},{2,18},{4,20},{6,22},{8,24},{10,26},{12,28},{14,30},{16,0},... | collective-permute-start | bytes 786440 | tf_op jit(solution)/shard_map/ppermute | solution.py:582
  95.1 15.1 %collective-permute-done.19.refs_2_ = bf16[2,2,2,32,512]{4,3,2,1,0:T(8,128)(2,1)} collective-permute-done((bf16[2,2,2,32,512]{4,3,2,1,0:T(8,128)(2,1)S(1)}, bf16[2,2,2,32,512]{4,3,2,1,0:T(8,128)(2,1)}, u32[]{:S(2)}, u32[]{:S(2)}) %collective-permute-start.19) | collective-permute-done | bytes 262176 | tf_op jit(solution)/shard_map/ppermute | solution.py:582
  115.9 2.4 collective-permute-done.20.refs_3_
  118.3 3.8 %collective-permute-done.15.refs_0_.refs_2_ = bf16[128,1024]{1,0:T(8,128)(2,1)S(1)} collective-permute-done((bf16[128,1024]{1,0:T(8,128)(2,1)S(1)}, bf16[128,1024]{1,0:T(8,128)(2,1)S(1)}, u32[]{:S(2)}, u32[]{:S(2)}) %collective-permute-start.15) | collective-permute-done | bytes 262176 | tf_op jit(solution)/shard_map/ppermute | solution.py:577
  126.5 3.0 %shard_map.173 = (bf16[2,2,4,2,32,512]{5,4,3,2,1,0:T(8,128)(2,1)}, bf16[2,2,128,1024]{3,2,1,0:T(8,128)(2,1)}) custom-call(s32[72]{0:T(128)} %stack.103.at_ref, bf16[2,2,2,32,512]{4,3,2,1,0:T(8,128)(2,1)} %copy-done.10, bf16[2,2,2,32,512]{4,3,2,1,0:T(8,128)(2,1)} %collective-permute-done.18.refs_1_, ...), custom_call_target="tpu_custom_call" | custom-call | flops 1 | bytes 1 | tf_op jit(solution)/shard_map/pallas_call | solution.py:299
  129.5 4.8 %shard_map.174 = (bf16[256,512]{1,0:T(8,128)(2,1)}, bf16[256,512]{1,0:T(8,128)(2,1)}, f32[128,1024]{1,0:T(8,128)}, bf16[128,1024]{1,0:T(8,128)(2,1)}, f32[128,1024]{1,0:T(8,128)}, /*index=5*/bf16[128,1024]{1,0:T(8,128)(2,1)}) custom-call(s32[1]{0:T(128)} %bitcast.35.place_ref, bf16[128,1024]{1,0:T(8,128)(2,1)} %copy-done.9, bf16[128,1024]{1,0:T(8,128)(2,1)} %copy-done.28, ...), custom_call_target="tpu_custom_call" | custom-call | flops 1 | bytes 1 | tf_op jit(solution)/shard_map/pallas_call | solution.py:299
  135.2 6.4 %shard_map.175 = (bf16[512,512]{1,0:T(8,128)(2,1)}, bf16[512,512]{1,0:T(8,128)(2,1)}, f32[128,1024]{1,0:T(8,128)}, f32[128,1024]{1,0:T(8,128)}, bf16[128,1024]{1...) custom-call(s32[1]{0:T(128)} %bitcast.35.place_ref, ...), custom_call_target="tpu_custom_call" | custom-call | flops 1 | bytes 1 | tf_op jit(solution)/shard_map/pallas_call | solution.py:299
  142.3 4.8 %shard_map.176 = (bf16[256,512]{1,0:T(8,128)(2,1)}, bf16[256,512]{1,0:T(8,128)(2,1)}, f32[128,1024]{1,0:T(8,128)}, bf16[128,1024]{1,0:T(8,128)(2,1)}, f32[128,1024]{1,0:T(8,128)}, /*index=5*/bf16[128,1024]{1,0:T(8,128)(2,1)}) custom-call(s32[1]{0:T(128)} %bitcast.35.place_ref, bf16[128,1024]{1,0:T(8,128)(2,1)} %copy-done.29, bf16[128,1024]{1,0:T(8,128)(2,1)} %copy-done.30, ...), custom_call_target="tpu_custom_call" | custom-call | flops 1 | bytes 1 | tf_op jit(solution)/shard_map/pallas_call | solution.py:299
  150.7 6.7 %shard_map.177 = (bf16[2,512,512]{2,1,0:T(8,128)(2,1)}, bf16[2,512,512]{2,1,0:T(8,128)(2,1)}) custom-call(s32[5]{0:T(128)} %stack.113.at_ref, bf16[128,1024]{1,0:T(8,128)(2,1)} %copy-done.9, bf16[128,1024]{1,0:T(8,128)(2,1)} %copy-done.28, bf16[128,1024]{1,0:T(8,128)(2,1)} %copy-done.32, bf16[128,1024]{1,0:T(8,128)(2,1)} %copy-done.33, ...), custom_call_target="tpu_custom_call" | custom-call | flops 30000001024 | bytes 1 | tf_op jit(solution)/shard_map/pallas_call | solution.py:299
  163.0 11.4 %collective-permute-done.31 = bf16[128,1024]{1,0:T(8,128)(2,1)S(1)} collective-permute-done((bf16[128,1024]{1,0:T(8,128)(2,1)S(1)}, bf16[128,1024]{1,0:T(8,128)(2,1)S(1)}, u32[]{:S(2)}, u32[]{:S(2)}) %collective-permute-start.31) | collective-permute-done | bytes 262176 | tf_op jit(solution)/shard_map/ppermute | solution.py:577
  177.7 4.1 %all-to-all-start.2 = ((bf16[16,64,128]{2,1,0:T(8,128)(2,1)}), bf16[16,64,128]{2,1,0:T(8,128)(2,1)S(1)}, u32[]{:S(2)}, u32[]{:S(2)}) async-start(bf16[16,64,128]{2,1,0:T(8,128)(2,1)} %bitcast.56), calls=%async_computation.2 | async-start | bytes 524288 | tf_op jit(solution)/shard_map/all_to_all | solution.py:965
  182.5 2.6 shard_map.179
  187.2 5.5 %all-to-all-done.2 = bf16[16,64,128]{2,1,0:T(8,128)(2,1)S(1)} async-done(((bf16[16,64,128]{2,1,0:T(8,128)(2,1)}), bf16[16,64,128]{2,1,0:T(8,128)(2,1)S(1)}, u32[]{:S(2)}, u32[]{:S(2)}) %all-to-all-start.2) | async-done | bytes 262176 | tf_op jit(solution)/shard_map/all_to_all | solution.py:965
  196.4 15.6 %shard_map.178 = (bf16[4,2,2,192,128]{4,3,2,1,0:T(8,128)(2,1)}, bf16[192,1024]{1,0:T(8,128)(2,1)}, bf16[192,1024]{1,0:T(8,128)(2,1)}) custom-call(s32[1]{0:T(128)} %bitcast.30.core_ref, bf16[192,1024]{1,0:T(8,128)(2,1)} %get-tuple-element.162.own_ref, bf16[192,1024]{1,0:T(8,128)(2,1)} %copy-done.25, s32[1,2048]{1,0:T(1,128)} %bitcast.161, ...), custom_call_target="tpu_custom_call" | custom-call | flops 30000001024 | bytes 1 | tf_op jit(solution)/shard_map/pallas_call | solution.py:218
  212.0 4.4 %all-to-all-start.3 = ((bf16[16,192,128]{2,1,0:T(8,128)(2,1)}), bf16[16,192,128]{2,1,0:T(8,128)(2,1)}, u32[]{:S(2)}, u32[]{:S(2)}) async-start(bf16[16,192,128]{2,1,0:T(8,128)(2,1)} %bitcast.150), calls=%async_computation.3 | async-start | bytes 1572864 | tf_op jit(solution)/shard_map/all_to_all | solution.py:990
  216.4 3.1 %shard_map.180 = (bf16[2,4,32,1024]{3,2,1,0:T(8,128)(2,1)}, bf16[2,4,32,1024]{3,2,1,0:T(8,128)(2,1)}, bf16[2,4,32,1024]{3,2,1,0:T(8,128)(2,1)}, bf16[2,4,32,1024]{3,2,1,0:T(8,128)(2,1)}) custom-call(s32[11]{0:T(128)} %stack.110.at_ref, bf16[1024,128]{1,0:T(8,128)(2,1)} %bitcast.138, bf16[128,1024]{1,0:T(8,128)(2,1)} %copy-done.1), custom_call_target="tpu_custom_call" | custom-call | flops 1 | bytes 1 | tf_op jit(solution)/shard_map/pallas_call | solution.py:299
  230.0 5.6 %all-to-all-done.3 = bf16[16,192,128]{2,1,0:T(8,128)(2,1)} async-done(((bf16[16,192,128]{2,1,0:T(8,128)(2,1)}), bf16[16,192,128]{2,1,0:T(8,128)(2,1)}, u32[]{:S(2)}, u32[]{:S(2)}) %all-to-all-start.3) | async-done | bytes 786464 | tf_op jit(solution)/shard_map/all_to_all | solution.py:990
  236.5 6.1 %all-to-all-start.4 = ((bf16[32,32,192]{2,1,0:T(8,128)(2,1)}), bf16[32,32,192]{2,1,0:T(8,128)(2,1)S(1)}, u32[]{:S(2)}, u32[]{:S(2)}) async-start(bf16[32,32,192]{2,1,0:T(8,128)(2,1)} %bitcast.61), calls=%async_computation.4 | async-start | bytes 1048576 | tf_op jit(solution)/shard_map/all_to_all | solution.py:1012
  242.6 4.0 %collective-permute-done.41 = bf16[2,2,32,512]{3,2,0,1:T(8,128)(2,1)S(1)} collective-permute-done((bf16[2,2,32,512]{3,2,0,1:T(8,128)(2,1)S(1)}, bf16[2,2,32,512]{3,2,0,1:T(8,128)(2,1)S(1)}, u32[]{:S(2)}, u32[]{:S(2)}) %collective-permute-start.41) | collective-permute-done | bytes 131104 | tf_op jit(solution)/shard_map/ppermute | solution.py:577
  250.0 6.4 %shard_map.181 = bf16[128,1024]{1,0:T(8,128)(2,1)} custom-call(bf16[3072,128]{1,0:T(8,128)(2,1)} %bitcast.68.got_ref, bf16[1024,3072]{1,0:T(8,128)(2,1)} %all-gather.7.cloned.1.call-done.weight_ref, bf16[128,1024]{1,0:T(8,128)(2,1)} %bitcast.149, f32[128,1024]{1,0:T(8,128)} %get-tuple-element.283.middle_ref), custom_call_target="tpu_custom_call" | custom-call | flops 30000001024 | bytes 1 | tf_op jit(solution)/shard_map/pallas_call | solution.py:475
  258.0 3.5 %collective-permute-start.50 = (bf16[32,1024]{1,0:T(8,128)(2,1)S(1)}, bf16[32,1024]{1,0:T(8,128)(2,1)S(1)}, u32[]{:S(2)}, u32[]{:S(2)}) collective-permute-start(bf16[32,1024]{1,0:T(8,128)(2,1)S(1)} %get-tuple-element.296), channel_id=1, source_target_pairs={{0,16},{2,18},{4,20},{6,22},{8,24},{10,26},{12,28},{14,30},{16,0},... | collective-permute-start | bytes 196616 | tf_op jit(solution)/shard_map/ppermute | solution.py:582
  269.7 2.4 shard_map.182
  (260 shorter events, 91.9 us)
Async XLA Ops:
  7.2 104.5 %all-gather.5.cloned.1.call-start = ((), (), s32[]{:S(2)}) async-start(), calls=%async_computation.5 | async-start | bytes 2162688 | tf_op jit(solution)/shard_map/all_gather | solution.py:752
  9.8 15.6 %collective-permute-start = (bf16[128,1024]{1,0:T(8,128)(2,1)}, bf16[128,1024]{1,0:T(8,128)(2,1)S(1)}, u32[]{:S(2)}, u32[]{:S(2)}) collective-permute-start(bf16[128,1024]{1,0:T(8,128)(2,1)} %shard_map.170.refs_0_), channel_id=1, source_target_pairs={{0,8},{2,10},{4,12},{6,14},{8,16},{10,18},{12,20},{14,22},{16,24},... | collective-permute-start | bytes 786440 | tf_op jit(solution)/shard_map/ppermute | solution.py:582
  12.8 14.6 %collective-permute-start.1 = (bf16[128,1024]{1,0:T(8,128)(2,1)}, bf16[128,1024]{1,0:T(8,128)(2,1)S(1)}, u32[]{:S(2)}, u32[]{:S(2)}) collective-permute-start(bf16[128,1024]{1,0:T(8,128)(2,1)} %shard_map.170.refs_0_), channel_id=1, source_target_pairs={{0,24},{2,26},{4,28},{6,30},{8,0},{10,2},{12,4},{14,6},{16,8},{18,... | collective-permute-start | bytes 786440 | tf_op jit(solution)/shard_map/ppermute | solution.py:582
  14.9 12.6 %collective-permute-start.2 = (bf16[128,1024]{1,0:T(8,128)(2,1)}, bf16[128,1024]{1,0:T(8,128)(2,1)S(1)}, u32[]{:S(2)}, u32[]{:S(2)}) collective-permute-start(bf16[128,1024]{1,0:T(8,128)(2,1)} %shard_map.170.refs_0_), channel_id=1, source_target_pairs={{0,4},{2,6},{4,0},{6,2},{8,12},{10,14},{12,8},{14,10},{16,20},{18,... | collective-permute-start | bytes 786440 | tf_op jit(solution)/shard_map/ppermute | solution.py:577
  20.1 22.6 %all-to-all-start = ((bf16[32,32,192]{2,1,0:T(8,128)(2,1)}), bf16[32,32,192]{2,1,0:T(8,128)(2,1)S(1)}, u32[]{:S(2)}, u32[]{:S(2)}) async-start(bf16[32,32,192]{2,1,0:T(8,128)(2,1)} %bitcast.10), calls=%async_computation | async-start | bytes 1048576 | tf_op jit(solution)/shard_map/all_to_all | solution.py:803
  23.2 100.9 %all-gather.9.cloned.1.call-start = ((), (), s32[]{:S(2)}) async-start(), calls=%async_computation.7 | async-start | bytes 2359296 | tf_op jit(solution)/shard_map/all_gather | solution.py:859
  32.2 21.7 %collective-permute-start.6 = (bf16[256,1024]{1,0:T(8,128)(2,1)S(1)}, bf16[256,1024]{1,0:T(8,128)(2,1)S(1)}, u32[]{:S(2)}, u32[]{:S(2)}) collective-permute-start(bf16[256,1024]{1,0:T(8,128)(2,1)S(1)} %pad_maximum_fusion), channel_id=1, source_target_pairs={{0,4},{2,6},{4,0},{6,2},{8,12},{10,14},{12,8},{14,10},{16,20},{18,... | collective-permute-start | bytes 1572872 | tf_op jit(solution)/shard_map/ppermute | solution.py:577
  60.6 132.1 %all-gather.7.cloned.1.call-start = ((), (), s32[]{:S(2)}) async-start(), calls=%async_computation.6 | async-start | bytes 6488064 | tf_op jit(solution)/shard_map/all_gather | solution.py:887
  60.6 22.6 %collective-permute-start.14 = (bf16[1024,1024]{1,0:T(8,128)(2,1)}, bf16[1024,1024]{1,0:T(8,128)(2,1)S(1)}, u32[]{:S(2)}, u32[]{:S(2)}) collective-permute-start(bf16[1024,1024]{1,0:T(8,128)(2,1)} %bitcast.139), channel_id=1, source_target_pairs={{0,2},{2,0},{4,6},{6,4},{8,10},{10,8},{12,14},{14,12},{16,18},{18,... | collective-permute-start | bytes 6291464 | tf_op jit(solution)/shard_map/ppermute | solution.py:577
  63.8 19.4 %collective-permute-start.11 = (bf16[128,1024]{1,0:T(8,128)(2,1)S(1)}, bf16[128,1024]{1,0:T(8,128)(2,1)}, u32[]{:S(2)}, u32[]{:S(2)}) collective-permute-start(bf16[128,1024]{1,0:T(8,128)(2,1)S(1)} %copy-done.26), channel_id=1, source_target_pairs={{0,1},{1,0},{2,3},{3,2},{4,5},{5,4},{6,7},{7,6},{8,9},{9,8},{10,11... | collective-permute-start | bytes 786440 | tf_op jit(solution)/shard_map/ppermute | solution.py:582
  64.6 18.7 %collective-permute-start.13 = (bf16[128,1024]{1,0:T(8,128)(2,1)S(1)}, bf16[128,1024]{1,0:T(8,128)(2,1)}, u32[]{:S(2)}, u32[]{:S(2)}) collective-permute-start(bf16[128,1024]{1,0:T(8,128)(2,1)S(1)} %copy-done.26), channel_id=1, source_target_pairs={{0,16},{2,18},{4,20},{6,22},{8,24},{10,26},{12,28},{14,30},{16,0},... | collective-permute-start | bytes 786440 | tf_op jit(solution)/shard_map/ppermute | solution.py:582
  69.6 13.6 %collective-permute-start.12 = (bf16[2,2,32,512]{3,2,1,0:T(8,128)(2,1)S(1)}, bf16[2,2,32,512]{3,2,1,0:T(8,128)(2,1)S(1)}, u32[]{:S(2)}, u32[]{:S(2)}) collective-permute-start(bf16[2,2,32,512]{3,2,1,0:T(8,128)(2,1)S(1)} %get-tuple-element.301), channel_id=1, source_target_pairs={{0,8},{2,10},{4,12},{6,14},{8,0},{10,2},{12,4},{14,6},{16,24},{18,... | collective-permute-start | bytes 393224 | tf_op jit(solution)/shard_map/ppermute | solution.py:577
  85.3 26.4 %all-to-all-start.1 = ((bf16[16,64,128]{2,1,0:T(8,128)(2,1)}), bf16[16,64,128]{2,1,0:T(8,128)(2,1)S(1)}, u32[]{:S(2)}, u32[]{:S(2)}) async-start(bf16[16,64,128]{2,1,0:T(8,128)(2,1)} %bitcast.152), calls=%async_computation.1 | async-start | bytes 524288 | tf_op jit(solution)/shard_map/all_to_all | solution.py:879
  90.2 20.0 %collective-permute-start.19 = (bf16[2,2,2,32,512]{4,3,2,1,0:T(8,128)(2,1)S(1)}, bf16[2,2,2,32,512]{4,3,2,1,0:T(8,128)(2,1)}, u32[]{:S(2)}, u32[]{:S(2)}) collective-permute-start(bf16[2,2,2,32,512]{4,3,2,1,0:T(8,128)(2,1)S(1)} %pad_maximum_fusion.3.refs_0_), channel_id=1, source_target_pairs={{0,16},{2,18},{4,20},{6,22},{8,24},{10,26},{12,28},{14,30},{16,0},... | collective-permute-start | bytes 786440 | tf_op jit(solution)/shard_map/ppermute | solution.py:582
  93.1 22.8 %collective-permute-start.18 = (bf16[2,2,2,32,512]{4,3,2,1,0:T(8,128)(2,1)S(1)}, bf16[2,2,2,32,512]{4,3,2,1,0:T(8,128)(2,1)}, u32[]{:S(2)}, u32[]{:S(2)}) collective-permute-start(bf16[2,2,2,32,512]{4,3,2,1,0:T(8,128)(2,1)S(1)} %pad_maximum_fusion.3.refs_0_), channel_id=1, source_target_pairs={{0,1},{1,0},{2,3},{3,2},{4,5},{5,4},{6,7},{7,6},{8,9},{9,8},{10,11... | collective-permute-start | bytes 786440 | tf_op jit(solution)/shard_map/ppermute | solution.py:582
  94.6 21.3 %collective-permute-start.21 = (bf16[128,1024]{1,0:T(8,128)(2,1)}, bf16[128,1024]{1,0:T(8,128)(2,1)}, u32[]{:S(2)}, u32[]{:S(2)}) collective-permute-start(bf16[128,1024]{1,0:T(8,128)(2,1)} %collective-permute-done.13.refs_6_), channel_id=1, source_target_pairs={{0,1},{1,0},{2,3},{3,2},{4,5},{5,4},{6,7},{7,6},{8,9},{9,8},{10,11... | collective-permute-start | bytes 786440 | tf_op jit(solution)/shard_map/ppermute | solution.py:582
  160.1 14.3 %collective-permute-start.31 = (bf16[128,1024]{1,0:T(8,128)(2,1)S(1)}, bf16[128,1024]{1,0:T(8,128)(2,1)S(1)}, u32[]{:S(2)}, u32[]{:S(2)}) collective-permute-start(bf16[128,1024]{1,0:T(8,128)(2,1)S(1)} %add_convert_fusion.3), channel_id=1, source_target_pairs={{0,4},{2,6},{4,0},{6,2},{8,12},{10,14},{12,8},{14,10},{16,20},{18,... | collective-permute-start | bytes 786440 | tf_op jit(solution)/shard_map/ppermute | solution.py:577
  162.4 12.5 %collective-permute-start.25 = (bf16[128,1024]{1,0:T(8,128)(2,1)S(1)}, bf16[128,1024]{1,0:T(8,128)(2,1)S(1)}, u32[]{:S(2)}, u32[]{:S(2)}) collective-permute-start(bf16[128,1024]{1,0:T(8,128)(2,1)S(1)} %copy-done.43), channel_id=1, source_target_pairs={{0,2},{2,0},{4,6},{6,4},{8,10},{10,8},{12,14},{14,12},{16,18},{18,... | collective-permute-start | bytes 786440 | tf_op jit(solution)/shard_map/ppermute | solution.py:577
  162.5 30.2 %collective-permute-start.34 = (bf16[2,512,512]{2,1,0:T(8,128)(2,1)}, bf16[2,512,512]{2,1,0:T(8,128)(2,1)}, u32[]{:S(2)}, u32[]{:S(2)}) collective-permute-start(bf16[2,512,512]{2,1,0:T(8,128)(2,1)} %get-tuple-element.231), channel_id=1, source_target_pairs={{0,1},{1,0},{2,3},{3,2},{4,5},{5,4},{6,7},{7,6},{8,9},{9,8},{10,11... | collective-permute-start | bytes 3145736 | tf_op jit(solution)/shard_map/ppermute | solution.py:582
  162.6 19.2 %collective-permute-start.35 = (bf16[128,1024]{1,0:T(8,128)(2,1)}, bf16[128,1024]{1,0:T(8,128)(2,1)S(1)}, u32[]{:S(2)}, u32[]{:S(2)}) collective-permute-start(bf16[128,1024]{1,0:T(8,128)(2,1)} %get-tuple-element.243), channel_id=1, source_target_pairs={{0,2},{2,0},{4,6},{6,4},{8,10},{10,8},{12,14},{14,12},{16,18},{18,... | collective-permute-start | bytes 786440 | tf_op jit(solution)/shard_map/ppermute | solution.py:577
  174.4 89.1 %collective-permute-start.45 = (bf16[128,1024]{1,0:T(8,128)(2,1)}, bf16[128,1024]{1,0:T(8,128)(2,1)}, u32[]{:S(2)}, u32[]{:S(2)}) collective-permute-start(bf16[128,1024]{1,0:T(8,128)(2,1)} %get-tuple-element.265), channel_id=1, source_target_pairs={{0,2},{2,0},{4,6},{6,4},{8,10},{10,8},{12,14},{14,12},{16,18},{18,... | collective-permute-start | bytes 786440 | tf_op jit(solution)/shard_map/ppermute | solution.py:577
  177.7 15.0 %all-to-all-start.2 = ((bf16[16,64,128]{2,1,0:T(8,128)(2,1)}), bf16[16,64,128]{2,1,0:T(8,128)(2,1)S(1)}, u32[]{:S(2)}, u32[]{:S(2)}) async-start(bf16[16,64,128]{2,1,0:T(8,128)(2,1)} %bitcast.56), calls=%async_computation.2 | async-start | bytes 524288 | tf_op jit(solution)/shard_map/all_to_all | solution.py:965
  185.2 26.8 %collective-permute-start.37 = (bf16[128,1024]{1,0:T(8,128)(2,1)}, bf16[128,1024]{1,0:T(8,128)(2,1)}, u32[]{:S(2)}, u32[]{:S(2)}) collective-permute-start(bf16[128,1024]{1,0:T(8,128)(2,1)} %get-tuple-element.246), channel_id=1, source_target_pairs={{0,4},{2,6},{4,0},{6,2},{8,12},{10,14},{12,8},{14,10},{16,20},{18,... | collective-permute-start | bytes 786440 | tf_op jit(solution)/shard_map/ppermute | solution.py:577
  187.1 24.9 %collective-permute-start.38 = (bf16[128,1024]{1,0:T(8,128)(2,1)}, bf16[128,1024]{1,0:T(8,128)(2,1)}, u32[]{:S(2)}, u32[]{:S(2)}) collective-permute-start(bf16[128,1024]{1,0:T(8,128)(2,1)} %get-tuple-element.247), channel_id=1, source_target_pairs={{0,4},{2,6},{4,0},{6,2},{8,12},{10,14},{12,8},{14,10},{16,20},{18,... | collective-permute-start | bytes 786440 | tf_op jit(solution)/shard_map/ppermute | solution.py:577
  194.0 29.9 %collective-permute-start.39 = (bf16[512,512]{1,0:T(8,128)(2,1)S(1)}, bf16[512,512]{1,0:T(8,128)(2,1)}, u32[]{:S(2)}, u32[]{:S(2)}) collective-permute-start(bf16[512,512]{1,0:T(8,128)(2,1)S(1)} %add_bitcast_fusion), channel_id=1, source_target_pairs={{0,16},{2,18},{4,20},{6,22},{8,24},{10,26},{12,28},{14,30},{16,0},... | collective-permute-start | bytes 1572872 | tf_op jit(solution)/shard_map/ppermute | solution.py:582
  212.0 23.5 %all-to-all-start.3 = ((bf16[16,192,128]{2,1,0:T(8,128)(2,1)}), bf16[16,192,128]{2,1,0:T(8,128)(2,1)}, u32[]{:S(2)}, u32[]{:S(2)}) async-start(bf16[16,192,128]{2,1,0:T(8,128)(2,1)} %bitcast.150), calls=%async_computation.3 | async-start | bytes 1572864 | tf_op jit(solution)/shard_map/all_to_all | solution.py:990
  221.6 21.0 %collective-permute-start.44 = (bf16[128,1024]{1,0:T(8,128)(2,1)}, bf16[128,1024]{1,0:T(8,128)(2,1)}, u32[]{:S(2)}, u32[]{:S(2)}) collective-permute-start(bf16[128,1024]{1,0:T(8,128)(2,1)} %add.297), channel_id=1, source_target_pairs={{0,8},{2,10},{4,12},{6,14},{8,0},{10,2},{12,4},{14,6},{16,24},{18,... | collective-permute-start | bytes 786440 | tf_op jit(solution)/shard_map/ppermute | solution.py:577
  223.3 23.3 %collective-permute-start.46 = (bf16[2,4,32,1024]{3,2,1,0:T(8,128)(2,1)}, bf16[2,4,32,1024]{3,2,1,0:T(8,128)(2,1)}, u32[]{:S(2)}, u32[]{:S(2)}) collective-permute-start(bf16[2,4,32,1024]{3,2,1,0:T(8,128)(2,1)} %get-tuple-element.274), channel_id=1, source_target_pairs={{0,2},{2,0},{4,6},{6,4},{8,10},{10,8},{12,14},{14,12},{16,18},{18,... | collective-permute-start | bytes 1572872 | tf_op jit(solution)/shard_map/ppermute | solution.py:577
  226.9 19.7 %collective-permute-start.43 = (bf16[2,4,32,1024]{3,2,1,0:T(8,128)(2,1)S(1)}, bf16[2,4,32,1024]{3,2,1,0:T(8,128)(2,1)S(1)}, u32[]{:S(2)}, u32[]{:S(2)}) collective-permute-start(bf16[2,4,32,1024]{3,2,1,0:T(8,128)(2,1)S(1)} %add.296), channel_id=1, source_target_pairs={{0,4},{2,6},{4,0},{6,2},{8,12},{10,14},{12,8},{14,10},{16,20},{18,... | collective-permute-start | bytes 1572872 | tf_op jit(solution)/shard_map/ppermute | solution.py:577
  228.5 18.1 %collective-permute-start.41 = (bf16[2,2,32,512]{3,2,0,1:T(8,128)(2,1)S(1)}, bf16[2,2,32,512]{3,2,0,1:T(8,128)(2,1)S(1)}, u32[]{:S(2)}, u32[]{:S(2)}) collective-permute-start(bf16[2,2,32,512]{3,2,0,1:T(8,128)(2,1)S(1)} %get-tuple-element.294), channel_id=1, source_target_pairs={{0,4},{2,6},{4,0},{6,2},{8,12},{10,14},{12,8},{14,10},{16,20},{18,... | collective-permute-start | bytes 393224 | tf_op jit(solution)/shard_map/ppermute | solution.py:577
  236.5 32.4 %all-to-all-start.4 = ((bf16[32,32,192]{2,1,0:T(8,128)(2,1)}), bf16[32,32,192]{2,1,0:T(8,128)(2,1)S(1)}, u32[]{:S(2)}, u32[]{:S(2)}) async-start(bf16[32,32,192]{2,1,0:T(8,128)(2,1)} %bitcast.61), calls=%async_computation.4 | async-start | bytes 1048576 | tf_op jit(solution)/shard_map/all_to_all | solution.py:1012
  248.6 16.9 %collective-permute-start.51 = (bf16[2,2,32,512]{3,2,1,0:T(8,128)(2,1)S(1)}, bf16[2,2,32,512]{3,2,1,0:T(8,128)(2,1)S(1)}, u32[]{:S(2)}, u32[]{:S(2)}) collective-permute-start(bf16[2,2,32,512]{3,2,1,0:T(8,128)(2,1)S(1)} %get-tuple-element.291), channel_id=1, source_target_pairs={{0,8},{2,10},{4,12},{6,14},{8,0},{10,2},{12,4},{14,6},{16,24},{18,... | collective-permute-start | bytes 393224 | tf_op jit(solution)/shard_map/ppermute | solution.py:577
  (74 other events, 585.1 us)
Sparse Core Ops, SparseCore 0:
  11.1 66.6 all-gather.4
  79.4 29.3 all-gather.8
  111.7 74.3 all-gather.6
